TPU v7x, 32 devices: a whole 2x2x4 slice. The times are simulated.
32 devices in a mesh: dp: 16 (over z, y, x), tp: 2 (over core).
Axes of the slice: x: 2, y: 2, z: 4, core: 2. Of those that a mesh axis runs over, the one named last changes fastest.
Arguments:
- inputs: bfloat16 [76800, 512], P(('dp', 'tp')), may hold values from -6 to 6
- page_of: int32 [76800], P('dp'), may hold values from 0 to 3071, as said below
- rel_index: int32 [100, 100], replicated, may hold values from 0 to 360, as said below
- w_qkv: bfloat16 [3, 512, 512], P(None, None, 'tp'), may hold values from -0.25 to 0.25
- qv_bias: float32 [2, 512], P(None, 'tp'), may hold values from -1.5 to 1.5
- w_proj: bfloat16 [512, 512], P('tp'), may hold values from -1 to 1
- w_fc1: bfloat16 [512, 2048], P(None, 'tp'), may hold values from -0.25 to 0.25
- fc1_bias: float32 [2048], P('tp'), may hold values from -1.5 to 1.5
- w_fc2: bfloat16 [2048, 512], P('tp'), may hold values from -0.125 to 0.125
- out_biases: float32 [2, 512], replicated, may hold values from -1.5 to 1.5
- norm_gains: float32 [2, 512], replicated, may hold values from 0.1 to 1.9
- norm_biases: float32 [2, 512], replicated, may hold values from -1.5 to 1.5
- bias_table: float32 [361, 16], P(None, 'tp'), may hold values from -3 to 3
- out_grad: bfloat16 [76800, 512], P(('dp', 'tp')), may hold values from -6 to 6
Outputs:
- block_out: bfloat16 [76800, 512], P(('dp', 'tp'))
- grad_in: bfloat16 [76800, 512], P(('dp', 'tp'))
- g_qkv: float32 [3, 512, 512], P(None, None, 'tp')
- g_qv_bias: float32 [2, 512], P(None, 'tp')
- g_proj: float32 [512, 512], P('tp')
- g_fc1: float32 [512, 2048], P(None, 'tp')
- g_fc1_bias: float32 [2048], P('tp')
- g_fc2: float32 [2048, 512], P('tp')
- g_out_biases: float32 [2, 512], replicated
- g_norm_gains: float32 [2, 512], replicated
- g_norm_biases: float32 [2, 512], replicated
- g_table: float32 [361, 16], P(None, 'tp')
Inputs may be any that keep to these rules, and one draw needn't show every extreme that they name: `page_of`: within each window (100 consecutive patches, row-major), the regions are the rectangles cut by one row boundary and one column boundary; no two windows share a region. `rel_index`: entry [i, j] depends only on the offset of position i from position j within a window, each of the 361 offsets with its own table row.
All inputs are finite; a program needn't handle non-finite values.
Results may differ from a plain program's by a relative error of at most 0.015.
Values may be sent and summed in bfloat16 or wider, within the bound.
No kernel may reach another device: no remote copies, remote signals or barrier semaphores. Data moves between devices by JAX's collectives and lax.ppermute only.
A program may use at most 256 MiB of HBM per device.

v0:
```python
import functools

import jax
import jax.numpy as jnp
from jax import lax
from jax.experimental import pallas as pl
from jax.experimental.pallas import tpu as pltpu
from jax.sharding import PartitionSpec as P

HEAD = 32
EPS = 1e-05
WIN = 100
WS = 10
TAB = 361
KEYS = 104
LANES = 128
SLAB = 256
GROUP = 4
ROWS = GROUP * WIN
DENSE = 480
THIRD = 2
CHUNK = 256
LOG2E = 1.4426950408889634
NEG = -1e30
BF = jnp.bfloat16
F32 = jnp.float32
NT = (((1,), (1,)), ((), ()))
TN = (((0,), (0,)), ((), ()))


def dot(a, b):
    return jnp.dot(a, b, preferred_element_type=F32)


def dot_nt(a, b):
    return lax.dot_general(a, b, NT, preferred_element_type=F32)


def dot_tn(a, b):
    return lax.dot_general(a, b, TN, preferred_element_type=F32)


def norm_parts(v):
    mean = jnp.mean(v, axis=-1, keepdims=True)
    centered = v - mean
    var = jnp.mean(centered * centered, axis=-1, keepdims=True)
    r = lax.rsqrt(var + EPS)
    return centered * r, r


def fold_rows(v):
    rows, cols = v.shape
    return jnp.sum(v.reshape(rows // 8, 8, cols), axis=0)


def lane_mask(rows, test):
    lane = lax.broadcasted_iota(jnp.int32, (rows, SLAB), 1)
    return jnp.where(test(lane), 1.0, 0.0).astype(BF)


def attn_fwd_body(
    x_ref, xb_ref, page_ref, wa_ref, wb_ref, qva_ref, qvb_ref, bias_ref, pa_ref, pb_ref, ob_ref, gain_ref, shift_ref,
    n_ref, qkv_ref, mixed_ref, att_ref, p_ref,
    scr, cur, nxt, att_scr, att_rows,
):
    scale = (HEAD ** -0.5) * LOG2E

    @pl.when(pl.program_id(0) == 0)
    def _():
        scr[ROWS:, :] = jnp.zeros((scr.shape[0] - ROWS, scr.shape[1]), F32)

    def prepare():
        n, _ = norm_parts(x_ref[...].astype(F32))
        n = (n * gain_ref[0:1] + shift_ref[0:1]).astype(BF)
        n_ref[...] = n
        return n

    def project(n, i):
        for s, (w_ref, b_ref) in enumerate(((wa_ref, qva_ref), (wb_ref, qvb_ref))):
            cols = slice(512 * i + s * SLAB, 512 * i + s * SLAB + SLAB)
            out = dot(n, w_ref[i])
            scr[:ROWS, cols] = out if i == 1 else out + b_ref[i // 2 : i // 2 + 1]
        for w in range(GROUP):
            v = scr[w * WIN : w * WIN + LANES, 512 * i : 512 * i + 512].astype(BF)
            nxt[w, :, 512 * i : 512 * i + 512] = v
            qkv_ref[w, :, 512 * i : 512 * i + 512] = v

    def attend(beside):
        even = lane_mask(LANES, lambda c: (c // HEAD) % 2 == 0)
        odd = lane_mask(LANES, lambda c: (c // HEAD) % 2 == 1)
        low = lane_mask(KEYS, lambda c: c % 128 < 64)[:, :128]
        high = lane_mask(KEYS, lambda c: c % 128 >= 64)[:, :128]
        query_lane = lax.broadcasted_iota(jnp.int32, (1, SLAB), 1) % LANES
        valid = jnp.where(query_lane < WIN, 1.0, 0.0)
        first_head = lax.broadcasted_iota(jnp.int32, (2 * HEAD, LANES), 0) < HEAD
        for w in range(GROUP):
            pages = jnp.broadcast_to(page_ref[w], (LANES, LANES))
            mask = jnp.where(pages == pages.T, 0.0, NEG)[:KEYS]
            mask = jnp.concatenate([mask, mask], axis=1)
            scores, v_ts = [], []
            for s in range(2):
                lo = s * SLAB
                q = cur[w, :, lo : lo + SLAB]
                k = cur[w, :KEYS, 512 + lo : 512 + lo + SLAB]
                v_ts.append(cur[w, :, 1024 + lo : 1024 + lo + SLAB].T)
                q2 = jnp.concatenate([q * even, q * odd], axis=0)
                for p in range(4):
                    cols = slice(128 * (p // 2), 128 * (p // 2) + 128)
                    scores.append(dot_nt(k[:, cols] * (low if p % 2 == 0 else high), q2[:, cols]))
            beside(w)
            for s in range(2):
                outs = []
                for p in range(4):
                    st = scores[4 * s + p] * scale + bias_ref[4 * s + p] + mask
                    e = jnp.exp2(st - jnp.max(st, axis=0, keepdims=True))
                    pt = (e * (valid / jnp.sum(e, axis=0, keepdims=True))).astype(BF)
                    p_ref[w, 4 * s + p] = pt
                    ot = dot(v_ts[s][64 * p : 64 * p + 64, :KEYS], pt)
                    outs.append(jnp.where(first_head, ot[:, :LANES], ot[:, LANES:]))
                att_scr[w, :, s * SLAB : s * SLAB + SLAB] = jnp.concatenate(outs, axis=0).T
        for w in range(GROUP):
            att_rows[w * WIN : w * WIN + WIN, :] = att_scr[w, :WIN, :]
        att = att_rows[...].astype(BF)
        att_ref[...] = att
        mixed_ref[...] = (
            xb_ref[...].astype(F32) + ob_ref[0:1] + dot(att[:, :SLAB], pa_ref[...]) + dot(att[:, SLAB:], pb_ref[...])
        )

    step, end = pl.program_id(0), pl.num_programs(0) - 1

    @pl.when(step == 0)
    def _():
        n = prepare()
        for i in range(3):
            project(n, i)
        cur[...] = nxt[...]

    @pl.when((step > 0) & (step < end))
    def _():
        n = prepare()
        attend(lambda w: project(n, w) if w < 3 else None)
        cur[...] = nxt[...]

    @pl.when(step == end)
    def _():
        attend(lambda w: None)


def gelu_parts(h):
    phi = 0.5 + 0.5 * lax.erf(h * 0.7071067811865476)
    return phi, jnp.exp2(h * h * (-0.5 * LOG2E)) * 0.3989422804014327


def ffn_body(
    mixed_ref, go_ref, att_ref, w1a_ref, w1b_ref, w2a_ref, w2b_ref, b1a_ref, b1b_ref, pa_ref, pb_ref, gain_ref, shift_ref,
    act_ref, gm_ref, do_ref, gfa_ref, gfb_ref, gb1_ref, gs_ref,
    acc1, acc2, accp, accb, accs,
):
    step = pl.program_id(0)

    @pl.when(step == 0)
    def _():
        acc1[...] = jnp.zeros_like(acc1)
        acc2[...] = jnp.zeros_like(acc2)
        accp[...] = jnp.zeros_like(accp)
        accb[...] = jnp.zeros_like(accb)
        accs[...] = jnp.zeros_like(accs)

    mixed = mixed_ref[...]
    nh, r = norm_parts(mixed)
    n2 = (nh * gain_ref[1:2] + shift_ref[1:2]).astype(BF)
    go = go_ref[...]
    gn = jnp.zeros_like(mixed)
    per_half = 1024 // CHUNK

    def weights(c):
        col = slice(CHUNK * (c % per_half), CHUNK * (c % per_half) + CHUNK)
        return ((w1a_ref, w2a_ref, b1a_ref) if c < per_half else (w1b_ref, w2b_ref, b1b_ref)) + (col,)

    def front(c):
        w1_ref, w2_ref, b1_ref, col = weights(c)
        return dot(n2, w1_ref[:, col]) + b1_ref[0:1, col], dot_nt(go, w2_ref[col, :])

    ready = front(0)
    for c in range(2 * per_half):
        h, ga = ready
        if c + 1 < 2 * per_half:
            ready = front(c + 1)
        w1_ref, _, _, col = weights(c)
        full = slice(CHUNK * c, CHUNK * c + CHUNK)
        phi, density = gelu_parts(h)
        act = (h * phi).astype(BF)
        act_ref[:, full] = act
        ghf = ga * (phi + h * density)
        accb[:, full] += fold_rows(ghf)
        gh = ghf.astype(BF)
        gn += dot_nt(gh, w1_ref[:, col])
        acc2[full, :] += dot_tn(act, go)
        acc1[:, full] += dot_tn(n2, gh)
    gof = go.astype(F32)
    e = gn * gain_ref[1:2]
    gm = gof + r * (
        e - jnp.mean(e, axis=-1, keepdims=True) - nh * jnp.mean(e * nh, axis=-1, keepdims=True)
    )
    gm_ref[...] = gm
    gml = gm.astype(BF)
    accp[...] += dot_tn(att_ref[...], gml)
    do_ref[:, :SLAB] = dot_nt(gml, pa_ref[...]).astype(BF)
    do_ref[:, SLAB:] = dot_nt(gml, pb_ref[...]).astype(BF)
    accs[0] += fold_rows(gm)
    accs[1] += fold_rows(gof)
    accs[2] += fold_rows(gn * nh)
    accs[3] += fold_rows(gn)

    @pl.when(step == pl.num_programs(0) - 1)
    def _():
        for s, gf_ref in enumerate((gfa_ref, gfb_ref)):
            gf_ref[:1024] = acc2[1024 * s : 1024 * s + 1024, :].astype(BF)
            gf_ref[1024:1536] = acc1[:, 1024 * s : 1024 * s + 512].astype(BF)
            gf_ref[1536:2048] = acc1[:, 1024 * s + 512 : 1024 * s + 1024].astype(BF)
            gf_ref[2048:2304] = accp[SLAB * s : SLAB * s + SLAB, :].astype(BF)
        gb1_ref[...] = jnp.sum(accb[...], axis=0, keepdims=True)
        gs_ref[...] = jnp.sum(accs[...], axis=1)


def out_body(mixed_ref, act_ref, w2a_ref, w2b_ref, ob_ref, *refs):
    out_ref = refs[-1]
    out = mixed_ref[...] + ob_ref[1:2] + dot(act_ref[:, :1024], w2a_ref[...]) + dot(act_ref[:, 1024:], w2b_ref[...])
    out_ref[...] = out.astype(BF)


def attn_bwd_body(
    n_ref, do_ref, qkv_ref, p_ref, d_ref, t_ref, gqa_ref, gqb_ref, gqv_ref, scr, prev, acc, accb
):
    scale = HEAD ** -0.5
    step, end = pl.program_id(0), pl.num_programs(0) - 1

    @pl.when(step == 0)
    def _():
        scr[ROWS:, :512] = jnp.zeros((scr.shape[0] - ROWS, 512), F32)
        t_ref[...] = jnp.zeros_like(t_ref)
        prev[...] = jnp.zeros_like(prev)
        acc[...] = jnp.zeros_like(acc)
        accb[...] = jnp.zeros_like(accb)

    def weights(i):
        cols = slice(512 * i, 512 * i + 512)
        d = prev[:, cols]
        acc[:, cols] += dot_tn(n_ref[...], d)
        if i != 1:
            accb[i // 2] += fold_rows(d.astype(F32))

    def windows():
        scr[:ROWS, :512] = do_ref[...].astype(F32)
        row = lax.broadcasted_iota(jnp.int32, (LANES, 512), 0)
        dos = [jnp.where(row < WIN, scr[w * WIN : w * WIN + LANES, :512], 0.0).astype(BF) for w in range(GROUP)]
        even = lane_mask(LANES, lambda c: (c // HEAD) % 2 == 0)
        odd = lane_mask(LANES, lambda c: (c // HEAD) % 2 == 1)
        low = lane_mask(KEYS, lambda c: c % 128 < 64)[:, :128]
        high = lane_mask(KEYS, lambda c: c % 128 >= 64)[:, :128]
        first_head = lax.broadcasted_iota(jnp.int32, (2 * HEAD, LANES), 0) < HEAD
        first_pair = lax.broadcasted_iota(jnp.int32, (KEYS, 128), 1) < 64
        for w in range(GROUP):
            rows = slice(w * WIN, w * WIN + WIN)
            q2s, d2s, k_ts, dps = [], [], [], []
            for s in range(2):
                lo = s * SLAB
                q = qkv_ref[w, :, lo : lo + SLAB]
                v = qkv_ref[w, :KEYS, 1024 + lo : 1024 + lo + SLAB]
                do = dos[w][:, lo : lo + SLAB]
                q2s.append(jnp.concatenate([q * even, q * odd], axis=0))
                d2s.append(jnp.concatenate([do * even, do * odd], axis=0))
                k_ts.append(qkv_ref[w, :, 512 + lo : 512 + lo + SLAB].T)
                for p in range(4):
                    cols = slice(128 * (p // 2), 128 * (p // 2) + 128)
                    dps.append(dot_nt(v[:, cols] * (low if p % 2 == 0 else high), d2s[s][:, cols]))
            if w < 3:
                weights(w)
            for s in range(2):
                lo = s * SLAB
                outs, dks, dvs = [], [], []
                for p in range(4):
                    cols = slice(128 * (p // 2), 128 * (p // 2) + 128)
                    pt = p_ref[w, 4 * s + p]
                    ptf = pt.astype(F32)
                    dp = dps[4 * s + p]
                    ds = ptf * (dp - jnp.sum(dp * ptf, axis=0, keepdims=True))
                    t_ref[4 * s + p] += ds
                    ds = ds.astype(BF)
                    qt = dot(k_ts[s][64 * p : 64 * p + 64, :KEYS], ds)
                    outs.append(jnp.where(first_head, qt[:, :LANES], qt[:, LANES:]))
                    dks.append(dot(ds, q2s[s][:, cols]))
                    dvs.append(dot(pt, d2s[s][:, cols]))
                scr[rows, lo : lo + SLAB] = (jnp.concatenate(outs, axis=0).T * scale)[:WIN]
                for g in range(2):
                    cols = slice(512 + lo + 128 * g, 512 + lo + 128 * g + 128)
                    scr[rows, cols] = (jnp.where(first_pair, dks[2 * g], dks[2 * g + 1]) * scale)[:WIN]
                    cols = slice(1024 + lo + 128 * g, 1024 + lo + 128 * g + 128)
                    scr[rows, cols] = jnp.where(first_pair, dvs[2 * g], dvs[2 * g + 1])[:WIN]
        d = scr[:ROWS, :].astype(BF)
        d_ref[...] = d
        prev[...] = d

    @pl.when(step < end)
    def _():
        windows()

    @pl.when(step == end)
    def _():
        for i in range(3):
            weights(i)
        for s, gq_ref in enumerate((gqa_ref, gqb_ref)):
            for i in range(3):
                cols = slice(512 * i + SLAB * s, 512 * i + SLAB * s + SLAB)
                gq_ref[256 * i : 256 * i + 256, :256] = acc[:256, cols].astype(BF)
                gq_ref[256 * i : 256 * i + 256, 256:] = acc[256:, cols].astype(BF)
        gqv_ref[...] = jnp.sum(accb[...], axis=1)


def input_grad_body(x_ref, gm_ref, d_ref, wa_ref, wb_ref, gain_ref, *refs):
    gin_ref, gs_ref, accs = refs[-3:]
    step = pl.program_id(0)

    @pl.when(step == 0)
    def _():
        accs[...] = jnp.zeros_like(accs)

    gn = jnp.zeros(gm_ref.shape, F32)
    for i in range(3):
        for s, w_ref in enumerate((wa_ref, wb_ref)):
            gn += dot_nt(d_ref[:, 512 * i + SLAB * s : 512 * i + SLAB * s + SLAB], w_ref[i])
    nh, r = norm_parts(x_ref[...].astype(F32))
    e = gn * gain_ref[0:1]
    gin = gm_ref[...] + r * (
        e - jnp.mean(e, axis=-1, keepdims=True) - nh * jnp.mean(e * nh, axis=-1, keepdims=True)
    )
    gin_ref[...] = gin.astype(BF)
    accs[0] += fold_rows(gn * nh)
    accs[1] += fold_rows(gn)

    @pl.when(step == pl.num_programs(0) - 1)
    def _():
        gs_ref[...] = jnp.sum(accs[...], axis=1)


def shaped(shape, dtype):
    return jax.ShapeDtypeStruct(shape, dtype)


def whole(shape):
    return pl.BlockSpec(shape, lambda i: (0,) * len(shape))


def by_rows(*shape, rows=ROWS):
    return pl.BlockSpec((rows,) + shape, lambda i: (i,) + (0,) * len(shape))


def dense_rows(*shape):
    return by_rows(*shape, rows=DENSE)


def by_windows(*shape):
    return pl.BlockSpec((GROUP,) + shape, lambda i: (i,) + (0,) * len(shape))


PARAMS = pltpu.CompilerParams(vmem_limit_bytes=60 << 20, dimension_semantics=("arbitrary",))


def attn_fwd(x, pages, wa, wb, qva, qvb, bias, pa, pb, ob, gain, shift):
    rows = x.shape[0]
    windows = rows // WIN
    last = rows // ROWS - 1
    front = lambda *shape: pl.BlockSpec(shape, lambda i: (jnp.minimum(i, last),) + (0,) * (len(shape) - 1))
    back = lambda *shape: pl.BlockSpec(shape, lambda i: (jnp.maximum(i - 1, 0),) + (0,) * (len(shape) - 1))
    return pl.pallas_call(
        attn_fwd_body,
        name="attn_fwd",
        grid=(rows // ROWS + 1,),
        in_specs=[front(ROWS, 512), back(ROWS, 512), back(GROUP, 1, LANES)]
        + [whole(a.shape) for a in (wa, wb, qva, qvb, bias, pa, pb, ob, gain, shift)],
        out_specs=[
            front(ROWS, 512), front(GROUP, LANES, 1536), back(ROWS, 512), back(ROWS, 512),
            back(GROUP, 8, KEYS, SLAB),
        ],
        out_shape=[
            shaped((rows, 512), BF),
            shaped((windows, LANES, 1536), BF),
            shaped((rows, 512), F32),
            shaped((rows, 512), BF),
            shaped((windows, 8, KEYS, SLAB), BF),
        ],
        scratch_shapes=[
            pltpu.VMEM((ROWS + 32, 1536), F32),
            pltpu.VMEM((GROUP, LANES, 1536), BF),
            pltpu.VMEM((GROUP, LANES, 1536), BF),
            pltpu.VMEM((GROUP, LANES, 512), F32),
            pltpu.VMEM((ROWS, 512), F32),
        ],
        compiler_params=PARAMS,
    )(x, x, pages, wa, wb, qva, qvb, bias, pa, pb, ob, gain, shift)


def cost(flops, moved):
    return pl.CostEstimate(flops=int(flops), bytes_accessed=int(moved), transcendentals=0)


def ffn(mixed, go, att, w1a, w1b, w2a, w2b, b1a, b1b, pa, pb, gain, shift):
    rows = mixed.shape[0]
    small = [w1a, w1b, w2a, w2b, b1a, b1b, pa, pb, gain, shift]
    return pl.pallas_call(
        ffn_body,
        name="feed_forward",
        grid=(rows // DENSE,),
        in_specs=[dense_rows(512)] * 3 + [whole(a.shape) for a in small],
        out_specs=[dense_rows(2048), dense_rows(512), dense_rows(512)]
        + [whole((2304, 512)), whole((2304, 512)), whole((1, 2048)), whole((4, 512))],
        out_shape=[
            shaped((rows, 2048), BF),
            shaped((rows, 512), F32),
            shaped((rows, 512), BF),
            shaped((2304, 512), BF),
            shaped((2304, 512), BF),
            shaped((1, 2048), F32),
            shaped((4, 512), F32),
        ],
        scratch_shapes=[
            pltpu.VMEM((512, 2048), F32),
            pltpu.VMEM((2048, 512), F32),
            pltpu.VMEM((512, 512), F32),
            pltpu.VMEM((8, 2048), F32),
            pltpu.VMEM((4, 8, 512), F32),
        ],
        compiler_params=PARAMS,
        cost_estimate=cost(50e9, 40e6),
    )(mixed, go, att, *small)


def third_rows(part):
    return lambda *shape: pl.BlockSpec((ROWS,) + shape, lambda i: (THIRD * part + i,) + (0,) * len(shape))


def out_rows(part, mixed, act, w2a, w2b, ob, *old):
    rows = mixed.shape[0]
    spec = third_rows(part)
    return pl.pallas_call(
        out_body,
        name="block_out",
        grid=(THIRD,),
        in_specs=[spec(512), spec(2048)] + [whole(a.shape) for a in (w2a, w2b, ob)] + [pl.BlockSpec(memory_space=pl.ANY)] * len(old),
        out_specs=spec(512),
        out_shape=shaped((rows, 512), BF),
        input_output_aliases={5: 0} if old else {},
        compiler_params=PARAMS,
        cost_estimate=cost(3e9, 7e6),
    )(mixed, act, w2a, w2b, ob, *old)


def attn_bwd(n, do, qkv, probs):
    rows = n.shape[0]
    last = rows // ROWS - 1
    front = lambda *shape: pl.BlockSpec(shape, lambda i: (jnp.minimum(i, last),) + (0,) * (len(shape) - 1))
    back = lambda *shape: pl.BlockSpec(shape, lambda i: (jnp.maximum(i - 1, 0),) + (0,) * (len(shape) - 1))
    return pl.pallas_call(
        attn_bwd_body,
        name="attn_bwd",
        grid=(rows // ROWS + 1,),
        in_specs=[back(ROWS, 512), front(ROWS, 512), front(GROUP, LANES, 1536), front(GROUP, 8, KEYS, SLAB)],
        out_specs=[
            front(ROWS, 1536), whole((8, KEYS, SLAB)), whole((768, 512)), whole((768, 512)), whole((2, 512)),
        ],
        out_shape=[
            shaped((rows, 1536), BF), shaped((8, KEYS, SLAB), F32), shaped((768, 512), BF), shaped((768, 512), BF),
            shaped((2, 512), F32),
        ],
        scratch_shapes=[
            pltpu.VMEM((ROWS + 32, 1536), F32),
            pltpu.VMEM((ROWS, 1536), BF),
            pltpu.VMEM((512, 1536), F32),
            pltpu.VMEM((2, 8, 512), F32),
        ],
        compiler_params=PARAMS,
        cost_estimate=cost(30e9, 60e6),
    )(n, do, qkv, probs)


def input_grad(part, x, gm, d, wa, wb, gain, *old):
    rows = x.shape[0]
    spec = third_rows(part)
    return pl.pallas_call(
        input_grad_body,
        name="input_grad",
        grid=(THIRD,),
        in_specs=[spec(512), spec(512), spec(1536)] + [whole(a.shape) for a in (wa, wb, gain)] + [pl.BlockSpec(memory_space=pl.ANY)] * len(old),
        out_specs=[spec(512), whole((2, 512))],
        out_shape=[shaped((rows, 512), BF), shaped((2, 512), F32)],
        scratch_shapes=[pltpu.VMEM((2, 8, 512), F32)],
        input_output_aliases={6: 0} if old else {},
        compiler_params=PARAMS,
        cost_estimate=cost(3e9, 7e6),
    )(x, gm, d, wa, wb, gain, *old)


def offset_onehot(index_row):
    slot = lax.broadcasted_iota(jnp.int32, (TAB, SLAB), 0).astype(F32)
    return jnp.where(slot == index_row, 1.0, 0.0).astype(BF)


def bias_body(rel_ref, ta_ref, tb_ref, bias_ref, idx_ref, scr):
    scr[...] = jnp.zeros_like(scr)
    scr[:WIN, :WIN] = rel_ref[...].astype(F32)
    scr[...] = scr[...].T
    lane = lax.broadcasted_iota(jnp.int32, (16, SLAB), 1)
    blank = jnp.zeros((16, SLAB - LANES), F32)

    def place(row, width, at):
        piece = jnp.concatenate([scr[row : row + 16, :], blank], axis=1)
        return pltpu.roll(jnp.where(lane < width, piece, 0.0), at, 1)

    idx = place(0, WIN, WIN - WS)
    for d in range(WS - 1):
        idx += place(WS * (WS - 1 - d), WS, WS * d)
    idx = jnp.where(lane < WIN + WIN - WS, idx, -1.0)
    idx_ref[...] = idx
    table = jnp.concatenate([ta_ref[...], tb_ref[...]], axis=1) * LOG2E
    high = table.astype(BF)
    rest = table - high.astype(F32)
    mid = rest.astype(BF)
    table = jnp.concatenate([high, mid, (rest - mid.astype(F32)).astype(BF)], axis=1)
    row = lax.broadcasted_iota(jnp.int32, (16, 48), 0)
    col = lax.broadcasted_iota(jnp.int32, (16, 48), 1)
    pick = jnp.where(col % 16 == 2 * (row % 8) + row // 8, 1.0, 0.0).astype(BF)
    for jx in range(WS):
        parts = dot_tn(table, offset_onehot(idx[jx : jx + 1]))
        values = dot(pick, parts.astype(BF))
        for jy in range(WS):
            shift = WS * (WS - 1 - jy)
            moved = pltpu.roll(values, (SLAB - shift) % SLAB, 1) if shift else values
            bias_ref[:, WS * jy + jx, :LANES] = moved[:8, :LANES]
            bias_ref[:, WS * jy + jx, LANES:] = moved[8:, :LANES]
    for key in range(WIN, KEYS):
        bias_ref[:, key, :] = jnp.zeros((8, SLAB), F32)


def expand_table(rel_index, ta, tb):
    return pl.pallas_call(
        bias_body,
        name="bias",
        out_shape=[shaped((8, KEYS, SLAB), F32), shaped((16, SLAB), F32)],
        scratch_shapes=[pltpu.VMEM((LANES, LANES), F32)],
        compiler_params=pltpu.CompilerParams(vmem_limit_bytes=16 << 20),
        cost_estimate=cost(3e9, 1e6),
    )(rel_index, ta, tb)


def small_body(idx_ref, t_ref, gs2_ref, gs1a_ref, gs1b_ref, gs1c_ref, gb1_ref, gqv_ref, own_ref, other_ref, scr):
    total = jnp.zeros((32, TAB), F32)
    blank = jnp.zeros((8, SLAB - LANES), F32)
    for jx in range(WS):
        even = jnp.zeros((8, SLAB), F32)
        odd = jnp.zeros((8, SLAB), F32)
        for jy in range(WS):
            shift = WS * (WS - 1 - jy)
            even += pltpu.roll(jnp.concatenate([t_ref[:, WS * jy + jx, :LANES], blank], axis=1), shift, 1)
            odd += pltpu.roll(jnp.concatenate([t_ref[:, WS * jy + jx, LANES:], blank], axis=1), shift, 1)
        heads = jnp.concatenate([even, odd], axis=0)
        high = heads.astype(BF)
        rest = (heads - high.astype(F32)).astype(BF)
        total += dot_nt(jnp.concatenate([high, rest], axis=0), offset_onehot(idx_ref[jx : jx + 1]))
    total = total[:16] + total[16:]
    for s, out_ref in enumerate((own_ref, other_ref)):
        scr[...] = jnp.zeros_like(scr)
        scr[0:4] = gs2_ref[...]
        scr[4:6] = gs1a_ref[...] + gs1b_ref[...] + gs1c_ref[...]
        scr[6:7] = gb1_ref[:, 1024 * s : 1024 * s + 512]
        scr[7:8] = gb1_ref[:, 1024 * s + 512 : 1024 * s + 1024]
        scr[8:9, :SLAB] = gqv_ref[0:1, SLAB * s : SLAB * s + SLAB]
        scr[8:9, SLAB:] = gqv_ref[1:2, SLAB * s : SLAB * s + SLAB]
        scr[16:20, :TAB] = total[4 * s : 4 * s + 4]
        scr[20:24, :TAB] = total[8 + 4 * s : 12 + 4 * s]
        out_ref[...] = scr[...].astype(BF)


def small_sums(*args):
    return pl.pallas_call(
        small_body,
        name="small_sums",
        out_shape=[shaped((32, 512), BF), shaped((32, 512), BF)],
        scratch_shapes=[pltpu.VMEM((32, 512), F32)],
        compiler_params=pltpu.CompilerParams(vmem_limit_bytes=16 << 20),
        cost_estimate=cost(3e9, 1e6),
    )(*args)


def finish_body(q_ref, late_ref, gq_ref, gqv_ref, gob_ref, gg_ref, gh_ref, gb1_ref, gt_ref, scr):
    for i in range(3):
        q = q_ref[256 * i : 256 * i + 256, :].astype(F32)
        gq_ref[i, :256, :] = q[:, :256]
        gq_ref[i, 256:, :] = q[:, 256:]
    late = late_ref[...].astype(F32)
    gob_ref[...] = late[0:2]
    gg_ref[0:1] = late[4:5]
    gg_ref[1:2] = late[2:3]
    gh_ref[0:1] = late[5:6]
    gh_ref[1:2] = late[3:4]
    gb1_ref[:, :512] = late[6:7]
    gb1_ref[:, 512:] = late[7:8]
    gqv_ref[0:1] = late[8:9, :SLAB]
    gqv_ref[1:2] = late[8:9, SLAB:]
    scr[...] = jnp.zeros_like(scr)
    for h in range(8):
        r = 16 + 4 * (h % 2) + h // 2
        scr[h : h + 1, :] = late[r : r + 1, :]
    gt_ref[...] = scr[...].T[:TAB, :8]


def finish(q, late):
    return pl.pallas_call(
        finish_body,
        name="finish",
        out_shape=[
            shaped((3, 512, SLAB), F32), shaped((2, SLAB), F32), shaped((2, 512), F32), shaped((2, 512), F32),
            shaped((2, 512), F32), shaped((1, 1024), F32), shaped((TAB, 8), F32),
        ],
        scratch_shapes=[pltpu.VMEM((LANES, 512), F32)],
        compiler_params=pltpu.CompilerParams(vmem_limit_bytes=16 << 20),
        cost_estimate=cost(1e9, 4e6),
    )(q, late)


SWAP = [(0, 1), (1, 0)]
SPLIT = True


def dp_bits(size):
    bits = []
    while 1 << len(bits) < size:
        bits.append(1 << len(bits))
    return bits


class Chain:
    def __init__(self, size, own, orders):
        self.orders, self.size, self.own, self.late = orders, size, own, None
        tp, dp = lax.axis_index("tp"), lax.axis_index("dp")
        self.upper = [jnp.where(tp == 0, dp & p, dp & q) != 0 for p, q in zip(*orders)]
        last = len(orders[0]) - 1
        self.steps = [("half", k) for k in range(last)] + [("full", last)]
        self.steps += [("join", k) for k in range(last - 1, -1, -1)]

    def begin(self):
        kind, k = self.steps[0]
        if kind == "half":
            half = self.own.shape[0] // 2
            up = self.upper[k].astype(jnp.int32)
            send = lax.dynamic_slice_in_dim(self.own, (1 - up) * half, half, 0)
            self.own = lax.dynamic_slice_in_dim(self.own, up * half, half, 0)
            return send
        if self.late is not None:
            return jnp.concatenate([self.own, self.late], axis=0)
        return self.own

    def move(self, send):
        k = self.steps[0][1]
        perm = [(2 * i + t, 2 * (i ^ self.orders[t][k]) + t) for i in range(self.size) for t in range(2)]
        return lax.ppermute(send, ("dp", "tp"), perm)

    def end(self, got):
        kind, k = self.steps.pop(0)
        if kind in ("full", "join") and self.late is not None:
            rows = self.own.shape[0]
            self.late = self.late + got[rows:]
            got = got[:rows]
        if kind == "join":
            up = self.upper[k]
            self.own = jnp.concatenate([jnp.where(up, got, self.own), jnp.where(up, self.own, got)], axis=0)
        else:
            self.own = self.own + got


class Pair:
    def __init__(self, own, other):
        self.own, self.other = own, other

    def begin(self):
        return self.other

    def move(self, send):
        return lax.ppermute(send, "tp", SWAP)

    def end(self, got):
        self.got = got

    def total(self):
        return self.own + self.got


tie = lax.optimization_barrier


def advance(chains, work=None, *inputs):
    sends, inputs = tie(([c.begin() for c in chains], inputs))
    gots = [c.move(v) for c, v in zip(chains, sends)]
    result = None if work is None else work(*inputs)
    gots, result = tie((gots, result))
    for c, got in zip(chains, gots):
        c.end(got)
    return result


class Flight:
    def __init__(self, chains):
        self.chains, self.sends, self.gots = chains, [c.begin() for c in chains], None

    def beside(self, chains, work, *inputs):
        sends = [c.begin() for c in chains]
        self.sends, sends, inputs = tie((self.sends, sends, inputs))
        if self.gots is None:
            self.gots = [c.move(v) for c, v in zip(self.chains, self.sends)]
        gots = [c.move(v) for c, v in zip(chains, sends)]
        gots, result = tie((gots, work(*inputs)))
        self.last = (gots, result)
        for c, got in zip(chains, gots):
            c.end(got)
        return result

    def land(self):
        self.gots, _ = tie((self.gots, self.last))
        for c, got in zip(self.chains, self.gots):
            c.end(got)


class Slices:
    def __init__(self, chain, count):
        self.chain, self.send, self.gots = chain, chain.begin(), []
        rows = self.send.shape[0]
        self.cuts = [rows * i // count // 8 * 8 for i in range(count)] + [rows]

    def begin(self):
        i = len(self.gots)
        return self.send[self.cuts[i] : self.cuts[i + 1]]

    def move(self, send):
        return self.chain.move(send)

    def end(self, got):
        self.gots.append(got)
        if len(self.gots) + 1 == len(self.cuts):
            self.chain.end(jnp.concatenate(self.gots, axis=0))


def forward(x, pages, bias, wa, wb, qva, qvb, pa, pb, w1a, w1b, b1a, b1b, w2a, w2b, ob, gain, shift, go):
    n, qkv, mixed, att, probs = attn_fwd(x, pages, wa, wb, qva, qvb, bias, pa, pb, ob, gain, shift)
    act, gm, do, gfa, gfb, gb1, gs2 = ffn(mixed, go, att, w1a, w1b, w2a, w2b, b1a, b1b, pa, pb, gain, shift)
    return mixed, n, qkv, probs, act, gm, do, (gfa, gfb), gb1, gs2


def local_block(x, pages, rel_index, wa, wb, qva, qvb, pa, pb, w1a, w1b, b1a, b1b, w2a, w2b, ob, gain, shift, ta, tb, go):
    bias, idx = expand_table(rel_index, ta, tb)
    mixed, n, qkv, probs, act, gm, do, gf, gb1, gs2 = forward(
        x, pages, bias, wa, wb, qva, qvb, pa, pb, w1a, w1b, b1a, b1b, w2a, w2b, ob, gain, shift, go
    )
    d, t, gqa, gqb, gqv = attn_bwd(n, do, qkv, probs)
    gin, out, sums = (), (), []
    for i in range(3):
        *gin, part = input_grad(i, x, gm, d, wa, wb, gain, *gin)
        sums.append(part)
        out = [out_rows(i, mixed, act, w2a, w2b, ob, *out)]
    own, other = small_sums(idx, t, gs2, *sums, gb1, gqv)
    gin, out = gin[0], out[0]
    return out, gin, gf, finish(gqa, own), finish(gqb, other)


def per_device(
    dp_size, inputs, page_of, rel_index, w_qkv, qv_bias, w_proj, w_fc1, fc1_bias, w_fc2, out_biases, norm_gains,
    norm_biases, bias_table, out_grad,
):
    me = lax.axis_index("tp")
    windows = inputs.shape[0] // WIN
    swap = lambda v: lax.ppermute(v, "tp", SWAP)
    pages = lax.dynamic_slice_in_dim(page_of.reshape(2 * windows, WIN), me * windows, windows, 0)
    pages = jnp.pad(pages.astype(F32), ((0, 0), (0, LANES - WIN)), constant_values=-1.0)[:, None, :]
    w_qkv_b, qv_bias_b, w_proj_b, table_b = (swap(v) for v in (w_qkv, qv_bias, w_proj, bias_table))
    later, w_qkv_b, table_b = tie(((w_fc1, fc1_bias, w_fc2), w_qkv_b, table_b))
    w_fc1_b, fc1_bias_b, w_fc2_b = (swap(v) for v in later)
    bias, idx = expand_table(rel_index, bias_table, table_b)
    mixed, n, qkv, probs, act, gm, do, gf, gb1, gs2 = forward(
        inputs, pages, bias, w_qkv, w_qkv_b, qv_bias, qv_bias_b, w_proj, w_proj_b, w_fc1, w_fc1_b,
        fc1_bias[None], fc1_bias_b[None], w_fc2, w_fc2_b, out_biases, norm_gains, norm_biases, out_grad,
    )
    bits = dp_bits(dp_size)
    turned = bits[1:] + bits[:1]
    mid = len(bits) // 2
    deep = bits[mid:-1] + bits[:mid] + bits[-1:]
    grad = lambda i, *old: (functools.partial(input_grad, i), inputs, gm, d, w_qkv, w_qkv_b, norm_gains) + old
    rows_out = lambda i, *old: (functools.partial(out_rows, i), mixed, act, w_fc2, w_fc2_b, out_biases) + old

    pair = Pair(*gf)
    out = advance([pair], *rows_out(0))
    if SPLIT:
        cut = 2 * pair.other.shape[0] // 3
        f = [Chain(dp_size, pair.total()[:cut], (bits, turned)), Chain(dp_size, pair.total()[cut:], (deep, deep))]
    else:
        f = [Chain(dp_size, pair.total(), (bits, turned))]
    d, t, gqa, gqb, gqv = advance(f, attn_bwd, n, do, qkv, probs)
    pair = Pair(gqa, gqb)
    gin, gs1a = advance(f + [pair], *grad(0))
    q = Chain(dp_size, pair.total(), (bits, turned))
    gin, gs1b = advance(f + [q], *grad(1, gin))
    gin, gs1c = advance(f + [q], *grad(2, gin))
    flight = Flight(f)
    low = Pair(*flight.beside([], small_sums, idx, t, gs2, gs1a, gs1b, gs1c, gb1, gqv))
    out = flight.beside([q, low], *rows_out(1, out))
    flight.land()
    q.late = low.total()
    while len(f[0].steps) > 1:
        advance(f + [q])
    parts = [Slices(c, max(1, len(q.steps) - 1)) for c in f]
    out = advance(parts + [q], *rows_out(2, out))
    while f[0].steps:
        advance(parts + [q])
    g_f = jnp.concatenate([c.own for c in f])
    g_fc2 = g_f[:1024].astype(F32)
    g_fc1 = jnp.concatenate([g_f[1024:1536], g_f[1536:2048]], axis=1).astype(F32)
    g_proj = g_f[2048:].astype(F32)
    while q.steps:
        advance([q])
    g_qkv, g_qv, g_ob, g_gains, g_shifts, g_fc1_bias, g_table = finish(q.own, q.late)
    return out, gin, g_qkv, g_qv, g_proj, g_fc1, g_fc1_bias.reshape(-1), g_fc2, g_ob, g_gains, g_shifts, g_table


def solution(mesh):
    rows = P(("dp", "tp"), None)
    placed = (
        rows, P("dp"), P(), P(None, None, "tp"), P(None, "tp"), P("tp", None), P(None, "tp"), P("tp"),
        P("tp", None), P(), P(), P(), P(None, "tp"), rows,
    )
    results = (
        rows, rows, P(None, None, "tp"), P(None, "tp"), P("tp", None), P(None, "tp"), P("tp"), P("tp", None),
        P(), P(), P(), P(None, "tp"),
    )
    return jax.shard_map(
        functools.partial(per_device, mesh.shape["dp"]), mesh=mesh, in_specs=placed, out_specs=results, check_vma=False
    )
```

profile of v0, /device:TPU:0, one launch (start us, length us, event | category | flops | bytes accessed | tf_op | source)
XLA Modules:
  0.0 195.4 jit_solution(9748723294376661503)
XLA Ops:
  0.6 0.5 collective-permute-start
  1.2 0.8 copy.30.ta_ref
  2.1 1.4 collective-permute-done.1.tb_ref
  3.7 0.3 collective-permute-start.5
  4.2 0.3 collective-permute-start.3
  4.5 0.8 reshape.30
  5.4 0.6 pad.4
  6.2 0.8 copy-done.1
  7.0 1.8 bias.1
  8.9 0.9 copy-done
  9.8 0.6 copy-done.14
  10.5 23.1 %attn_fwd.1 = (bf16[2400,512]{1,0:T(8,128)(2,1)}, bf16[24,128,1536]{2,1,0:T(8,128)(2,1)}, f32[2400,512]{1,0:T(8,128)}, bf16[2400,512]{1,0:T(8,128)(2,1)}, bf16[24,8,104,256]{3,2,1,0:T(8,128)(2,1)}) custom-call(bf16[2400,512]{1,0:T(8,128)(2,1)} %x_ref.4, bf16[2400,512]{1,0:T(8,128)(2,1)} %x_ref.4, f32[24,1,128]{2,1,0:T(1,128)} %bitcast.4, ...), custom_call_target="tpu_custom_call" | custom-call | tf_op jit(solution)/shard_map/attn_fwd/pallas_call | solution.py:375
  33.6 0.6 copy-done.15
  34.2 0.4 copy-done.10
  34.6 41.4 %feed_forward.1 = (bf16[2400,2048]{1,0:T(8,128)(2,1)}, f32[2400,512]{1,0:T(8,128)}, bf16[2400,512]{1,0:T(8,128)(2,1)}, bf16[2304,512]{1,0:T(8,128)(2,1)}, bf16[2...) custom-call(f32[2400,512]{1,0:T(8,128)} %get-tuple-element.292.mixed_ref, bf16[2400,512]{1,0:T(8,128)(2,1)} %go_ref.1, ...), custom_call_target="tpu_custom_call" | custom-call | flops 49999998976 | bytes 40000000 | tf_op jit(solution)/shard_map/feed_forward/pallas_call | solution.py:410
  76.0 0.3 collective-permute-start.7
  76.3 5.2 %block_out.3.refs_0_ = bf16[2400,512]{1,0:T(8,128)(2,1)} custom-call(f32[2400,512]{1,0:T(8,128)} %get-tuple-element.292.mixed_ref, bf16[2400,2048]{1,0:T(8,128)(2,1)} %get-tuple-element.293.act_ref, bf16[1024,512]{1,0:T(8,128)(2,1)} %w2a_ref.4, bf16[1024,512]{1,0:T(8,128)(2,1)} %copy-done.10, f32[2,512]{1,0:T(2,128)} %ob_ref.4), custom_call_target="tpu_custom_call" | custom-call | flops 3000000000 | bytes 7000000 | tf_op jit(solution)/shard_map/block_out/pallas_call | solution.py:445
  81.6 2.3 %add.100 = bf16[2304,512]{1,0:T(8,128)(2,1)S(1)} add(bf16[2304,512]{1,0:T(8,128)(2,1)S(1)} %copy-done.11, bf16[2304,512]{1,0:T(8,128)(2,1)} %collective-permute-done.7) | non-fusion elementwise | flops 1179648 | bytes 7077888 | tf_op jit(solution)/shard_map/add | solution.py:694
  84.2 0.8 constant_dynamic-slice_fusion.7
  85.0 2.7 %collective-permute-start.8 = (bf16[768,512]{1,0:T(8,128)(2,1)S(1)}, bf16[768,512]{1,0:T(8,128)(2,1)S(1)}, u32[]{:S(2)}, u32[]{:S(2)}) collective-permute-start(bf16[768,512]{1,0:T(8,128)(2,1)S(1)} %constant_dynamic-slice_fusion.8), channel_id=1, source_target_pairs={{0,2},{1,5},{2,0},{3,7},{4,6},{5,1},{6,4},{7,3},{8,10},{9,13},{10,... | collective-permute-start | bytes 2359304 | tf_op jit(solution)/shard_map/ppermute | solution.py:665
  87.7 1.6 collective-permute-start.9
  89.2 25.0 %attn_bwd.1 = (bf16[2400,1536]{1,0:T(8,128)(2,1)}, f32[8,104,256]{2,1,0:T(8,128)}, bf16[768,512]{1,0:T(8,128)(2,1)}, bf16[768,512]{1,0:T(8,128)(2,1)}, f32[2,512]{1,0:T(2,128)}) custom-call(bf16[2400,512]{1,0:T(8,128)(2,1)} %get-tuple-element.188.n_ref, bf16[2400,512]{1,0:T(8,128)(2,1)} %get-tuple-element.189.do_ref, ...), custom_call_target="tpu_custom_call" | custom-call | flops 30000001024 | bytes 60000000 | tf_op jit(solution)/shard_map/attn_bwd/pallas_call | solution.py:463
  114.5 1.1 dynamic-slice_add_fusion.2
  115.8 1.6 collective-permute-start.10
  117.3 0.5 collective-permute-start.11
  117.9 5.4 %input_grad.3 = (bf16[2400,512]{1,0:T(8,128)(2,1)}, f32[2,512]{1,0:T(2,128)}) custom-call(bf16[2400,512]{1,0:T(8,128)(2,1)} %x_ref.4, f32[2400,512]{1,0:T(8,128)} %get-tuple-element.238.gm_ref, bf16[2400,1536]{1,0:T(8,128)(2,1)} %get-tuple-element.239.d_ref, bf16[3,512,256]{2,1,0:T(8,128)(2,1)} %wa_ref.4, bf16[3,512,256]{2,1,0:T(8,128)(2,1)} %copy-done.9, ...), custom_call_target="tpu_custom_call" | custom-call | flops 3000000000 | bytes 7000000 | tf_op jit(solution)/shard_map/input_grad/pallas_call | solution.py:489
  123.3 0.3 collective-permute-done.10
  123.8 0.6 copy-done.12
  124.7 1.6 collective-permute-start.15
  126.2 0.4 collective-permute-start.13
  126.7 0.8 collective-permute-start.14
  127.5 5.4 %input_grad.4 = (bf16[2400,512]{1,0:T(8,128)(2,1)}, f32[2,512]{1,0:T(2,128)}) custom-call(bf16[2400,512]{1,0:T(8,128)(2,1)} %x_ref.4, f32[2400,512]{1,0:T(8,128)} %get-tuple-element.238.gm_ref, bf16[2400,1536]{1,0:T(8,128)(2,1)} %get-tuple-element.239.d_ref, bf16[3,512,256]{2,1,0:T(8,128)(2,1)} %wa_ref.4, ...), custom_call_target="tpu_custom_call", output_to_operand_aliasing={{0}: (6, {})} | custom-call | flops 3000000000 | bytes 7000000 | tf_op jit(solution)/shard_map/input_grad/pallas_call | solution.py:489
  133.4 2.4 %collective-permute-start.16 = (bf16[192,512]{1,0:T(8,128)(2,1)S(1)}, bf16[192,512]{1,0:T(8,128)(2,1)S(1)}, u32[]{:S(2)}, u32[]{:S(2)}) collective-permute-start(bf16[192,512]{1,0:T(8,128)(2,1)S(1)} %get-tuple-element.234), channel_id=1, source_target_pairs={{0,16},{1,3},{2,18},{3,1},{4,20},{5,7},{6,22},{7,5},{8,24},{9,11},... | collective-permute-start | bytes 589832 | tf_op jit(solution)/shard_map/ppermute | solution.py:665
  135.8 0.6 collective-permute-start.17
  136.4 1.0 collective-permute-start.18
  137.4 5.4 %input_grad.5 = (bf16[2400,512]{1,0:T(8,128)(2,1)}, f32[2,512]{1,0:T(2,128)}) custom-call(bf16[2400,512]{1,0:T(8,128)(2,1)} %x_ref.4, f32[2400,512]{1,0:T(8,128)} %get-tuple-element.238.gm_ref, bf16[2400,1536]{1,0:T(8,128)(2,1)} %get-tuple-element.239.d_ref, bf16[3,512,256]{2,1,0:T(8,128)(2,1)} %wa_ref.4, ...), custom_call_target="tpu_custom_call", output_to_operand_aliasing={{0}: (6, {})} | custom-call | flops 3000000000 | bytes 7000000 | tf_op jit(solution)/shard_map/input_grad/pallas_call | solution.py:489
  142.8 3.4 %collective-permute-done.17 = bf16[96,512]{1,0:T(8,128)(2,1)S(1)} collective-permute-done((bf16[96,512]{1,0:T(8,128)(2,1)S(1)}, bf16[96,512]{1,0:T(8,128)(2,1)S(1)}, u32[]{:S(2)}, u32[]{:S(2)}) %collective-permute-start.17) | collective-permute-done | bytes 98336 | tf_op jit(solution)/shard_map/ppermute | solution.py:665
  146.3 0.4 collective-permute-start.19
  146.7 1.4 collective-permute-start.20
  148.2 0.7 copy-done.4
  148.8 0.8 small_sums.1
  149.8 1.5 collective-permute-start.21
  151.3 5.1 %block_out.4.refs_0_ = bf16[2400,512]{1,0:T(8,128)(2,1)} custom-call(f32[2400,512]{1,0:T(8,128)} %get-tuple-element.292.mixed_ref, bf16[2400,2048]{1,0:T(8,128)(2,1)} %get-tuple-element.293.act_ref, bf16[1024,512]{1,0:T(8,128)(2,1)} %w2a_ref.4, bf16[1024,512]{1,0:T(8,128)(2,1)} %copy-done.10, f32[2,512]{1,0:T(2,128)} %ob_ref.4, ...), custom_call_target="tpu_custom_call", output_to_operand_aliasing={{}: (5, {})} | custom-call | flops 3000000000 | bytes 7000000 | tf_op jit(solution)/shard_map/block_out/pallas_call | solution.py:445
  156.6 0.9 collective-permute-start.23
  157.6 0.9 collective-permute-start.24
  158.4 1.7 collective-permute-start.25
  160.1 5.4 %collective-permute-done.25 = bf16[128,512]{1,0:T(8,128)(2,1)S(1)} collective-permute-done((bf16[128,512]{1,0:T(8,128)(2,1)S(1)}, bf16[128,512]{1,0:T(8,128)(2,1)S(1)}, u32[]{:S(2)}, u32[]{:S(2)}) %collective-permute-start.25) | collective-permute-done | bytes 131104 | tf_op jit(solution)/shard_map/ppermute | solution.py:665
  165.8 1.1 collective-permute-start.26
  166.9 1.1 collective-permute-start.27
  168.1 0.9 collective-permute-start.28
  168.9 5.1 %block_out.5 = bf16[2400,512]{1,0:T(8,128)(2,1)} custom-call(f32[2400,512]{1,0:T(8,128)} %get-tuple-element.292.mixed_ref, bf16[2400,2048]{1,0:T(8,128)(2,1)} %get-tuple-element.293.act_ref, bf16[1024,512]{1,0:T(8,128)(2,1)} %w2a_ref.4, bf16[1024,512]{1,0:T(8,128)(2,1)} %copy-done.10, f32[2,512]{1,0:T(2,128)} %ob_ref.4, ...), custom_call_target="tpu_custom_call", output_to_operand_aliasing={{}: (5, {})} | custom-call | flops 3000000000 | bytes 7000000 | tf_op jit(solution)/shard_map/block_out/pallas_call | solution.py:445
  174.0 2.0 %collective-permute-done.28 = bf16[128,512]{1,0:T(8,128)(2,1)S(1)} collective-permute-done((bf16[128,512]{1,0:T(8,128)(2,1)S(1)}, bf16[128,512]{1,0:T(8,128)(2,1)S(1)}, u32[]{:S(2)}, u32[]{:S(2)}) %collective-permute-start.28) | collective-permute-done | bytes 131104 | tf_op jit(solution)/shard_map/ppermute | solution.py:665
  176.1 1.0 collective-permute-start.29
  177.1 1.7 collective-permute-start.30
  178.8 0.8 collective-permute-start.31
  179.7 5.1 %collective-permute-done.30 = bf16[192,512]{1,0:T(8,128)(2,1)S(1)} collective-permute-done((bf16[192,512]{1,0:T(8,128)(2,1)S(1)}, bf16[192,512]{1,0:T(8,128)(2,1)S(1)}, u32[]{:S(2)}, u32[]{:S(2)}) %collective-permute-start.30) | collective-permute-done | bytes 196640 | tf_op jit(solution)/shard_map/ppermute | solution.py:665
  185.0 1.2 collective-permute-start.32
  186.4 0.3 broadcast_select_fusion
  186.7 1.6 fusion
  188.3 1.6 fusion.2
  189.9 0.9 slice_convert_fusion
  190.8 2.4 %collective-permute-done.32 = bf16[416,512]{1,0:T(8,128)(2,1)S(1)} collective-permute-done((bf16[416,512]{1,0:T(8,128)(2,1)S(1)}, bf16[416,512]{1,0:T(8,128)(2,1)S(1)}, u32[]{:S(2)}, u32[]{:S(2)}) %collective-permute-start.32) | collective-permute-done | bytes 426016 | tf_op jit(solution)/shard_map/ppermute | solution.py:665
  193.4 1.3 finish.1
  194.7 0.7 copy.32
  (104 shorter events, 3.7 us)
Async XLA Ops:
  0.6 2.9 %collective-permute-start = (bf16[3,512,256]{2,1,0:T(8,128)(2,1)}, bf16[3,512,256]{2,1,0:T(8,128)(2,1)S(1)}, u32[]{:S(2)}, u32[]{:S(2)}) collective-permute-start(bf16[3,512,256]{2,1,0:T(8,128)(2,1)} %wa_ref.4), channel_id=1, source_target_pairs={{0,1},{1,0},{2,3},{3,2},{4,5},{5,4},{6,7},{7,6},{8,9},{9,8},{10,11... | collective-permute-start | bytes 2359304 | tf_op jit(solution)/shard_map/ppermute | solution.py:779
  2.0 1.5 collective-permute-start.1
  3.5 5.3 %copy-start.9 = (bf16[3,512,256]{2,1,0:T(8,128)(2,1)}, bf16[3,512,256]{2,1,0:T(8,128)(2,1)S(1)}, u32[]{:S(2)}) copy-start(bf16[3,512,256]{2,1,0:T(8,128)(2,1)S(1)} %collective-permute-done.wb_ref) | copy-start | bytes 2359300
  3.5 30.1 %collective-permute-start.4 = (bf16[512,1024]{1,0:T(8,128)(2,1)}, bf16[512,1024]{1,0:T(8,128)(2,1)}, u32[]{:S(2)}, u32[]{:S(2)}) collective-permute-start(bf16[512,1024]{1,0:T(8,128)(2,1)} %w1a_ref.1), channel_id=1, source_target_pairs={{0,1},{1,0},{2,3},{3,2},{4,5},{5,4},{6,7},{7,6},{8,9},{9,8},{10,11... | collective-permute-start | bytes 3145736 | tf_op jit(solution)/shard_map/ppermute | solution.py:779
  3.7 29.9 %collective-permute-start.5 = (bf16[1024,512]{1,0:T(8,128)(2,1)}, bf16[1024,512]{1,0:T(8,128)(2,1)S(1)}, u32[]{:S(2)}, u32[]{:S(2)}) collective-permute-start(bf16[1024,512]{1,0:T(8,128)(2,1)} %w2a_ref.4), channel_id=1, source_target_pairs={{0,1},{1,0},{2,3},{3,2},{4,5},{5,4},{6,7},{7,6},{8,9},{9,8},{10,11... | collective-permute-start | bytes 3145736 | tf_op jit(solution)/shard_map/ppermute | solution.py:779
  4.0 5.7 %collective-permute-start.2 = (f32[2,256]{1,0:T(2,128)}, f32[2,256]{1,0:T(2,128)S(1)}, u32[]{:S(2)}, u32[]{:S(2)}) collective-permute-start(f32[2,256]{1,0:T(2,128)} %qva_ref.1), channel_id=1, source_target_pairs={{0,1},{1,0},{2,3},{3,2},{4,5},{5,4},{6,7},{7,6},{8,9},{9,8},{10,11... | collective-permute-start | bytes 6152 | tf_op jit(solution)/shard_map/ppermute | solution.py:779
  4.2 5.5 %collective-permute-start.3 = (bf16[256,512]{1,0:T(8,128)(2,1)}, bf16[256,512]{1,0:T(8,128)(2,1)S(1)}, u32[]{:S(2)}, u32[]{:S(2)}) collective-permute-start(bf16[256,512]{1,0:T(8,128)(2,1)} %pa_ref.3), channel_id=1, source_target_pairs={{0,1},{1,0},{2,3},{3,2},{4,5},{5,4},{6,7},{7,6},{8,9},{9,8},{10,11... | collective-permute-start | bytes 786440 | tf_op jit(solution)/shard_map/ppermute | solution.py:779
  6.0 27.6 %collective-permute-start.6 = (f32[1024]{0:T(1024)}, f32[1024]{0:T(1024)S(1)}, u32[]{:S(2)}, u32[]{:S(2)}) collective-permute-start(f32[1024]{0:T(1024)} %param.21), channel_id=1, source_target_pairs={{0,1},{1,0},{2,3},{3,2},{4,5},{5,4},{6,7},{7,6},{8,9},{9,8},{10,11... | collective-permute-start | bytes 12296 | tf_op jit(solution)/shard_map/ppermute | solution.py:779
  6.2 0.8 copy-start.1
  8.8 0.9 copy-start
  9.8 0.6 copy-start.14
  9.8 0.7 copy-start.13
  33.6 0.6 copy-start.15
  33.6 1.0 copy-start.10
  76.0 5.6 %collective-permute-start.7 = (bf16[2304,512]{1,0:T(8,128)(2,1)}, bf16[2304,512]{1,0:T(8,128)(2,1)}, u32[]{:S(2)}, u32[]{:S(2)}) collective-permute-start(bf16[2304,512]{1,0:T(8,128)(2,1)} %get-tuple-element.175), channel_id=1, source_target_pairs={{0,1},{1,0},{2,3},{3,2},{4,5},{5,4},{6,7},{7,6},{8,9},{9,8},{10,11... | collective-permute-start | bytes 7077896 | tf_op jit(solution)/shard_map/ppermute | solution.py:688
  76.3 5.2 %copy-start.11 = (bf16[2304,512]{1,0:T(8,128)(2,1)S(1)}, bf16[2304,512]{1,0:T(8,128)(2,1)}, u32[]{:S(2)}) copy-start(bf16[2304,512]{1,0:T(8,128)(2,1)} %get-tuple-element.172) | copy-start | bytes 7077892
  85.0 29.3 %collective-permute-start.8 = (bf16[768,512]{1,0:T(8,128)(2,1)S(1)}, bf16[768,512]{1,0:T(8,128)(2,1)S(1)}, u32[]{:S(2)}, u32[]{:S(2)}) collective-permute-start(bf16[768,512]{1,0:T(8,128)(2,1)S(1)} %constant_dynamic-slice_fusion.8), channel_id=1, source_target_pairs={{0,2},{1,5},{2,0},{3,7},{4,6},{5,1},{6,4},{7,3},{8,10},{9,13},{10,... | collective-permute-start | bytes 2359304 | tf_op jit(solution)/shard_map/ppermute | solution.py:665
  87.7 26.6 %collective-permute-start.9 = (bf16[384,512]{1,0:T(8,128)(2,1)}, bf16[384,512]{1,0:T(8,128)(2,1)}, u32[]{:S(2)}, u32[]{:S(2)}) collective-permute-start(bf16[384,512]{1,0:T(8,128)(2,1)} %constant_dynamic-slice_fusion.7), channel_id=1, source_target_pairs={{0,8},{1,9},{2,10},{3,11},{4,12},{5,13},{6,14},{7,15},{8,0},{9,1},... | collective-permute-start | bytes 1179656 | tf_op jit(solution)/shard_map/ppermute | solution.py:665
  115.7 7.9 %collective-permute-start.12 = (bf16[768,512]{1,0:T(8,128)(2,1)}, bf16[768,512]{1,0:T(8,128)(2,1)S(1)}, u32[]{:S(2)}, u32[]{:S(2)}) collective-permute-start(bf16[768,512]{1,0:T(8,128)(2,1)} %get-tuple-element.204), channel_id=1, source_target_pairs={{0,1},{1,0},{2,3},{3,2},{4,5},{5,4},{6,7},{7,6},{8,9},{9,8},{10,11... | collective-permute-start | bytes 2359304 | tf_op jit(solution)/shard_map/ppermute | solution.py:688
  115.8 7.8 %collective-permute-start.10 = (bf16[384,512]{1,0:T(8,128)(2,1)S(1)}, bf16[384,512]{1,0:T(8,128)(2,1)S(1)}, u32[]{:S(2)}, u32[]{:S(2)}) collective-permute-start(bf16[384,512]{1,0:T(8,128)(2,1)S(1)} %constant_dynamic-slice_fusion.6), channel_id=1, source_target_pairs={{0,4},{1,9},{2,6},{3,11},{4,0},{5,13},{6,2},{7,15},{8,12},{9,1},{1... | collective-permute-start | bytes 1179656 | tf_op jit(solution)/shard_map/ppermute | solution.py:665
  117.3 5.9 %collective-permute-start.11 = (bf16[192,512]{1,0:T(8,128)(2,1)S(1)}, bf16[192,512]{1,0:T(8,128)(2,1)S(1)}, u32[]{:S(2)}, u32[]{:S(2)}) collective-permute-start(bf16[192,512]{1,0:T(8,128)(2,1)S(1)} %constant_dynamic-slice_fusion.5), channel_id=1, source_target_pairs={{0,2},{1,3},{2,0},{3,1},{4,6},{5,7},{6,4},{7,5},{8,10},{9,11},{10,... | collective-permute-start | bytes 589832 | tf_op jit(solution)/shard_map/ppermute | solution.py:665
  123.3 1.1 copy-start.12
  124.7 8.5 %collective-permute-start.15 = (bf16[384,512]{1,0:T(8,128)(2,1)S(1)}, bf16[384,512]{1,0:T(8,128)(2,1)S(1)}, u32[]{:S(2)}, u32[]{:S(2)}) collective-permute-start(bf16[384,512]{1,0:T(8,128)(2,1)S(1)} %constant_dynamic-slice_fusion.2), channel_id=1, source_target_pairs={{0,2},{1,5},{2,0},{3,7},{4,6},{5,1},{6,4},{7,3},{8,10},{9,13},{10,... | collective-permute-start | bytes 1179656 | tf_op jit(solution)/shard_map/ppermute | solution.py:665
  126.2 6.9 %collective-permute-start.13 = (bf16[192,512]{1,0:T(8,128)(2,1)S(1)}, bf16[192,512]{1,0:T(8,128)(2,1)S(1)}, u32[]{:S(2)}, u32[]{:S(2)}) collective-permute-start(bf16[192,512]{1,0:T(8,128)(2,1)S(1)} %constant_dynamic-slice_fusion.4), channel_id=1, source_target_pairs={{0,8},{1,17},{2,10},{3,19},{4,12},{5,21},{6,14},{7,23},{8,0},{9,25... | collective-permute-start | bytes 589832 | tf_op jit(solution)/shard_map/ppermute | solution.py:665
  126.7 6.2 %collective-permute-start.14 = (bf16[96,512]{1,0:T(8,128)(2,1)S(1)}, bf16[96,512]{1,0:T(8,128)(2,1)S(1)}, u32[]{:S(2)}, u32[]{:S(2)}) collective-permute-start(bf16[96,512]{1,0:T(8,128)(2,1)S(1)} %constant_dynamic-slice_fusion.3), channel_id=1, source_target_pairs={{0,4},{1,5},{2,6},{3,7},{4,0},{5,1},{6,2},{7,3},{8,12},{9,13},{10,... | collective-permute-start | bytes 294920 | tf_op jit(solution)/shard_map/ppermute | solution.py:665
  133.3 14.8 %copy-start.2 = (f32[2,512]{1,0:T(2,128)S(1)}, f32[2,512]{1,0:T(2,128)}, u32[]{:S(2)}) copy-start(f32[2,512]{1,0:T(2,128)} %get-tuple-element.262.gs1a_ref) | copy-start | bytes 12292
  133.4 14.8 %copy-start.3 = (f32[2,512]{1,0:T(2,128)S(1)}, f32[2,512]{1,0:T(2,128)}, u32[]{:S(2)}) copy-start(f32[2,512]{1,0:T(2,128)} %get-tuple-element.263.gs1b_ref) | copy-start | bytes 12292
  133.4 14.8 %copy-start.5 = (f32[8,104,256]{2,1,0:T(8,128)S(1)}, f32[8,104,256]{2,1,0:T(8,128)}, u32[]{:S(2)}) copy-start(f32[8,104,256]{2,1,0:T(8,128)} %get-tuple-element.260.t_ref) | copy-start | bytes 2555908
  133.4 14.7 %copy-start.6 = (f32[1,2048]{1,0:T(1,128)S(1)}, f32[1,2048]{1,0:T(1,128)}, u32[]{:S(2)}) copy-start(f32[1,2048]{1,0:T(1,128)} %get-tuple-element.265.gb1_ref) | copy-start | bytes 24580
  133.4 14.7 %copy-start.7 = (f32[4,512]{1,0:T(4,128)S(1)}, f32[4,512]{1,0:T(4,128)}, u32[]{:S(2)}) copy-start(f32[4,512]{1,0:T(4,128)} %get-tuple-element.261.gs2_ref) | copy-start | bytes 24580
  133.4 14.7 %copy-start.8 = (f32[2,512]{1,0:T(2,128)S(1)}, f32[2,512]{1,0:T(2,128)}, u32[]{:S(2)}) copy-start(f32[2,512]{1,0:T(2,128)} %get-tuple-element.266.gqv_ref) | copy-start | bytes 12292
  133.4 12.8 %collective-permute-start.16 = (bf16[192,512]{1,0:T(8,128)(2,1)S(1)}, bf16[192,512]{1,0:T(8,128)(2,1)S(1)}, u32[]{:S(2)}, u32[]{:S(2)}) collective-permute-start(bf16[192,512]{1,0:T(8,128)(2,1)S(1)} %get-tuple-element.234), channel_id=1, source_target_pairs={{0,16},{1,3},{2,18},{3,1},{4,20},{5,7},{6,22},{7,5},{8,24},{9,11},... | collective-permute-start | bytes 589832 | tf_op jit(solution)/shard_map/ppermute | solution.py:665
  135.8 10.4 %collective-permute-start.17 = (bf16[96,512]{1,0:T(8,128)(2,1)S(1)}, bf16[96,512]{1,0:T(8,128)(2,1)S(1)}, u32[]{:S(2)}, u32[]{:S(2)}) collective-permute-start(bf16[96,512]{1,0:T(8,128)(2,1)S(1)} %dynamic-slice_add_fusion.8), channel_id=1, source_target_pairs={{0,16},{1,17},{2,18},{3,19},{4,20},{5,21},{6,22},{7,23},{8,24},{9,... | collective-permute-start | bytes 294920 | tf_op jit(solution)/shard_map/ppermute | solution.py:665
  136.4 9.8 %collective-permute-start.18 = (bf16[192,512]{1,0:T(8,128)(2,1)S(1)}, bf16[192,512]{1,0:T(8,128)(2,1)S(1)}, u32[]{:S(2)}, u32[]{:S(2)}) collective-permute-start(bf16[192,512]{1,0:T(8,128)(2,1)S(1)} %get-tuple-element.236), channel_id=1, source_target_pairs={{0,4},{1,9},{2,6},{3,11},{4,0},{5,13},{6,2},{7,15},{8,12},{9,1},{1... | collective-permute-start | bytes 589832 | tf_op jit(solution)/shard_map/ppermute | solution.py:665
  146.3 10.2 %collective-permute-start.19 = (bf16[192,512]{1,0:T(8,128)(2,1)S(1)}, bf16[192,512]{1,0:T(8,128)(2,1)S(1)}, u32[]{:S(2)}, u32[]{:S(2)}) collective-permute-start(bf16[192,512]{1,0:T(8,128)(2,1)S(1)} %add.117), channel_id=1, source_target_pairs={{0,8},{1,17},{2,10},{3,19},{4,12},{5,21},{6,14},{7,23},{8,0},{9,25... | collective-permute-start | bytes 589832 | tf_op jit(solution)/shard_map/ppermute | solution.py:665
  146.7 9.8 %collective-permute-start.20 = (bf16[96,512]{1,0:T(8,128)(2,1)S(1)}, bf16[96,512]{1,0:T(8,128)(2,1)S(1)}, u32[]{:S(2)}, u32[]{:S(2)}) collective-permute-start(bf16[96,512]{1,0:T(8,128)(2,1)S(1)} %add.118), channel_id=1, source_target_pairs={{0,4},{1,5},{2,6},{3,7},{4,0},{5,1},{6,2},{7,3},{8,12},{9,13},{10,... | collective-permute-start | bytes 294920 | tf_op jit(solution)/shard_map/ppermute | solution.py:665
  148.1 0.7 copy-start.4
  149.8 6.6 %collective-permute-start.21 = (bf16[96,512]{1,0:T(8,128)(2,1)S(1)}, bf16[96,512]{1,0:T(8,128)(2,1)S(1)}, u32[]{:S(2)}, u32[]{:S(2)}) collective-permute-start(bf16[96,512]{1,0:T(8,128)(2,1)S(1)} %constant_dynamic-slice_fusion), channel_id=1, source_target_pairs={{0,8},{1,17},{2,10},{3,19},{4,12},{5,21},{6,14},{7,23},{8,0},{9,25... | collective-permute-start | bytes 294920 | tf_op jit(solution)/shard_map/ppermute | solution.py:665
  151.3 5.1 %collective-permute-start.22 = (bf16[32,512]{1,0:T(8,128)(2,1)S(1)}, bf16[32,512]{1,0:T(8,128)(2,1)S(1)}, u32[]{:S(2)}, u32[]{:S(2)}) collective-permute-start(bf16[32,512]{1,0:T(8,128)(2,1)S(1)} %get-tuple-element.270), channel_id=1, source_target_pairs={{0,1},{1,0},{2,3},{3,2},{4,5},{5,4},{6,7},{7,6},{8,9},{9,8},{10,11... | collective-permute-start | bytes 98312 | tf_op jit(solution)/shard_map/ppermute | solution.py:688
  156.6 8.9 %collective-permute-start.23 = (bf16[384,512]{1,0:T(8,128)(2,1)S(1)}, bf16[384,512]{1,0:T(8,128)(2,1)S(1)}, u32[]{:S(2)}, u32[]{:S(2)}) collective-permute-start(bf16[384,512]{1,0:T(8,128)(2,1)S(1)} %pad_maximum_fusion.5), channel_id=1, source_target_pairs={{0,4},{1,9},{2,6},{3,11},{4,0},{5,13},{6,2},{7,15},{8,12},{9,1},{1... | collective-permute-start | bytes 1179656 | tf_op jit(solution)/shard_map/ppermute | solution.py:665
  157.6 7.9 %collective-permute-start.24 = (bf16[192,512]{1,0:T(8,128)(2,1)S(1)}, bf16[192,512]{1,0:T(8,128)(2,1)S(1)}, u32[]{:S(2)}, u32[]{:S(2)}) collective-permute-start(bf16[192,512]{1,0:T(8,128)(2,1)S(1)} %pad_maximum_fusion.9), channel_id=1, source_target_pairs={{0,2},{1,3},{2,0},{3,1},{4,6},{5,7},{6,4},{7,5},{8,10},{9,11},{10,... | collective-permute-start | bytes 589832 | tf_op jit(solution)/shard_map/ppermute | solution.py:665
  158.4 7.1 %collective-permute-start.25 = (bf16[128,512]{1,0:T(8,128)(2,1)S(1)}, bf16[128,512]{1,0:T(8,128)(2,1)S(1)}, u32[]{:S(2)}, u32[]{:S(2)}) collective-permute-start(bf16[128,512]{1,0:T(8,128)(2,1)S(1)} %pad_maximum_fusion.11), channel_id=1, source_target_pairs={{0,16},{1,3},{2,18},{3,1},{4,20},{5,7},{6,22},{7,5},{8,24},{9,11},... | collective-permute-start | bytes 393224 | tf_op jit(solution)/shard_map/ppermute | solution.py:665
  165.8 10.3 %collective-permute-start.26 = (bf16[384,512]{1,0:T(8,128)(2,1)S(1)}, bf16[384,512]{1,0:T(8,128)(2,1)S(1)}, u32[]{:S(2)}, u32[]{:S(2)}) collective-permute-start(bf16[384,512]{1,0:T(8,128)(2,1)S(1)} %get-tuple-element.289), channel_id=1, source_target_pairs={{0,2},{1,5},{2,0},{3,7},{4,6},{5,1},{6,4},{7,3},{8,10},{9,13},{10,... | collective-permute-start | bytes 1179656 | tf_op jit(solution)/shard_map/ppermute | solution.py:665
  166.9 9.1 %collective-permute-start.27 = (bf16[192,512]{1,0:T(8,128)(2,1)S(1)}, bf16[192,512]{1,0:T(8,128)(2,1)S(1)}, u32[]{:S(2)}, u32[]{:S(2)}) collective-permute-start(bf16[192,512]{1,0:T(8,128)(2,1)S(1)} %get-tuple-element.290), channel_id=1, source_target_pairs={{0,8},{1,9},{2,10},{3,11},{4,12},{5,13},{6,14},{7,15},{8,0},{9,1},... | collective-permute-start | bytes 589832 | tf_op jit(solution)/shard_map/ppermute | solution.py:665
  168.1 8.0 %collective-permute-start.28 = (bf16[128,512]{1,0:T(8,128)(2,1)S(1)}, bf16[128,512]{1,0:T(8,128)(2,1)S(1)}, u32[]{:S(2)}, u32[]{:S(2)}) collective-permute-start(bf16[128,512]{1,0:T(8,128)(2,1)S(1)} %pad_maximum_fusion.12), channel_id=1, source_target_pairs={{0,8},{1,17},{2,10},{3,19},{4,12},{5,21},{6,14},{7,23},{8,0},{9,25... | collective-permute-start | bytes 393224 | tf_op jit(solution)/shard_map/ppermute | solution.py:665
  176.1 8.8 %collective-permute-start.29 = (bf16[384,512]{1,0:T(8,128)(2,1)S(1)}, bf16[384,512]{1,0:T(8,128)(2,1)S(1)}, u32[]{:S(2)}, u32[]{:S(2)}) collective-permute-start(bf16[384,512]{1,0:T(8,128)(2,1)S(1)} %get-tuple-element.301), channel_id=1, source_target_pairs={{0,2},{1,5},{2,0},{3,7},{4,6},{5,1},{6,4},{7,3},{8,10},{9,13},{10,... | collective-permute-start | bytes 1179656 | tf_op jit(solution)/shard_map/ppermute | solution.py:665
  177.1 7.8 %collective-permute-start.30 = (bf16[192,512]{1,0:T(8,128)(2,1)S(1)}, bf16[192,512]{1,0:T(8,128)(2,1)S(1)}, u32[]{:S(2)}, u32[]{:S(2)}) collective-permute-start(bf16[192,512]{1,0:T(8,128)(2,1)S(1)} %get-tuple-element.302), channel_id=1, source_target_pairs={{0,8},{1,9},{2,10},{3,11},{4,12},{5,13},{6,14},{7,15},{8,0},{9,1},... | collective-permute-start | bytes 589832 | tf_op jit(solution)/shard_map/ppermute | solution.py:665
  178.8 6.0 %collective-permute-start.31 = (bf16[224,512]{1,0:T(8,128)(2,1)S(1)}, bf16[224,512]{1,0:T(8,128)(2,1)S(1)}, u32[]{:S(2)}, u32[]{:S(2)}) collective-permute-start(bf16[224,512]{1,0:T(8,128)(2,1)S(1)} %pad_maximum_fusion.8), channel_id=1, source_target_pairs={{0,4},{1,9},{2,6},{3,11},{4,0},{5,13},{6,2},{7,15},{8,12},{9,1},{1... | collective-permute-start | bytes 688136 | tf_op jit(solution)/shard_map/ppermute | solution.py:665
  185.0 8.2 %collective-permute-start.32 = (bf16[416,512]{1,0:T(8,128)(2,1)S(1)}, bf16[416,512]{1,0:T(8,128)(2,1)S(1)}, u32[]{:S(2)}, u32[]{:S(2)}) collective-permute-start(bf16[416,512]{1,0:T(8,128)(2,1)S(1)} %pad_maximum_fusion.4), channel_id=1, source_target_pairs={{0,2},{1,5},{2,0},{3,7},{4,6},{5,1},{6,4},{7,3},{8,10},{9,13},{10,... | collective-permute-start | bytes 1277960 | tf_op jit(solution)/shard_map/ppermute | solution.py:665
where the time goes:
time: 196 us; the launch traced here: 195 us
  Pallas kernels  125 us (64%)
  starting transfers between devices  30.2 us (15%)
  waiting for transfers between devices  20.4 us (10%)
  other arithmetic  9.63 us (5%)
  local copies, waits for them, and re-layouts  8.89 us (5%)
    pallas_call x1, Pallas kernels, ffn(): pl.pallas_call(ffn_body, name='feed_forward', grid=(rows // DENSE,), in_s...  41.4 us
    ppermute x23, starting transfers between devices, move(): return lax.ppermute(send, ('dp', 'tp'), perm)  27.9 us
    pallas_call x1, Pallas kernels, attn_bwd(): pl.pallas_call(attn_bwd_body, name='attn_bwd', grid=(rows // ROWS + 1,),...  25 us
    pallas_call x1, Pallas kernels, attn_fwd(): pl.pallas_call(attn_fwd_body, name='attn_fwd', grid=(rows // ROWS + 1,),...  23.1 us
    ppermute x23, waiting for transfers between devices, move(): return lax.ppermute(send, ('dp', 'tp'), perm)  19 us
    pallas_call x3, Pallas kernels, input_grad(): pl.pallas_call(input_grad_body, name='input_grad', grid=(THIRD,), in_spec...  16.2 us
    pallas_call x3, Pallas kernels, out_rows(): pl.pallas_call(out_body, name='block_out', grid=(THIRD,), in_specs=[spec(...  15.4 us
    unnamed x36, local copies, waits for them, and re-layouts  6.23 us
  transfers between devices with their start and end apart: 33, of which 8 were waited for; matrix products, arithmetic and copies ran while one was open for 4% of the time, Pallas kernels for 42%

commit v1 on v0

--- a/solution.py
+++ b/solution.py
@@ -59,9 +59,10 @@
 
 
 def attn_fwd_body(
-    x_ref, xb_ref, page_ref, wa_ref, wb_ref, qva_ref, qvb_ref, bias_ref, pa_ref, pb_ref, ob_ref, gain_ref, shift_ref,
-    n_ref, qkv_ref, mixed_ref, att_ref, p_ref,
-    scr, cur, nxt, att_scr, att_rows,
+    x_ref, xb_ref, page_ref, rel_ref, ta_ref, tb_ref, wa_ref, wb_ref, qva_ref, qvb_ref, pa_ref, pb_ref, ob_ref, gain_ref,
+    shift_ref,
+    n_ref, qkv_ref, mixed_ref, att_ref, p_ref, idx_ref,
+    scr, cur, nxt, att_scr, att_rows, bias_ref, turn,
 ):
     scale = (HEAD ** -0.5) * LOG2E
 
@@ -134,6 +135,7 @@
         for i in range(3):
             project(n, i)
         cur[...] = nxt[...]
+        expand_table(rel_ref, ta_ref, tb_ref, bias_ref, idx_ref, turn)
 
     @pl.when((step > 0) & (step < end))
     def _():
@@ -366,7 +368,7 @@
 PARAMS = pltpu.CompilerParams(vmem_limit_bytes=60 << 20, dimension_semantics=("arbitrary",))
 
 
-def attn_fwd(x, pages, wa, wb, qva, qvb, bias, pa, pb, ob, gain, shift):
+def attn_fwd(x, pages, rel_index, ta, tb, wa, wb, qva, qvb, pa, pb, ob, gain, shift):
     rows = x.shape[0]
     windows = rows // WIN
     last = rows // ROWS - 1
@@ -377,10 +379,10 @@
         name="attn_fwd",
         grid=(rows // ROWS + 1,),
         in_specs=[front(ROWS, 512), back(ROWS, 512), back(GROUP, 1, LANES)]
-        + [whole(a.shape) for a in (wa, wb, qva, qvb, bias, pa, pb, ob, gain, shift)],
+        + [whole(a.shape) for a in (rel_index, ta, tb, wa, wb, qva, qvb, pa, pb, ob, gain, shift)],
         out_specs=[
             front(ROWS, 512), front(GROUP, LANES, 1536), back(ROWS, 512), back(ROWS, 512),
-            back(GROUP, 8, KEYS, SLAB),
+            back(GROUP, 8, KEYS, SLAB), whole((16, SLAB)),
         ],
         out_shape=[
             shaped((rows, 512), BF),
@@ -388,6 +390,7 @@
             shaped((rows, 512), F32),
             shaped((rows, 512), BF),
             shaped((windows, 8, KEYS, SLAB), BF),
+            shaped((16, SLAB), F32),
         ],
         scratch_shapes=[
             pltpu.VMEM((ROWS + 32, 1536), F32),
@@ -395,9 +398,11 @@
             pltpu.VMEM((GROUP, LANES, 1536), BF),
             pltpu.VMEM((GROUP, LANES, 512), F32),
             pltpu.VMEM((ROWS, 512), F32),
+            pltpu.VMEM((8, KEYS, SLAB), F32),
+            pltpu.VMEM((LANES, LANES), F32),
         ],
         compiler_params=PARAMS,
-    )(x, x, pages, wa, wb, qva, qvb, bias, pa, pb, ob, gain, shift)
+    )(x, x, pages, rel_index, ta, tb, wa, wb, qva, qvb, pa, pb, ob, gain, shift)
 
 
 def cost(flops, moved):
@@ -505,7 +510,7 @@
     return jnp.where(slot == index_row, 1.0, 0.0).astype(BF)
 
 
-def bias_body(rel_ref, ta_ref, tb_ref, bias_ref, idx_ref, scr):
+def expand_table(rel_ref, ta_ref, tb_ref, bias_ref, idx_ref, scr):
     scr[...] = jnp.zeros_like(scr)
     scr[:WIN, :WIN] = rel_ref[...].astype(F32)
     scr[...] = scr[...].T
@@ -521,17 +526,16 @@
         idx += place(WS * (WS - 1 - d), WS, WS * d)
     idx = jnp.where(lane < WIN + WIN - WS, idx, -1.0)
     idx_ref[...] = idx
-    table = jnp.concatenate([ta_ref[...], tb_ref[...]], axis=1) * LOG2E
+    table = jnp.concatenate([ta_ref[...], tb_ref[...]], axis=0) * LOG2E
     high = table.astype(BF)
     rest = table - high.astype(F32)
     mid = rest.astype(BF)
-    table = jnp.concatenate([high, mid, (rest - mid.astype(F32)).astype(BF)], axis=1)
+    table = jnp.concatenate([high, mid, (rest - mid.astype(F32)).astype(BF)], axis=0)
     row = lax.broadcasted_iota(jnp.int32, (16, 48), 0)
     col = lax.broadcasted_iota(jnp.int32, (16, 48), 1)
     pick = jnp.where(col % 16 == 2 * (row % 8) + row // 8, 1.0, 0.0).astype(BF)
     for jx in range(WS):
-        parts = dot_tn(table, offset_onehot(idx[jx : jx + 1]))
-        values = dot(pick, parts.astype(BF))
+        values = dot(pick, dot(table, offset_onehot(idx[jx : jx + 1])).astype(BF))
         for jy in range(WS):
             shift = WS * (WS - 1 - jy)
             moved = pltpu.roll(values, (SLAB - shift) % SLAB, 1) if shift else values
@@ -539,17 +543,6 @@
             bias_ref[:, WS * jy + jx, LANES:] = moved[8:, :LANES]
     for key in range(WIN, KEYS):
         bias_ref[:, key, :] = jnp.zeros((8, SLAB), F32)
-
-
-def expand_table(rel_index, ta, tb):
-    return pl.pallas_call(
-        bias_body,
-        name="bias",
-        out_shape=[shaped((8, KEYS, SLAB), F32), shaped((16, SLAB), F32)],
-        scratch_shapes=[pltpu.VMEM((LANES, LANES), F32)],
-        compiler_params=pltpu.CompilerParams(vmem_limit_bytes=16 << 20),
-        cost_estimate=cost(3e9, 1e6),
-    )(rel_index, ta, tb)
 
 
 def small_body(idx_ref, t_ref, gs2_ref, gs1a_ref, gs1b_ref, gs1c_ref, gb1_ref, gqv_ref, own_ref, other_ref, scr):
@@ -606,11 +599,10 @@
     gb1_ref[:, 512:] = late[7:8]
     gqv_ref[0:1] = late[8:9, :SLAB]
     gqv_ref[1:2] = late[8:9, SLAB:]
-    scr[...] = jnp.zeros_like(scr)
     for h in range(8):
         r = 16 + 4 * (h % 2) + h // 2
         scr[h : h + 1, :] = late[r : r + 1, :]
-    gt_ref[...] = scr[...].T[:TAB, :8]
+    gt_ref[...] = scr[:, :TAB]
 
 
 def finish(q, late):
@@ -619,9 +611,9 @@
         name="finish",
         out_shape=[
             shaped((3, 512, SLAB), F32), shaped((2, SLAB), F32), shaped((2, 512), F32), shaped((2, 512), F32),
-            shaped((2, 512), F32), shaped((1, 1024), F32), shaped((TAB, 8), F32),
+            shaped((2, 512), F32), shaped((1, 1024), F32), shaped((8, TAB), F32),
         ],
-        scratch_shapes=[pltpu.VMEM((LANES, 512), F32)],
+        scratch_shapes=[pltpu.VMEM((8, 512), F32)],
         compiler_params=pltpu.CompilerParams(vmem_limit_bytes=16 << 20),
         cost_estimate=cost(1e9, 4e6),
     )(q, late)
@@ -748,16 +740,15 @@
             self.chain.end(jnp.concatenate(self.gots, axis=0))
 
 
-def forward(x, pages, bias, wa, wb, qva, qvb, pa, pb, w1a, w1b, b1a, b1b, w2a, w2b, ob, gain, shift, go):
-    n, qkv, mixed, att, probs = attn_fwd(x, pages, wa, wb, qva, qvb, bias, pa, pb, ob, gain, shift)
+def forward(x, pages, rel_index, ta, tb, wa, wb, qva, qvb, pa, pb, w1a, w1b, b1a, b1b, w2a, w2b, ob, gain, shift, go):
+    n, qkv, mixed, att, probs, idx = attn_fwd(x, pages, rel_index, ta, tb, wa, wb, qva, qvb, pa, pb, ob, gain, shift)
     act, gm, do, gfa, gfb, gb1, gs2 = ffn(mixed, go, att, w1a, w1b, w2a, w2b, b1a, b1b, pa, pb, gain, shift)
-    return mixed, n, qkv, probs, act, gm, do, (gfa, gfb), gb1, gs2
+    return idx, mixed, n, qkv, probs, act, gm, do, (gfa, gfb), gb1, gs2
 
 
 def local_block(x, pages, rel_index, wa, wb, qva, qvb, pa, pb, w1a, w1b, b1a, b1b, w2a, w2b, ob, gain, shift, ta, tb, go):
-    bias, idx = expand_table(rel_index, ta, tb)
-    mixed, n, qkv, probs, act, gm, do, gf, gb1, gs2 = forward(
-        x, pages, bias, wa, wb, qva, qvb, pa, pb, w1a, w1b, b1a, b1b, w2a, w2b, ob, gain, shift, go
+    idx, mixed, n, qkv, probs, act, gm, do, gf, gb1, gs2 = forward(
+        x, pages, rel_index, ta.T, tb.T, wa, wb, qva, qvb, pa, pb, w1a, w1b, b1a, b1b, w2a, w2b, ob, gain, shift, go
     )
     d, t, gqa, gqb, gqv = attn_bwd(n, do, qkv, probs)
     gin, out, sums = (), (), []
@@ -779,12 +770,14 @@
     swap = lambda v: lax.ppermute(v, "tp", SWAP)
     pages = lax.dynamic_slice_in_dim(page_of.reshape(2 * windows, WIN), me * windows, windows, 0)
     pages = jnp.pad(pages.astype(F32), ((0, 0), (0, LANES - WIN)), constant_values=-1.0)[:, None, :]
-    w_qkv_b, qv_bias_b, w_proj_b, table_b = (swap(v) for v in (w_qkv, qv_bias, w_proj, bias_table))
-    later, w_qkv_b, table_b = tie(((w_fc1, fc1_bias, w_fc2), w_qkv_b, table_b))
+    table = bias_table.T
+    w_qkv_b, qv_bias_b, w_proj_b, table_b = (swap(v) for v in (w_qkv, qv_bias, w_proj, table))
+    later, w_qkv_b, qv_bias_b, w_proj_b, table_b, pages = tie(
+        ((w_fc1, fc1_bias, w_fc2), w_qkv_b, qv_bias_b, w_proj_b, table_b, pages)
+    )
     w_fc1_b, fc1_bias_b, w_fc2_b = (swap(v) for v in later)
-    bias, idx = expand_table(rel_index, bias_table, table_b)
-    mixed, n, qkv, probs, act, gm, do, gf, gb1, gs2 = forward(
-        inputs, pages, bias, w_qkv, w_qkv_b, qv_bias, qv_bias_b, w_proj, w_proj_b, w_fc1, w_fc1_b,
+    idx, mixed, n, qkv, probs, act, gm, do, gf, gb1, gs2 = forward(
+        inputs, pages, rel_index, table, table_b, w_qkv, w_qkv_b, qv_bias, qv_bias_b, w_proj, w_proj_b, w_fc1, w_fc1_b,
         fc1_bias[None], fc1_bias_b[None], w_fc2, w_fc2_b, out_biases, norm_gains, norm_biases, out_grad,
     )
     bits = dp_bits(dp_size)
@@ -825,7 +818,7 @@
     while q.steps:
         advance([q])
     g_qkv, g_qv, g_ob, g_gains, g_shifts, g_fc1_bias, g_table = finish(q.own, q.late)
-    return out, gin, g_qkv, g_qv, g_proj, g_fc1, g_fc1_bias.reshape(-1), g_fc2, g_ob, g_gains, g_shifts, g_table
+    return out, gin, g_qkv, g_qv, g_proj, g_fc1, g_fc1_bias.reshape(-1), g_fc2, g_ob, g_gains, g_shifts, g_table.T
 
 
 def solution(mesh):

time: 196 us -> 191 us (0.974)
  local copies, waits for them, and re-layouts: 8.89 us -> 5.31 us
    unnamed x36, local copies, waits for them, and re-layouts: 6.23 us -> 2.65 us
  transfers between devices with their start and end apart: 33 -> 33, of which waited for: 8 -> 8; matrix products, arithmetic and copies ran while one was open for 4% -> 3% of each run, Pallas kernels for 42% -> 43%
where the time goes in v1:
time: 191 us
  Pallas kernels  125 us (65%)
  starting transfers between devices  30.3 us (16%)
  waiting for transfers between devices  19.6 us (10%)
  other arithmetic  9.63 us (5%)
  local copies, waits for them, and re-layouts  5.31 us (3%)
    pallas_call x1, Pallas kernels, ffn(): pl.pallas_call(ffn_body, name='feed_forward', grid=(rows // DENSE,), in_s...  41.4 us
    ppermute x23, starting transfers between devices, move(): return lax.ppermute(send, ('dp', 'tp'), perm)  27.8 us
    pallas_call x1, Pallas kernels, attn_bwd(): pl.pallas_call(attn_bwd_body, name='attn_bwd', grid=(rows // ROWS + 1,),...  25 us
    pallas_call x1, Pallas kernels, attn_fwd(): pl.pallas_call(attn_fwd_body, name='attn_fwd', grid=(rows // ROWS + 1,),...  24.6 us
    ppermute x23, waiting for transfers between devices, move(): return lax.ppermute(send, ('dp', 'tp'), perm)  19.1 us
    pallas_call x3, Pallas kernels, input_grad(): pl.pallas_call(input_grad_body, name='input_grad', grid=(THIRD,), in_spec...  16.2 us
    pallas_call x3, Pallas kernels, out_rows(): pl.pallas_call(out_body, name='block_out', grid=(THIRD,), in_specs=[spec(...  15.4 us
  transfers between devices with their start and end apart: 33, of which 8 were waited for; matrix products, arithmetic and copies ran while one was open for 3% of the time, Pallas kernels for 43%

profile of v1, /device:TPU:0, one launch (start us, length us, event | category | flops | bytes accessed | tf_op | source)
XLA Modules:
  0.0 190.8 jit_solution(4566909788086208882)
XLA Ops:
  0.6 0.5 collective-permute-start
  1.2 0.4 collective-permute-start.1
  1.8 0.8 reshape.30
  2.6 0.6 pad.4
  3.2 0.4 collective-permute-done.1.qvb_ref
  3.7 0.4 collective-permute-start.4
  4.3 0.4 collective-permute-start.6
  4.7 24.6 %attn_fwd.1 = (bf16[2400,512]{1,0:T(8,128)(2,1)}, bf16[24,128,1536]{2,1,0:T(8,128)(2,1)}, f32[2400,512]{1,0:T(8,128)}, bf16[2400,512]{1,0:T(8,128)(2,1)}, bf16[2...) custom-call(bf16[2400,512]{1,0:T(8,128)(2,1)} %x_ref.4, bf16[2400,512]{1,0:T(8,128)(2,1)} %x_ref.4, f32[24,1,128]{2,1,0:T(1,128)} %bitcast.6, ...), custom_call_target="tpu_custom_call" | custom-call | tf_op jit(solution)/shard_map/attn_fwd/pallas_call | solution.py:377
  29.4 0.5 copy-done.16
  29.9 0.4 copy-done.15
  30.3 0.3 copy-done.9
  30.7 41.4 %feed_forward.1 = (bf16[2400,2048]{1,0:T(8,128)(2,1)}, f32[2400,512]{1,0:T(8,128)}, bf16[2400,512]{1,0:T(8,128)(2,1)}, bf16[2304,512]{1,0:T(8,128)(2,1)}, bf16[2...) custom-call(f32[2400,512]{1,0:T(8,128)} %get-tuple-element.296.mixed_ref, bf16[2400,512]{1,0:T(8,128)(2,1)} %go_ref.1, ...), custom_call_target="tpu_custom_call" | custom-call | flops 49999998976 | bytes 40000000 | tf_op jit(solution)/shard_map/feed_forward/pallas_call | solution.py:415
  72.1 0.4 collective-permute-start.7
  72.5 5.2 %block_out.3.refs_0_ = bf16[2400,512]{1,0:T(8,128)(2,1)} custom-call(f32[2400,512]{1,0:T(8,128)} %get-tuple-element.296.mixed_ref, bf16[2400,2048]{1,0:T(8,128)(2,1)} %get-tuple-element.297.act_ref, bf16[1024,512]{1,0:T(8,128)(2,1)} %w2a_ref.4, bf16[1024,512]{1,0:T(8,128)(2,1)} %copy-done.9, f32[2,512]{1,0:T(2,128)} %ob_ref.4), custom_call_target="tpu_custom_call" | custom-call | flops 3000000000 | bytes 7000000 | tf_op jit(solution)/shard_map/block_out/pallas_call | solution.py:450
  77.7 2.3 %add.100 = bf16[2304,512]{1,0:T(8,128)(2,1)S(1)} add(bf16[2304,512]{1,0:T(8,128)(2,1)S(1)} %copy-done.10, bf16[2304,512]{1,0:T(8,128)(2,1)} %collective-permute-done.7) | non-fusion elementwise | flops 1179648 | bytes 7077888 | tf_op jit(solution)/shard_map/add | solution.py:686
  80.3 0.8 constant_dynamic-slice_fusion.7
  81.1 2.7 %collective-permute-start.8 = (bf16[768,512]{1,0:T(8,128)(2,1)S(1)}, bf16[768,512]{1,0:T(8,128)(2,1)S(1)}, u32[]{:S(2)}, u32[]{:S(2)}) collective-permute-start(bf16[768,512]{1,0:T(8,128)(2,1)S(1)} %constant_dynamic-slice_fusion.8), channel_id=1, source_target_pairs={{0,2},{1,5},{2,0},{3,7},{4,6},{5,1},{6,4},{7,3},{8,10},{9,13},{10,... | collective-permute-start | bytes 2359304 | tf_op jit(solution)/shard_map/ppermute | solution.py:657
  83.7 1.6 collective-permute-start.9
  85.3 25.0 %attn_bwd.1 = (bf16[2400,1536]{1,0:T(8,128)(2,1)}, f32[8,104,256]{2,1,0:T(8,128)}, bf16[768,512]{1,0:T(8,128)(2,1)}, bf16[768,512]{1,0:T(8,128)(2,1)}, f32[2,512]{1,0:T(2,128)}) custom-call(bf16[2400,512]{1,0:T(8,128)(2,1)} %get-tuple-element.192.n_ref, bf16[2400,512]{1,0:T(8,128)(2,1)} %get-tuple-element.193.do_ref, ...), custom_call_target="tpu_custom_call" | custom-call | flops 30000001024 | bytes 60000000 | tf_op jit(solution)/shard_map/attn_bwd/pallas_call | solution.py:468
  110.3 0.2 dynamic-slice_add_fusion
  110.6 1.1 dynamic-slice_add_fusion.2
  111.8 1.6 collective-permute-start.10
  113.4 0.5 collective-permute-start.11
  114.0 5.4 %input_grad.3 = (bf16[2400,512]{1,0:T(8,128)(2,1)}, f32[2,512]{1,0:T(2,128)}) custom-call(bf16[2400,512]{1,0:T(8,128)(2,1)} %x_ref.4, f32[2400,512]{1,0:T(8,128)} %get-tuple-element.242.gm_ref, bf16[2400,1536]{1,0:T(8,128)(2,1)} %get-tuple-element.243.d_ref, bf16[3,512,256]{2,1,0:T(8,128)(2,1)} %wa_ref.4, bf16[3,512,256]{2,1,0:T(8,128)(2,1)} %copy-done.8, ...), custom_call_target="tpu_custom_call" | custom-call | flops 3000000000 | bytes 7000000 | tf_op jit(solution)/shard_map/input_grad/pallas_call | solution.py:494
  119.4 0.3 collective-permute-done.10
  119.9 0.6 copy-done.11
  120.5 0.2 add.111
  120.7 1.6 collective-permute-start.15
  122.3 0.4 collective-permute-start.13
  122.7 0.8 collective-permute-start.14
  123.5 5.4 %input_grad.4 = (bf16[2400,512]{1,0:T(8,128)(2,1)}, f32[2,512]{1,0:T(2,128)}) custom-call(bf16[2400,512]{1,0:T(8,128)(2,1)} %x_ref.4, f32[2400,512]{1,0:T(8,128)} %get-tuple-element.242.gm_ref, bf16[2400,1536]{1,0:T(8,128)(2,1)} %get-tuple-element.243.d_ref, bf16[3,512,256]{2,1,0:T(8,128)(2,1)} %wa_ref.4, ...), custom_call_target="tpu_custom_call", output_to_operand_aliasing={{0}: (6, {})} | custom-call | flops 3000000000 | bytes 7000000 | tf_op jit(solution)/shard_map/input_grad/pallas_call | solution.py:494
  128.9 0.3 collective-permute-done.13
  129.5 2.4 %collective-permute-start.16 = (bf16[192,512]{1,0:T(8,128)(2,1)S(1)}, bf16[192,512]{1,0:T(8,128)(2,1)S(1)}, u32[]{:S(2)}, u32[]{:S(2)}) collective-permute-start(bf16[192,512]{1,0:T(8,128)(2,1)S(1)} %get-tuple-element.238), channel_id=1, source_target_pairs={{0,16},{1,3},{2,18},{3,1},{4,20},{5,7},{6,22},{7,5},{8,24},{9,11},... | collective-permute-start | bytes 589832 | tf_op jit(solution)/shard_map/ppermute | solution.py:657
  131.9 0.6 collective-permute-start.17
  132.5 1.0 collective-permute-start.18
  133.5 5.4 %input_grad.5 = (bf16[2400,512]{1,0:T(8,128)(2,1)}, f32[2,512]{1,0:T(2,128)}) custom-call(bf16[2400,512]{1,0:T(8,128)(2,1)} %x_ref.4, f32[2400,512]{1,0:T(8,128)} %get-tuple-element.242.gm_ref, bf16[2400,1536]{1,0:T(8,128)(2,1)} %get-tuple-element.243.d_ref, bf16[3,512,256]{2,1,0:T(8,128)(2,1)} %wa_ref.4, ...), custom_call_target="tpu_custom_call", output_to_operand_aliasing={{0}: (6, {})} | custom-call | flops 3000000000 | bytes 7000000 | tf_op jit(solution)/shard_map/input_grad/pallas_call | solution.py:494
  138.9 3.4 %collective-permute-done.17 = bf16[96,512]{1,0:T(8,128)(2,1)S(1)} collective-permute-done((bf16[96,512]{1,0:T(8,128)(2,1)S(1)}, bf16[96,512]{1,0:T(8,128)(2,1)S(1)}, u32[]{:S(2)}, u32[]{:S(2)}) %collective-permute-start.17) | collective-permute-done | bytes 98336 | tf_op jit(solution)/shard_map/ppermute | solution.py:657
  142.4 0.4 collective-permute-start.19
  142.8 1.4 collective-permute-start.20
  144.2 0.7 copy-done.3
  144.9 0.8 small_sums.1
  145.9 1.5 collective-permute-start.21
  147.4 5.1 %block_out.4.refs_0_ = bf16[2400,512]{1,0:T(8,128)(2,1)} custom-call(f32[2400,512]{1,0:T(8,128)} %get-tuple-element.296.mixed_ref, bf16[2400,2048]{1,0:T(8,128)(2,1)} %get-tuple-element.297.act_ref, bf16[1024,512]{1,0:T(8,128)(2,1)} %w2a_ref.4, bf16[1024,512]{1,0:T(8,128)(2,1)} %copy-done.9, f32[2,512]{1,0:T(2,128)} %ob_ref.4, ...), custom_call_target="tpu_custom_call", output_to_operand_aliasing={{}: (5, {})} | custom-call | flops 3000000000 | bytes 7000000 | tf_op jit(solution)/shard_map/block_out/pallas_call | solution.py:450
  152.7 1.0 collective-permute-start.23
  153.7 0.9 collective-permute-start.24
  154.6 1.7 collective-permute-start.25
  156.2 5.4 %collective-permute-done.25 = bf16[128,512]{1,0:T(8,128)(2,1)S(1)} collective-permute-done((bf16[128,512]{1,0:T(8,128)(2,1)S(1)}, bf16[128,512]{1,0:T(8,128)(2,1)S(1)}, u32[]{:S(2)}, u32[]{:S(2)}) %collective-permute-start.25) | collective-permute-done | bytes 131104 | tf_op jit(solution)/shard_map/ppermute | solution.py:657
  161.9 1.1 collective-permute-start.26
  163.0 1.1 collective-permute-start.27
  164.1 0.9 collective-permute-start.28
  165.0 5.1 %block_out.5 = bf16[2400,512]{1,0:T(8,128)(2,1)} custom-call(f32[2400,512]{1,0:T(8,128)} %get-tuple-element.296.mixed_ref, bf16[2400,2048]{1,0:T(8,128)(2,1)} %get-tuple-element.297.act_ref, bf16[1024,512]{1,0:T(8,128)(2,1)} %w2a_ref.4, bf16[1024,512]{1,0:T(8,128)(2,1)} %copy-done.9, f32[2,512]{1,0:T(2,128)} %ob_ref.4, ...), custom_call_target="tpu_custom_call", output_to_operand_aliasing={{}: (5, {})} | custom-call | flops 3000000000 | bytes 7000000 | tf_op jit(solution)/shard_map/block_out/pallas_call | solution.py:450
  170.1 2.0 %collective-permute-done.28 = bf16[128,512]{1,0:T(8,128)(2,1)S(1)} collective-permute-done((bf16[128,512]{1,0:T(8,128)(2,1)S(1)}, bf16[128,512]{1,0:T(8,128)(2,1)S(1)}, u32[]{:S(2)}, u32[]{:S(2)}) %collective-permute-start.28) | collective-permute-done | bytes 131104 | tf_op jit(solution)/shard_map/ppermute | solution.py:657
  172.2 1.0 collective-permute-start.29
  173.3 1.7 collective-permute-start.30
  174.9 0.8 collective-permute-start.31
  175.8 5.1 %collective-permute-done.30 = bf16[192,512]{1,0:T(8,128)(2,1)S(1)} collective-permute-done((bf16[192,512]{1,0:T(8,128)(2,1)S(1)}, bf16[192,512]{1,0:T(8,128)(2,1)S(1)}, u32[]{:S(2)}, u32[]{:S(2)}) %collective-permute-start.30) | collective-permute-done | bytes 196640 | tf_op jit(solution)/shard_map/ppermute | solution.py:657
  181.1 1.2 collective-permute-start.32
  182.5 0.3 broadcast_select_fusion
  182.8 1.6 fusion
  184.4 1.6 fusion.2
  186.0 0.9 slice_convert_fusion
  186.9 2.4 %collective-permute-done.32 = bf16[416,512]{1,0:T(8,128)(2,1)S(1)} collective-permute-done((bf16[416,512]{1,0:T(8,128)(2,1)S(1)}, bf16[416,512]{1,0:T(8,128)(2,1)S(1)}, u32[]{:S(2)}, u32[]{:S(2)}) %collective-permute-start.32) | collective-permute-done | bytes 426016 | tf_op jit(solution)/shard_map/ppermute | solution.py:657
  189.3 0.2 broadcast_select_fusion.5
  189.5 1.3 finish.1
  (103 shorter events, 2.3 us)
Async XLA Ops:
  0.6 3.0 %collective-permute-start = (bf16[3,512,256]{2,1,0:T(8,128)(2,1)}, bf16[3,512,256]{2,1,0:T(8,128)(2,1)S(1)}, u32[]{:S(2)}, u32[]{:S(2)}) collective-permute-start(bf16[3,512,256]{2,1,0:T(8,128)(2,1)} %wa_ref.4), channel_id=1, source_target_pairs={{0,1},{1,0},{2,3},{3,2},{4,5},{5,4},{6,7},{7,6},{8,9},{9,8},{10,11... | collective-permute-start | bytes 2359304 | tf_op jit(solution)/shard_map/ppermute | solution.py:770
  1.2 2.5 %collective-permute-start.2 = (bf16[256,512]{1,0:T(8,128)(2,1)}, bf16[256,512]{1,0:T(8,128)(2,1)S(1)}, u32[]{:S(2)}, u32[]{:S(2)}) collective-permute-start(bf16[256,512]{1,0:T(8,128)(2,1)} %pa_ref.3), channel_id=1, source_target_pairs={{0,1},{1,0},{2,3},{3,2},{4,5},{5,4},{6,7},{7,6},{8,9},{9,8},{10,11... | collective-permute-start | bytes 786440 | tf_op jit(solution)/shard_map/ppermute | solution.py:770
  1.2 2.4 %collective-permute-start.1 = (f32[2,256]{1,0:T(2,128)}, f32[2,256]{1,0:T(2,128)S(1)}, u32[]{:S(2)}, u32[]{:S(2)}) collective-permute-start(f32[2,256]{1,0:T(2,128)} %qva_ref.1), channel_id=1, source_target_pairs={{0,1},{1,0},{2,3},{3,2},{4,5},{5,4},{6,7},{7,6},{8,9},{9,8},{10,11... | collective-permute-start | bytes 6152 | tf_op jit(solution)/shard_map/ppermute | solution.py:770
  1.7 2.0 %collective-permute-start.3 = (f32[8,361]{1,0:T(8,128)}, f32[8,361]{1,0:T(8,128)S(1)}, u32[]{:S(2)}, u32[]{:S(2)}) collective-permute-start(f32[8,361]{1,0:T(8,128)} %bitcast.7), channel_id=1, source_target_pairs={{0,1},{1,0},{2,3},{3,2},{4,5},{5,4},{6,7},{7,6},{8,9},{9,8},{10,11... | collective-permute-start | bytes 34664 | tf_op jit(solution)/shard_map/ppermute | solution.py:770
  3.7 1.0 copy-start.14
  3.7 1.0 copy-start.13
  3.7 1.0 copy-start.12
  3.7 1.0 copy-start.8
  3.7 25.6 %collective-permute-start.4 = (bf16[512,1024]{1,0:T(8,128)(2,1)}, bf16[512,1024]{1,0:T(8,128)(2,1)S(1)}, u32[]{:S(2)}, u32[]{:S(2)}) collective-permute-start(bf16[512,1024]{1,0:T(8,128)(2,1)} %w1a_ref.1), channel_id=1, source_target_pairs={{0,1},{1,0},{2,3},{3,2},{4,5},{5,4},{6,7},{7,6},{8,9},{9,8},{10,11... | collective-permute-start | bytes 3145736 | tf_op jit(solution)/shard_map/ppermute | solution.py:770
  4.1 25.2 %collective-permute-start.5 = (bf16[1024,512]{1,0:T(8,128)(2,1)}, bf16[1024,512]{1,0:T(8,128)(2,1)S(1)}, u32[]{:S(2)}, u32[]{:S(2)}) collective-permute-start(bf16[1024,512]{1,0:T(8,128)(2,1)} %w2a_ref.4), channel_id=1, source_target_pairs={{0,1},{1,0},{2,3},{3,2},{4,5},{5,4},{6,7},{7,6},{8,9},{9,8},{10,11... | collective-permute-start | bytes 3145736 | tf_op jit(solution)/shard_map/ppermute | solution.py:770
  4.3 25.0 %collective-permute-start.6 = (f32[1024]{0:T(1024)}, f32[1024]{0:T(1024)S(1)}, u32[]{:S(2)}, u32[]{:S(2)}) collective-permute-start(f32[1024]{0:T(1024)} %param.21), channel_id=1, source_target_pairs={{0,1},{1,0},{2,3},{3,2},{4,5},{5,4},{6,7},{7,6},{8,9},{9,8},{10,11... | collective-permute-start | bytes 12296 | tf_op jit(solution)/shard_map/ppermute | solution.py:770
  29.3 0.6 copy-start.16
  29.4 1.0 copy-start.15
  29.4 1.3 copy-start.9
  72.1 5.6 %collective-permute-start.7 = (bf16[2304,512]{1,0:T(8,128)(2,1)}, bf16[2304,512]{1,0:T(8,128)(2,1)}, u32[]{:S(2)}, u32[]{:S(2)}) collective-permute-start(bf16[2304,512]{1,0:T(8,128)(2,1)} %get-tuple-element.179), channel_id=1, source_target_pairs={{0,1},{1,0},{2,3},{3,2},{4,5},{5,4},{6,7},{7,6},{8,9},{9,8},{10,11... | collective-permute-start | bytes 7077896 | tf_op jit(solution)/shard_map/ppermute | solution.py:680
  72.5 5.2 %copy-start.10 = (bf16[2304,512]{1,0:T(8,128)(2,1)S(1)}, bf16[2304,512]{1,0:T(8,128)(2,1)}, u32[]{:S(2)}) copy-start(bf16[2304,512]{1,0:T(8,128)(2,1)} %get-tuple-element.176) | copy-start | bytes 7077892
  81.1 29.3 %collective-permute-start.8 = (bf16[768,512]{1,0:T(8,128)(2,1)S(1)}, bf16[768,512]{1,0:T(8,128)(2,1)S(1)}, u32[]{:S(2)}, u32[]{:S(2)}) collective-permute-start(bf16[768,512]{1,0:T(8,128)(2,1)S(1)} %constant_dynamic-slice_fusion.8), channel_id=1, source_target_pairs={{0,2},{1,5},{2,0},{3,7},{4,6},{5,1},{6,4},{7,3},{8,10},{9,13},{10,... | collective-permute-start | bytes 2359304 | tf_op jit(solution)/shard_map/ppermute | solution.py:657
  83.7 26.6 %collective-permute-start.9 = (bf16[384,512]{1,0:T(8,128)(2,1)}, bf16[384,512]{1,0:T(8,128)(2,1)}, u32[]{:S(2)}, u32[]{:S(2)}) collective-permute-start(bf16[384,512]{1,0:T(8,128)(2,1)} %constant_dynamic-slice_fusion.7), channel_id=1, source_target_pairs={{0,8},{1,9},{2,10},{3,11},{4,12},{5,13},{6,14},{7,15},{8,0},{9,1},... | collective-permute-start | bytes 1179656 | tf_op jit(solution)/shard_map/ppermute | solution.py:657
  111.7 7.9 %collective-permute-start.12 = (bf16[768,512]{1,0:T(8,128)(2,1)}, bf16[768,512]{1,0:T(8,128)(2,1)S(1)}, u32[]{:S(2)}, u32[]{:S(2)}) collective-permute-start(bf16[768,512]{1,0:T(8,128)(2,1)} %get-tuple-element.208), channel_id=1, source_target_pairs={{0,1},{1,0},{2,3},{3,2},{4,5},{5,4},{6,7},{7,6},{8,9},{9,8},{10,11... | collective-permute-start | bytes 2359304 | tf_op jit(solution)/shard_map/ppermute | solution.py:680
  111.8 7.8 %collective-permute-start.10 = (bf16[384,512]{1,0:T(8,128)(2,1)S(1)}, bf16[384,512]{1,0:T(8,128)(2,1)S(1)}, u32[]{:S(2)}, u32[]{:S(2)}) collective-permute-start(bf16[384,512]{1,0:T(8,128)(2,1)S(1)} %constant_dynamic-slice_fusion.6), channel_id=1, source_target_pairs={{0,4},{1,9},{2,6},{3,11},{4,0},{5,13},{6,2},{7,15},{8,12},{9,1},{1... | collective-permute-start | bytes 1179656 | tf_op jit(solution)/shard_map/ppermute | solution.py:657
  113.4 5.9 %collective-permute-start.11 = (bf16[192,512]{1,0:T(8,128)(2,1)S(1)}, bf16[192,512]{1,0:T(8,128)(2,1)S(1)}, u32[]{:S(2)}, u32[]{:S(2)}) collective-permute-start(bf16[192,512]{1,0:T(8,128)(2,1)S(1)} %constant_dynamic-slice_fusion.5), channel_id=1, source_target_pairs={{0,2},{1,3},{2,0},{3,1},{4,6},{5,7},{6,4},{7,5},{8,10},{9,11},{10,... | collective-permute-start | bytes 589832 | tf_op jit(solution)/shard_map/ppermute | solution.py:657
  119.4 1.1 copy-start.11
  120.7 8.5 %collective-permute-start.15 = (bf16[384,512]{1,0:T(8,128)(2,1)S(1)}, bf16[384,512]{1,0:T(8,128)(2,1)S(1)}, u32[]{:S(2)}, u32[]{:S(2)}) collective-permute-start(bf16[384,512]{1,0:T(8,128)(2,1)S(1)} %constant_dynamic-slice_fusion.2), channel_id=1, source_target_pairs={{0,2},{1,5},{2,0},{3,7},{4,6},{5,1},{6,4},{7,3},{8,10},{9,13},{10,... | collective-permute-start | bytes 1179656 | tf_op jit(solution)/shard_map/ppermute | solution.py:657
  122.3 6.9 %collective-permute-start.13 = (bf16[192,512]{1,0:T(8,128)(2,1)S(1)}, bf16[192,512]{1,0:T(8,128)(2,1)S(1)}, u32[]{:S(2)}, u32[]{:S(2)}) collective-permute-start(bf16[192,512]{1,0:T(8,128)(2,1)S(1)} %constant_dynamic-slice_fusion.4), channel_id=1, source_target_pairs={{0,8},{1,17},{2,10},{3,19},{4,12},{5,21},{6,14},{7,23},{8,0},{9,25... | collective-permute-start | bytes 589832 | tf_op jit(solution)/shard_map/ppermute | solution.py:657
  122.7 6.2 %collective-permute-start.14 = (bf16[96,512]{1,0:T(8,128)(2,1)S(1)}, bf16[96,512]{1,0:T(8,128)(2,1)S(1)}, u32[]{:S(2)}, u32[]{:S(2)}) collective-permute-start(bf16[96,512]{1,0:T(8,128)(2,1)S(1)} %constant_dynamic-slice_fusion.3), channel_id=1, source_target_pairs={{0,4},{1,5},{2,6},{3,7},{4,0},{5,1},{6,2},{7,3},{8,12},{9,13},{10,... | collective-permute-start | bytes 294920 | tf_op jit(solution)/shard_map/ppermute | solution.py:657
  129.4 14.8 %copy-start = (f32[16,256]{1,0:T(8,128)S(1)}, f32[16,256]{1,0:T(8,128)}, u32[]{:S(2)}) copy-start(f32[16,256]{1,0:T(8,128)} %get-tuple-element.263.idx_ref) | copy-start | bytes 49156
  129.4 14.8 %copy-start.1 = (f32[2,512]{1,0:T(2,128)S(1)}, f32[2,512]{1,0:T(2,128)}, u32[]{:S(2)}) copy-start(f32[2,512]{1,0:T(2,128)} %get-tuple-element.266.gs1a_ref) | copy-start | bytes 12292
  129.4 14.8 %copy-start.2 = (f32[2,512]{1,0:T(2,128)S(1)}, f32[2,512]{1,0:T(2,128)}, u32[]{:S(2)}) copy-start(f32[2,512]{1,0:T(2,128)} %get-tuple-element.267.gs1b_ref) | copy-start | bytes 12292
  129.4 14.8 %copy-start.4 = (f32[8,104,256]{2,1,0:T(8,128)S(1)}, f32[8,104,256]{2,1,0:T(8,128)}, u32[]{:S(2)}) copy-start(f32[8,104,256]{2,1,0:T(8,128)} %get-tuple-element.264.t_ref) | copy-start | bytes 2555908
  129.5 14.7 %copy-start.5 = (f32[1,2048]{1,0:T(1,128)S(1)}, f32[1,2048]{1,0:T(1,128)}, u32[]{:S(2)}) copy-start(f32[1,2048]{1,0:T(1,128)} %get-tuple-element.269.gb1_ref) | copy-start | bytes 24580
  129.5 14.7 %copy-start.6 = (f32[4,512]{1,0:T(4,128)S(1)}, f32[4,512]{1,0:T(4,128)}, u32[]{:S(2)}) copy-start(f32[4,512]{1,0:T(4,128)} %get-tuple-element.265.gs2_ref) | copy-start | bytes 24580
  129.5 14.7 %copy-start.7 = (f32[2,512]{1,0:T(2,128)S(1)}, f32[2,512]{1,0:T(2,128)}, u32[]{:S(2)}) copy-start(f32[2,512]{1,0:T(2,128)} %get-tuple-element.270.gqv_ref) | copy-start | bytes 12292
  129.5 12.8 %collective-permute-start.16 = (bf16[192,512]{1,0:T(8,128)(2,1)S(1)}, bf16[192,512]{1,0:T(8,128)(2,1)S(1)}, u32[]{:S(2)}, u32[]{:S(2)}) collective-permute-start(bf16[192,512]{1,0:T(8,128)(2,1)S(1)} %get-tuple-element.238), channel_id=1, source_target_pairs={{0,16},{1,3},{2,18},{3,1},{4,20},{5,7},{6,22},{7,5},{8,24},{9,11},... | collective-permute-start | bytes 589832 | tf_op jit(solution)/shard_map/ppermute | solution.py:657
  131.9 10.4 %collective-permute-start.17 = (bf16[96,512]{1,0:T(8,128)(2,1)S(1)}, bf16[96,512]{1,0:T(8,128)(2,1)S(1)}, u32[]{:S(2)}, u32[]{:S(2)}) collective-permute-start(bf16[96,512]{1,0:T(8,128)(2,1)S(1)} %dynamic-slice_add_fusion.8), channel_id=1, source_target_pairs={{0,16},{1,17},{2,18},{3,19},{4,20},{5,21},{6,22},{7,23},{8,24},{9,... | collective-permute-start | bytes 294920 | tf_op jit(solution)/shard_map/ppermute | solution.py:657
  132.5 9.8 %collective-permute-start.18 = (bf16[192,512]{1,0:T(8,128)(2,1)S(1)}, bf16[192,512]{1,0:T(8,128)(2,1)S(1)}, u32[]{:S(2)}, u32[]{:S(2)}) collective-permute-start(bf16[192,512]{1,0:T(8,128)(2,1)S(1)} %get-tuple-element.240), channel_id=1, source_target_pairs={{0,4},{1,9},{2,6},{3,11},{4,0},{5,13},{6,2},{7,15},{8,12},{9,1},{1... | collective-permute-start | bytes 589832 | tf_op jit(solution)/shard_map/ppermute | solution.py:657
  142.4 10.2 %collective-permute-start.19 = (bf16[192,512]{1,0:T(8,128)(2,1)S(1)}, bf16[192,512]{1,0:T(8,128)(2,1)S(1)}, u32[]{:S(2)}, u32[]{:S(2)}) collective-permute-start(bf16[192,512]{1,0:T(8,128)(2,1)S(1)} %add.117), channel_id=1, source_target_pairs={{0,8},{1,17},{2,10},{3,19},{4,12},{5,21},{6,14},{7,23},{8,0},{9,25... | collective-permute-start | bytes 589832 | tf_op jit(solution)/shard_map/ppermute | solution.py:657
  142.8 9.8 %collective-permute-start.20 = (bf16[96,512]{1,0:T(8,128)(2,1)S(1)}, bf16[96,512]{1,0:T(8,128)(2,1)S(1)}, u32[]{:S(2)}, u32[]{:S(2)}) collective-permute-start(bf16[96,512]{1,0:T(8,128)(2,1)S(1)} %add.118), channel_id=1, source_target_pairs={{0,4},{1,5},{2,6},{3,7},{4,0},{5,1},{6,2},{7,3},{8,12},{9,13},{10,... | collective-permute-start | bytes 294920 | tf_op jit(solution)/shard_map/ppermute | solution.py:657
  144.2 0.7 copy-start.3
  145.9 6.6 %collective-permute-start.21 = (bf16[96,512]{1,0:T(8,128)(2,1)S(1)}, bf16[96,512]{1,0:T(8,128)(2,1)S(1)}, u32[]{:S(2)}, u32[]{:S(2)}) collective-permute-start(bf16[96,512]{1,0:T(8,128)(2,1)S(1)} %constant_dynamic-slice_fusion), channel_id=1, source_target_pairs={{0,8},{1,17},{2,10},{3,19},{4,12},{5,21},{6,14},{7,23},{8,0},{9,25... | collective-permute-start | bytes 294920 | tf_op jit(solution)/shard_map/ppermute | solution.py:657
  147.4 5.1 %collective-permute-start.22 = (bf16[32,512]{1,0:T(8,128)(2,1)S(1)}, bf16[32,512]{1,0:T(8,128)(2,1)S(1)}, u32[]{:S(2)}, u32[]{:S(2)}) collective-permute-start(bf16[32,512]{1,0:T(8,128)(2,1)S(1)} %get-tuple-element.274), channel_id=1, source_target_pairs={{0,1},{1,0},{2,3},{3,2},{4,5},{5,4},{6,7},{7,6},{8,9},{9,8},{10,11... | collective-permute-start | bytes 98312 | tf_op jit(solution)/shard_map/ppermute | solution.py:680
  152.7 9.0 %collective-permute-start.23 = (bf16[384,512]{1,0:T(8,128)(2,1)S(1)}, bf16[384,512]{1,0:T(8,128)(2,1)S(1)}, u32[]{:S(2)}, u32[]{:S(2)}) collective-permute-start(bf16[384,512]{1,0:T(8,128)(2,1)S(1)} %pad_maximum_fusion.5), channel_id=1, source_target_pairs={{0,4},{1,9},{2,6},{3,11},{4,0},{5,13},{6,2},{7,15},{8,12},{9,1},{1... | collective-permute-start | bytes 1179656 | tf_op jit(solution)/shard_map/ppermute | solution.py:657
  153.7 8.0 %collective-permute-start.24 = (bf16[192,512]{1,0:T(8,128)(2,1)S(1)}, bf16[192,512]{1,0:T(8,128)(2,1)S(1)}, u32[]{:S(2)}, u32[]{:S(2)}) collective-permute-start(bf16[192,512]{1,0:T(8,128)(2,1)S(1)} %pad_maximum_fusion.9), channel_id=1, source_target_pairs={{0,2},{1,3},{2,0},{3,1},{4,6},{5,7},{6,4},{7,5},{8,10},{9,11},{10,... | collective-permute-start | bytes 589832 | tf_op jit(solution)/shard_map/ppermute | solution.py:657
  154.6 7.1 %collective-permute-start.25 = (bf16[128,512]{1,0:T(8,128)(2,1)S(1)}, bf16[128,512]{1,0:T(8,128)(2,1)S(1)}, u32[]{:S(2)}, u32[]{:S(2)}) collective-permute-start(bf16[128,512]{1,0:T(8,128)(2,1)S(1)} %pad_maximum_fusion.11), channel_id=1, source_target_pairs={{0,16},{1,3},{2,18},{3,1},{4,20},{5,7},{6,22},{7,5},{8,24},{9,11},... | collective-permute-start | bytes 393224 | tf_op jit(solution)/shard_map/ppermute | solution.py:657
  161.9 10.2 %collective-permute-start.26 = (bf16[384,512]{1,0:T(8,128)(2,1)S(1)}, bf16[384,512]{1,0:T(8,128)(2,1)S(1)}, u32[]{:S(2)}, u32[]{:S(2)}) collective-permute-start(bf16[384,512]{1,0:T(8,128)(2,1)S(1)} %get-tuple-element.293), channel_id=1, source_target_pairs={{0,2},{1,5},{2,0},{3,7},{4,6},{5,1},{6,4},{7,3},{8,10},{9,13},{10,... | collective-permute-start | bytes 1179656 | tf_op jit(solution)/shard_map/ppermute | solution.py:657
  163.0 9.2 %collective-permute-start.27 = (bf16[192,512]{1,0:T(8,128)(2,1)S(1)}, bf16[192,512]{1,0:T(8,128)(2,1)S(1)}, u32[]{:S(2)}, u32[]{:S(2)}) collective-permute-start(bf16[192,512]{1,0:T(8,128)(2,1)S(1)} %get-tuple-element.294), channel_id=1, source_target_pairs={{0,8},{1,9},{2,10},{3,11},{4,12},{5,13},{6,14},{7,15},{8,0},{9,1},... | collective-permute-start | bytes 589832 | tf_op jit(solution)/shard_map/ppermute | solution.py:657
  164.1 8.0 %collective-permute-start.28 = (bf16[128,512]{1,0:T(8,128)(2,1)S(1)}, bf16[128,512]{1,0:T(8,128)(2,1)S(1)}, u32[]{:S(2)}, u32[]{:S(2)}) collective-permute-start(bf16[128,512]{1,0:T(8,128)(2,1)S(1)} %pad_maximum_fusion.12), channel_id=1, source_target_pairs={{0,8},{1,17},{2,10},{3,19},{4,12},{5,21},{6,14},{7,23},{8,0},{9,25... | collective-permute-start | bytes 393224 | tf_op jit(solution)/shard_map/ppermute | solution.py:657
  172.2 8.8 %collective-permute-start.29 = (bf16[384,512]{1,0:T(8,128)(2,1)S(1)}, bf16[384,512]{1,0:T(8,128)(2,1)S(1)}, u32[]{:S(2)}, u32[]{:S(2)}) collective-permute-start(bf16[384,512]{1,0:T(8,128)(2,1)S(1)} %get-tuple-element.305), channel_id=1, source_target_pairs={{0,2},{1,5},{2,0},{3,7},{4,6},{5,1},{6,4},{7,3},{8,10},{9,13},{10,... | collective-permute-start | bytes 1179656 | tf_op jit(solution)/shard_map/ppermute | solution.py:657
  173.3 7.7 %collective-permute-start.30 = (bf16[192,512]{1,0:T(8,128)(2,1)S(1)}, bf16[192,512]{1,0:T(8,128)(2,1)S(1)}, u32[]{:S(2)}, u32[]{:S(2)}) collective-permute-start(bf16[192,512]{1,0:T(8,128)(2,1)S(1)} %get-tuple-element.306), channel_id=1, source_target_pairs={{0,8},{1,9},{2,10},{3,11},{4,12},{5,13},{6,14},{7,15},{8,0},{9,1},... | collective-permute-start | bytes 589832 | tf_op jit(solution)/shard_map/ppermute | solution.py:657
  174.9 6.0 %collective-permute-start.31 = (bf16[224,512]{1,0:T(8,128)(2,1)S(1)}, bf16[224,512]{1,0:T(8,128)(2,1)S(1)}, u32[]{:S(2)}, u32[]{:S(2)}) collective-permute-start(bf16[224,512]{1,0:T(8,128)(2,1)S(1)} %pad_maximum_fusion.8), channel_id=1, source_target_pairs={{0,4},{1,9},{2,6},{3,11},{4,0},{5,13},{6,2},{7,15},{8,12},{9,1},{1... | collective-permute-start | bytes 688136 | tf_op jit(solution)/shard_map/ppermute | solution.py:657
  181.1 8.2 %collective-permute-start.32 = (bf16[416,512]{1,0:T(8,128)(2,1)S(1)}, bf16[416,512]{1,0:T(8,128)(2,1)S(1)}, u32[]{:S(2)}, u32[]{:S(2)}) collective-permute-start(bf16[416,512]{1,0:T(8,128)(2,1)S(1)} %pad_maximum_fusion.4), channel_id=1, source_target_pairs={{0,2},{1,5},{2,0},{3,7},{4,6},{5,1},{6,4},{7,3},{8,10},{9,13},{10,... | collective-permute-start | bytes 1277960 | tf_op jit(solution)/shard_map/ppermute | solution.py:657

commit v2 on v1

--- a/solution.py
+++ b/solution.py
@@ -365,7 +365,8 @@
     return pl.BlockSpec((GROUP,) + shape, lambda i: (i,) + (0,) * len(shape))
 
 
-PARAMS = pltpu.CompilerParams(vmem_limit_bytes=60 << 20, dimension_semantics=("arbitrary",))
+def params(mib):
+    return pltpu.CompilerParams(vmem_limit_bytes=mib << 20, dimension_semantics=("arbitrary",))
 
 
 def attn_fwd(x, pages, rel_index, ta, tb, wa, wb, qva, qvb, pa, pb, ob, gain, shift):
@@ -401,7 +402,7 @@
             pltpu.VMEM((8, KEYS, SLAB), F32),
             pltpu.VMEM((LANES, LANES), F32),
         ],
-        compiler_params=PARAMS,
+        compiler_params=params(58),
     )(x, x, pages, rel_index, ta, tb, wa, wb, qva, qvb, pa, pb, ob, gain, shift)
 
 
@@ -435,7 +436,7 @@
             pltpu.VMEM((8, 2048), F32),
             pltpu.VMEM((4, 8, 512), F32),
         ],
-        compiler_params=PARAMS,
+        compiler_params=params(50),
         cost_estimate=cost(50e9, 40e6),
     )(mixed, go, att, *small)
 
@@ -455,7 +456,7 @@
         out_specs=spec(512),
         out_shape=shaped((rows, 512), BF),
         input_output_aliases={5: 0} if old else {},
-        compiler_params=PARAMS,
+        compiler_params=params(60),
         cost_estimate=cost(3e9, 7e6),
     )(mixed, act, w2a, w2b, ob, *old)
 
@@ -483,7 +484,7 @@
             pltpu.VMEM((512, 1536), F32),
             pltpu.VMEM((2, 8, 512), F32),
         ],
-        compiler_params=PARAMS,
+        compiler_params=params(54),
         cost_estimate=cost(30e9, 60e6),
     )(n, do, qkv, probs)
 
@@ -500,7 +501,7 @@
         out_shape=[shaped((rows, 512), BF), shaped((2, 512), F32)],
         scratch_shapes=[pltpu.VMEM((2, 8, 512), F32)],
         input_output_aliases={6: 0} if old else {},
-        compiler_params=PARAMS,
+        compiler_params=params(60),
         cost_estimate=cost(3e9, 7e6),
     )(x, gm, d, wa, wb, gain, *old)
 
@@ -790,7 +791,7 @@
     pair = Pair(*gf)
     out = advance([pair], *rows_out(0))
     if SPLIT:
-        cut = 2 * pair.other.shape[0] // 3
+        cut = 1664
         f = [Chain(dp_size, pair.total()[:cut], (bits, turned)), Chain(dp_size, pair.total()[cut:], (deep, deep))]
     else:
         f = [Chain(dp_size, pair.total(), (bits, turned))]

time: 191 us -> 188 us (0.984)
  transfers between devices with their start and end apart: 33 -> 33, of which waited for: 8 -> 8; matrix products, arithmetic and copies ran while one was open for 3% -> 3% of each run, Pallas kernels for 43% -> 44%
where the time goes in v2:
time: 188 us
  Pallas kernels  124 us (66%)
  starting transfers between devices  29.4 us (16%)
  waiting for transfers between devices  19.4 us (10%)
  other arithmetic  8.63 us (5%)
  local copies, waits for them, and re-layouts  4.89 us (3%)
    pallas_call x1, Pallas kernels, ffn(): pl.pallas_call(ffn_body, name='feed_forward', grid=(rows // DENSE,), in_s...  40.9 us
    ppermute x23, starting transfers between devices, move(): return lax.ppermute(send, ('dp', 'tp'), perm)  26.9 us
    pallas_call x1, Pallas kernels, attn_bwd(): pl.pallas_call(attn_bwd_body, name='attn_bwd', grid=(rows // ROWS + 1,),...  25 us
    pallas_call x1, Pallas kernels, attn_fwd(): pl.pallas_call(attn_fwd_body, name='attn_fwd', grid=(rows // ROWS + 1,),...  24.7 us
    ppermute x23, waiting for transfers between devices, move(): return lax.ppermute(send, ('dp', 'tp'), perm)  18.9 us
    pallas_call x3, Pallas kernels, input_grad(): pl.pallas_call(input_grad_body, name='input_grad', grid=(THIRD,), in_spec...  16.2 us
    pallas_call x3, Pallas kernels, out_rows(): pl.pallas_call(out_body, name='block_out', grid=(THIRD,), in_specs=[spec(...  15.4 us
  transfers between devices with their start and end apart: 33, of which 8 were waited for; matrix products, arithmetic and copies ran while one was open for 3% of the time, Pallas kernels for 44%

profile of v2, /device:TPU:0, one launch (start us, length us, event | category | flops | bytes accessed | tf_op | source)
XLA Modules:
  0.0 187.9 jit_solution(17850067093457139613)
XLA Ops:
  0.6 0.5 collective-permute-start
  1.2 0.4 collective-permute-start.1
  1.8 0.8 reshape.30
  2.6 0.6 pad.4
  3.2 0.4 collective-permute-done.1.qvb_ref
  3.8 0.4 collective-permute-start.4
  4.2 0.1 collective-permute-start.5
  4.4 0.4 collective-permute-start.6
  4.7 24.7 %attn_fwd.1 = (bf16[2400,512]{1,0:T(8,128)(2,1)}, bf16[24,128,1536]{2,1,0:T(8,128)(2,1)}, f32[2400,512]{1,0:T(8,128)}, bf16[2400,512]{1,0:T(8,128)(2,1)}, bf16[2...) custom-call(bf16[2400,512]{1,0:T(8,128)(2,1)} %x_ref.4, bf16[2400,512]{1,0:T(8,128)(2,1)} %x_ref.4, f32[24,1,128]{2,1,0:T(1,128)} %bitcast.8, ...), custom_call_target="tpu_custom_call" | custom-call | tf_op jit(solution)/shard_map/attn_fwd/pallas_call | solution.py:378
  29.5 1.0 copy-done.15
  30.5 0.9 copy-done.3
  31.4 40.9 %feed_forward.1 = (bf16[2400,2048]{1,0:T(8,128)(2,1)}, f32[2400,512]{1,0:T(8,128)}, bf16[2400,512]{1,0:T(8,128)(2,1)}, bf16[2304,512]{1,0:T(8,128)(2,1)}, bf16[2...) custom-call(f32[2400,512]{1,0:T(8,128)} %get-tuple-element.296.mixed_ref, ...), custom_call_target="tpu_custom_call" | custom-call | flops 49999998976 | bytes 40000000 | tf_op jit(solution)/shard_map/feed_forward/pallas_call | solution.py:416
  72.3 0.4 collective-permute-start.7
  72.8 5.2 %block_out.3.refs_0_ = bf16[2400,512]{1,0:T(8,128)(2,1)} custom-call(f32[2400,512]{1,0:T(8,128)} %get-tuple-element.296.mixed_ref, bf16[2400,2048]{1,0:T(8,128)(2,1)} %get-tuple-element.297.act_ref, bf16[1024,512]{1,0:T(8,128)(2,1)} %w2a_ref.4, bf16[1024,512]{1,0:T(8,128)(2,1)} %copy-done.15, f32[2,512]{1,0:T(2,128)} %ob_ref.4), custom_call_target="tpu_custom_call" | custom-call | flops 3000000000 | bytes 7000000 | tf_op jit(solution)/shard_map/block_out/pallas_call | solution.py:451
  78.0 2.3 %add.100 = bf16[2304,512]{1,0:T(8,128)(2,1)S(1)} add(bf16[2304,512]{1,0:T(8,128)(2,1)S(1)} %copy-done.16, bf16[2304,512]{1,0:T(8,128)(2,1)} %collective-permute-done.7) | non-fusion elementwise | flops 1179648 | bytes 7077888 | tf_op jit(solution)/shard_map/add | solution.py:687
  80.6 2.7 %collective-permute-start.8 = (bf16[832,512]{1,0:T(8,128)(2,1)S(1)}, bf16[832,512]{1,0:T(8,128)(2,1)S(1)}, u32[]{:S(2)}, u32[]{:S(2)}) collective-permute-start(bf16[832,512]{1,0:T(8,128)(2,1)S(1)} %constant_dynamic-slice_fusion.8), channel_id=1, source_target_pairs={{0,2},{1,5},{2,0},{3,7},{4,6},{5,1},{6,4},{7,3},{8,10},{9,13},{10,... | collective-permute-start | bytes 2555912 | tf_op jit(solution)/shard_map/ppermute | solution.py:658
  83.3 1.6 collective-permute-start.9
  84.9 25.0 %attn_bwd.1 = (bf16[2400,1536]{1,0:T(8,128)(2,1)}, f32[8,104,256]{2,1,0:T(8,128)}, bf16[768,512]{1,0:T(8,128)(2,1)}, bf16[768,512]{1,0:T(8,128)(2,1)}, f32[2,512]{1,0:T(2,128)}) custom-call(bf16[2400,512]{1,0:T(8,128)(2,1)} %get-tuple-element.192.n_ref, bf16[2400,512]{1,0:T(8,128)(2,1)} %get-tuple-element.193.do_ref, ...), custom_call_target="tpu_custom_call" | custom-call | flops 30000001024 | bytes 60000000 | tf_op jit(solution)/shard_map/attn_bwd/pallas_call | solution.py:469
  109.9 0.2 dynamic-slice_add_fusion
  110.4 1.6 collective-permute-start.10
  112.0 0.5 collective-permute-start.11
  112.5 5.4 %input_grad.3 = (bf16[2400,512]{1,0:T(8,128)(2,1)}, f32[2,512]{1,0:T(2,128)}) custom-call(bf16[2400,512]{1,0:T(8,128)(2,1)} %x_ref.4, f32[2400,512]{1,0:T(8,128)} %get-tuple-element.242.gm_ref, bf16[2400,1536]{1,0:T(8,128)(2,1)} %get-tuple-element.243.d_ref, bf16[3,512,256]{2,1,0:T(8,128)(2,1)} %wa_ref.4, bf16[3,512,256]{2,1,0:T(8,128)(2,1)} %copy-done.14, ...), custom_call_target="tpu_custom_call" | custom-call | flops 3000000000 | bytes 7000000 | tf_op jit(solution)/shard_map/input_grad/pallas_call | solution.py:495
  117.9 0.7 collective-permute-done.10
  118.8 0.2 copy-done.17
  119.1 0.2 add.111
  119.3 1.6 collective-permute-start.15
  120.9 0.5 collective-permute-start.13
  121.4 0.5 collective-permute-start.14
  121.8 5.4 %input_grad.4 = (bf16[2400,512]{1,0:T(8,128)(2,1)}, f32[2,512]{1,0:T(2,128)}) custom-call(bf16[2400,512]{1,0:T(8,128)(2,1)} %x_ref.4, f32[2400,512]{1,0:T(8,128)} %get-tuple-element.242.gm_ref, bf16[2400,1536]{1,0:T(8,128)(2,1)} %get-tuple-element.243.d_ref, bf16[3,512,256]{2,1,0:T(8,128)(2,1)} %wa_ref.4, ...), custom_call_target="tpu_custom_call", output_to_operand_aliasing={{0}: (6, {})} | custom-call | flops 3000000000 | bytes 7000000 | tf_op jit(solution)/shard_map/input_grad/pallas_call | solution.py:495
  127.2 1.2 collective-permute-done.13
  128.6 0.1 dynamic-slice_add_fusion.2
  128.8 1.4 collective-permute-start.16
  130.2 1.6 collective-permute-start.17
  131.8 0.3 collective-permute-start.18
  132.1 5.4 %input_grad.5 = (bf16[2400,512]{1,0:T(8,128)(2,1)}, f32[2,512]{1,0:T(2,128)}) custom-call(bf16[2400,512]{1,0:T(8,128)(2,1)} %x_ref.4, f32[2400,512]{1,0:T(8,128)} %get-tuple-element.242.gm_ref, bf16[2400,1536]{1,0:T(8,128)(2,1)} %get-tuple-element.243.d_ref, bf16[3,512,256]{2,1,0:T(8,128)(2,1)} %wa_ref.4, ...), custom_call_target="tpu_custom_call", output_to_operand_aliasing={{0}: (6, {})} | custom-call | flops 3000000000 | bytes 7000000 | tf_op jit(solution)/shard_map/input_grad/pallas_call | solution.py:495
  137.5 3.0 %collective-permute-done.17 = bf16[80,512]{1,0:T(8,128)(2,1)S(1)} collective-permute-done((bf16[80,512]{1,0:T(8,128)(2,1)S(1)}, bf16[80,512]{1,0:T(8,128)(2,1)S(1)}, u32[]{:S(2)}, u32[]{:S(2)}) %collective-permute-start.17) | collective-permute-done | bytes 81952 | tf_op jit(solution)/shard_map/ppermute | solution.py:658
  140.6 0.2 collective-permute-start.19
  140.9 1.2 collective-permute-start.20
  142.1 0.7 copy-done.11
  142.8 0.8 small_sums.1
  143.7 1.9 %collective-permute-start.21 = (bf16[96,512]{1,0:T(8,128)(2,1)S(1)}, bf16[96,512]{1,0:T(8,128)(2,1)S(1)}, u32[]{:S(2)}, u32[]{:S(2)}) collective-permute-start(bf16[96,512]{1,0:T(8,128)(2,1)S(1)} %constant_dynamic-slice_fusion), channel_id=1, source_target_pairs={{0,8},{1,17},{2,10},{3,19},{4,12},{5,21},{6,14},{7,23},{8,0},{9,25... | collective-permute-start | bytes 294920 | tf_op jit(solution)/shard_map/ppermute | solution.py:658
  145.6 5.1 %block_out.4.refs_0_ = bf16[2400,512]{1,0:T(8,128)(2,1)} custom-call(f32[2400,512]{1,0:T(8,128)} %get-tuple-element.296.mixed_ref, bf16[2400,2048]{1,0:T(8,128)(2,1)} %get-tuple-element.297.act_ref, bf16[1024,512]{1,0:T(8,128)(2,1)} %w2a_ref.4, bf16[1024,512]{1,0:T(8,128)(2,1)} %copy-done.15, f32[2,512]{1,0:T(2,128)} %ob_ref.4, ...), custom_call_target="tpu_custom_call", output_to_operand_aliasing={{}: (5, {})} | custom-call | flops 3000000000 | bytes 7000000 | tf_op jit(solution)/shard_map/block_out/pallas_call | solution.py:451
  151.0 0.9 collective-permute-start.23
  151.9 1.0 collective-permute-start.24
  152.9 1.8 collective-permute-start.25
  154.7 5.1 %collective-permute-done.25 = bf16[128,512]{1,0:T(8,128)(2,1)S(1)} collective-permute-done((bf16[128,512]{1,0:T(8,128)(2,1)S(1)}, bf16[128,512]{1,0:T(8,128)(2,1)S(1)}, u32[]{:S(2)}, u32[]{:S(2)}) %collective-permute-start.25) | collective-permute-done | bytes 131104 | tf_op jit(solution)/shard_map/ppermute | solution.py:658
  159.9 0.2 broadcast_select_fusion.2
  160.1 1.3 collective-permute-start.26
  161.4 0.8 collective-permute-start.27
  162.2 1.2 collective-permute-start.28
  163.4 5.1 %block_out.5 = bf16[2400,512]{1,0:T(8,128)(2,1)} custom-call(f32[2400,512]{1,0:T(8,128)} %get-tuple-element.296.mixed_ref, bf16[2400,2048]{1,0:T(8,128)(2,1)} %get-tuple-element.297.act_ref, bf16[1024,512]{1,0:T(8,128)(2,1)} %w2a_ref.4, bf16[1024,512]{1,0:T(8,128)(2,1)} %copy-done.15, f32[2,512]{1,0:T(2,128)} %ob_ref.4, ...), custom_call_target="tpu_custom_call", output_to_operand_aliasing={{}: (5, {})} | custom-call | flops 3000000000 | bytes 7000000 | tf_op jit(solution)/shard_map/block_out/pallas_call | solution.py:451
  168.5 1.3 collective-permute-done.28
  169.9 1.1 collective-permute-start.29
  171.0 0.9 collective-permute-start.30
  171.9 1.1 collective-permute-start.31
  173.0 5.1 %collective-permute-done.30 = bf16[160,512]{1,0:T(8,128)(2,1)S(1)} collective-permute-done((bf16[160,512]{1,0:T(8,128)(2,1)S(1)}, bf16[160,512]{1,0:T(8,128)(2,1)S(1)}, u32[]{:S(2)}, u32[]{:S(2)}) %collective-permute-start.30) | collective-permute-done | bytes 163872 | tf_op jit(solution)/shard_map/ppermute | solution.py:658
  178.2 1.2 collective-permute-start.32
  179.6 0.3 broadcast_select_fusion
  179.9 1.6 fusion
  181.6 1.6 fusion.2
  183.1 0.9 slice_convert_fusion
  184.0 2.4 %collective-permute-done.32 = bf16[416,512]{1,0:T(8,128)(2,1)S(1)} collective-permute-done((bf16[416,512]{1,0:T(8,128)(2,1)S(1)}, bf16[416,512]{1,0:T(8,128)(2,1)S(1)}, u32[]{:S(2)}, u32[]{:S(2)}) %collective-permute-start.32) | collective-permute-done | bytes 426016 | tf_op jit(solution)/shard_map/ppermute | solution.py:658
  186.4 0.1 broadcast_select_fusion.5
  186.6 1.3 finish.1
  (110 shorter events, 2.0 us)
Async XLA Ops:
  0.6 3.0 %collective-permute-start = (bf16[3,512,256]{2,1,0:T(8,128)(2,1)}, bf16[3,512,256]{2,1,0:T(8,128)(2,1)S(1)}, u32[]{:S(2)}, u32[]{:S(2)}) collective-permute-start(bf16[3,512,256]{2,1,0:T(8,128)(2,1)} %wa_ref.4), channel_id=1, source_target_pairs={{0,1},{1,0},{2,3},{3,2},{4,5},{5,4},{6,7},{7,6},{8,9},{9,8},{10,11... | collective-permute-start | bytes 2359304 | tf_op jit(solution)/shard_map/ppermute | solution.py:771
  1.2 2.5 %collective-permute-start.2 = (bf16[256,512]{1,0:T(8,128)(2,1)}, bf16[256,512]{1,0:T(8,128)(2,1)S(1)}, u32[]{:S(2)}, u32[]{:S(2)}) collective-permute-start(bf16[256,512]{1,0:T(8,128)(2,1)} %pa_ref.3), channel_id=1, source_target_pairs={{0,1},{1,0},{2,3},{3,2},{4,5},{5,4},{6,7},{7,6},{8,9},{9,8},{10,11... | collective-permute-start | bytes 786440 | tf_op jit(solution)/shard_map/ppermute | solution.py:771
  1.2 2.4 %collective-permute-start.1 = (f32[2,256]{1,0:T(2,128)}, f32[2,256]{1,0:T(2,128)S(1)}, u32[]{:S(2)}, u32[]{:S(2)}) collective-permute-start(f32[2,256]{1,0:T(2,128)} %qva_ref.1), channel_id=1, source_target_pairs={{0,1},{1,0},{2,3},{3,2},{4,5},{5,4},{6,7},{7,6},{8,9},{9,8},{10,11... | collective-permute-start | bytes 6152 | tf_op jit(solution)/shard_map/ppermute | solution.py:771
  1.7 2.0 %collective-permute-start.3 = (f32[8,361]{1,0:T(8,128)}, f32[8,361]{1,0:T(8,128)S(1)}, u32[]{:S(2)}, u32[]{:S(2)}) collective-permute-start(f32[8,361]{1,0:T(8,128)} %bitcast.9), channel_id=1, source_target_pairs={{0,1},{1,0},{2,3},{3,2},{4,5},{5,4},{6,7},{7,6},{8,9},{9,8},{10,11... | collective-permute-start | bytes 34664 | tf_op jit(solution)/shard_map/ppermute | solution.py:771
  3.7 1.1 copy-start.19
  3.7 1.1 copy-start.18
  3.7 1.1 copy-start.2
  3.7 1.0 copy-start.14
  3.7 26.7 %copy-start = (bf16[1024,512]{1,0:T(8,128)(2,1)S(1)}, bf16[1024,512]{1,0:T(8,128)(2,1)}, u32[]{:S(2)}) copy-start(bf16[1024,512]{1,0:T(8,128)(2,1)} %w2a_ref.4) | copy-start | bytes 3145732
  3.7 26.7 %copy-start.1 = (bf16[256,512]{1,0:T(8,128)(2,1)S(1)}, bf16[256,512]{1,0:T(8,128)(2,1)}, u32[]{:S(2)}) copy-start(bf16[256,512]{1,0:T(8,128)(2,1)} %pa_ref.3) | copy-start | bytes 786436
  3.7 26.7 %copy-start.4 = (f32[2,512]{1,0:T(2,128)S(1)}, f32[2,512]{1,0:T(2,128)}, u32[]{:S(2)}) copy-start(f32[2,512]{1,0:T(2,128)} %gain_ref.6) | copy-start | bytes 12292
  3.7 26.7 %copy-start.5 = (f32[2,512]{1,0:T(2,128)S(1)}, f32[2,512]{1,0:T(2,128)}, u32[]{:S(2)}) copy-start(f32[2,512]{1,0:T(2,128)} %shift_ref.3) | copy-start | bytes 12292
  3.8 26.7 %copy-start.6 = (bf16[512,1024]{1,0:T(8,128)(2,1)S(1)}, bf16[512,1024]{1,0:T(8,128)(2,1)}, u32[]{:S(2)}) copy-start(bf16[512,1024]{1,0:T(8,128)(2,1)} %w1a_ref.1) | copy-start | bytes 3145732
  3.8 26.7 %copy-start.8 = (f32[1024]{0:T(1024)S(1)}, f32[1024]{0:T(1024)}, u32[]{:S(2)}) copy-start(f32[1024]{0:T(1024)} %param.21) | copy-start | bytes 12292
  3.8 25.7 %collective-permute-start.4 = (bf16[512,1024]{1,0:T(8,128)(2,1)}, bf16[512,1024]{1,0:T(8,128)(2,1)S(1)}, u32[]{:S(2)}, u32[]{:S(2)}) collective-permute-start(bf16[512,1024]{1,0:T(8,128)(2,1)} %w1a_ref.1), channel_id=1, source_target_pairs={{0,1},{1,0},{2,3},{3,2},{4,5},{5,4},{6,7},{7,6},{8,9},{9,8},{10,11... | collective-permute-start | bytes 3145736 | tf_op jit(solution)/shard_map/ppermute | solution.py:771
  4.2 25.2 %collective-permute-start.5 = (bf16[1024,512]{1,0:T(8,128)(2,1)}, bf16[1024,512]{1,0:T(8,128)(2,1)S(1)}, u32[]{:S(2)}, u32[]{:S(2)}) collective-permute-start(bf16[1024,512]{1,0:T(8,128)(2,1)} %w2a_ref.4), channel_id=1, source_target_pairs={{0,1},{1,0},{2,3},{3,2},{4,5},{5,4},{6,7},{7,6},{8,9},{9,8},{10,11... | collective-permute-start | bytes 3145736 | tf_op jit(solution)/shard_map/ppermute | solution.py:771
  4.4 25.1 %collective-permute-start.6 = (f32[1024]{0:T(1024)}, f32[1024]{0:T(1024)S(1)}, u32[]{:S(2)}, u32[]{:S(2)}) collective-permute-start(f32[1024]{0:T(1024)} %param.21), channel_id=1, source_target_pairs={{0,1},{1,0},{2,3},{3,2},{4,5},{5,4},{6,7},{7,6},{8,9},{9,8},{10,11... | collective-permute-start | bytes 12296 | tf_op jit(solution)/shard_map/ppermute | solution.py:771
  29.5 1.0 copy-start.15
  30.5 1.0 copy-start.3
  72.3 5.7 %collective-permute-start.7 = (bf16[2304,512]{1,0:T(8,128)(2,1)}, bf16[2304,512]{1,0:T(8,128)(2,1)}, u32[]{:S(2)}, u32[]{:S(2)}) collective-permute-start(bf16[2304,512]{1,0:T(8,128)(2,1)} %get-tuple-element.179), channel_id=1, source_target_pairs={{0,1},{1,0},{2,3},{3,2},{4,5},{5,4},{6,7},{7,6},{8,9},{9,8},{10,11... | collective-permute-start | bytes 7077896 | tf_op jit(solution)/shard_map/ppermute | solution.py:681
  72.8 5.2 %copy-start.16 = (bf16[2304,512]{1,0:T(8,128)(2,1)S(1)}, bf16[2304,512]{1,0:T(8,128)(2,1)}, u32[]{:S(2)}) copy-start(bf16[2304,512]{1,0:T(8,128)(2,1)} %get-tuple-element.176) | copy-start | bytes 7077892
  80.6 29.3 %collective-permute-start.8 = (bf16[832,512]{1,0:T(8,128)(2,1)S(1)}, bf16[832,512]{1,0:T(8,128)(2,1)S(1)}, u32[]{:S(2)}, u32[]{:S(2)}) collective-permute-start(bf16[832,512]{1,0:T(8,128)(2,1)S(1)} %constant_dynamic-slice_fusion.8), channel_id=1, source_target_pairs={{0,2},{1,5},{2,0},{3,7},{4,6},{5,1},{6,4},{7,3},{8,10},{9,13},{10,... | collective-permute-start | bytes 2555912 | tf_op jit(solution)/shard_map/ppermute | solution.py:658
  83.3 26.6 %collective-permute-start.9 = (bf16[320,512]{1,0:T(8,128)(2,1)S(1)}, bf16[320,512]{1,0:T(8,128)(2,1)S(1)}, u32[]{:S(2)}, u32[]{:S(2)}) collective-permute-start(bf16[320,512]{1,0:T(8,128)(2,1)S(1)} %constant_dynamic-slice_fusion.7), channel_id=1, source_target_pairs={{0,8},{1,9},{2,10},{3,11},{4,12},{5,13},{6,14},{7,15},{8,0},{9,1},... | collective-permute-start | bytes 983048 | tf_op jit(solution)/shard_map/ppermute | solution.py:658
  110.3 8.3 %collective-permute-start.12 = (bf16[768,512]{1,0:T(8,128)(2,1)}, bf16[768,512]{1,0:T(8,128)(2,1)S(1)}, u32[]{:S(2)}, u32[]{:S(2)}) collective-permute-start(bf16[768,512]{1,0:T(8,128)(2,1)} %get-tuple-element.208), channel_id=1, source_target_pairs={{0,1},{1,0},{2,3},{3,2},{4,5},{5,4},{6,7},{7,6},{8,9},{9,8},{10,11... | collective-permute-start | bytes 2359304 | tf_op jit(solution)/shard_map/ppermute | solution.py:681
  110.4 8.2 %collective-permute-start.10 = (bf16[416,512]{1,0:T(8,128)(2,1)S(1)}, bf16[416,512]{1,0:T(8,128)(2,1)S(1)}, u32[]{:S(2)}, u32[]{:S(2)}) collective-permute-start(bf16[416,512]{1,0:T(8,128)(2,1)S(1)} %constant_dynamic-slice_fusion.6), channel_id=1, source_target_pairs={{0,4},{1,9},{2,6},{3,11},{4,0},{5,13},{6,2},{7,15},{8,12},{9,1},{1... | collective-permute-start | bytes 1277960 | tf_op jit(solution)/shard_map/ppermute | solution.py:658
  112.0 5.9 %collective-permute-start.11 = (bf16[160,512]{1,0:T(8,128)(2,1)S(1)}, bf16[160,512]{1,0:T(8,128)(2,1)S(1)}, u32[]{:S(2)}, u32[]{:S(2)}) collective-permute-start(bf16[160,512]{1,0:T(8,128)(2,1)S(1)} %constant_dynamic-slice_fusion.5), channel_id=1, source_target_pairs={{0,2},{1,3},{2,0},{3,1},{4,6},{5,7},{6,4},{7,5},{8,10},{9,11},{10,... | collective-permute-start | bytes 491528 | tf_op jit(solution)/shard_map/ppermute | solution.py:658
  117.9 1.1 copy-start.17
  119.3 9.2 %collective-permute-start.15 = (bf16[384,512]{1,0:T(8,128)(2,1)S(1)}, bf16[384,512]{1,0:T(8,128)(2,1)S(1)}, u32[]{:S(2)}, u32[]{:S(2)}) collective-permute-start(bf16[384,512]{1,0:T(8,128)(2,1)S(1)} %constant_dynamic-slice_fusion.2), channel_id=1, source_target_pairs={{0,2},{1,5},{2,0},{3,7},{4,6},{5,1},{6,4},{7,3},{8,10},{9,13},{10,... | collective-permute-start | bytes 1179656 | tf_op jit(solution)/shard_map/ppermute | solution.py:658
  120.9 7.6 %collective-permute-start.13 = (bf16[208,512]{1,0:T(8,128)(2,1)S(1)}, bf16[208,512]{1,0:T(8,128)(2,1)S(1)}, u32[]{:S(2)}, u32[]{:S(2)}) collective-permute-start(bf16[208,512]{1,0:T(8,128)(2,1)S(1)} %constant_dynamic-slice_fusion.4), channel_id=1, source_target_pairs={{0,8},{1,17},{2,10},{3,19},{4,12},{5,21},{6,14},{7,23},{8,0},{9,25... | collective-permute-start | bytes 638984 | tf_op jit(solution)/shard_map/ppermute | solution.py:658
  121.4 5.9 %collective-permute-start.14 = (bf16[80,512]{1,0:T(8,128)(2,1)S(1)}, bf16[80,512]{1,0:T(8,128)(2,1)S(1)}, u32[]{:S(2)}, u32[]{:S(2)}) collective-permute-start(bf16[80,512]{1,0:T(8,128)(2,1)S(1)} %constant_dynamic-slice_fusion.3), channel_id=1, source_target_pairs={{0,4},{1,5},{2,6},{3,7},{4,0},{5,1},{6,2},{7,3},{8,12},{9,13},{10,... | collective-permute-start | bytes 245768 | tf_op jit(solution)/shard_map/ppermute | solution.py:658
  128.7 13.4 %copy-start.7 = (f32[16,256]{1,0:T(8,128)S(1)}, f32[16,256]{1,0:T(8,128)}, u32[]{:S(2)}) copy-start(f32[16,256]{1,0:T(8,128)} %get-tuple-element.263.idx_ref) | copy-start | bytes 49156
  128.7 13.4 %copy-start.9 = (f32[2,512]{1,0:T(2,128)S(1)}, f32[2,512]{1,0:T(2,128)}, u32[]{:S(2)}) copy-start(f32[2,512]{1,0:T(2,128)} %get-tuple-element.266.gs1a_ref) | copy-start | bytes 12292
  128.7 13.3 %copy-start.10 = (f32[2,512]{1,0:T(2,128)S(1)}, f32[2,512]{1,0:T(2,128)}, u32[]{:S(2)}) copy-start(f32[2,512]{1,0:T(2,128)} %get-tuple-element.267.gs1b_ref) | copy-start | bytes 12292
  128.8 13.3 %copy-start.12 = (f32[8,104,256]{2,1,0:T(8,128)S(1)}, f32[8,104,256]{2,1,0:T(8,128)}, u32[]{:S(2)}) copy-start(f32[8,104,256]{2,1,0:T(8,128)} %get-tuple-element.264.t_ref) | copy-start | bytes 2555908
  128.8 13.3 %copy-start.13 = (f32[2,512]{1,0:T(2,128)S(1)}, f32[2,512]{1,0:T(2,128)}, u32[]{:S(2)}) copy-start(f32[2,512]{1,0:T(2,128)} %get-tuple-element.270.gqv_ref) | copy-start | bytes 12292
  128.8 11.8 %collective-permute-start.16 = (bf16[208,512]{1,0:T(8,128)(2,1)S(1)}, bf16[208,512]{1,0:T(8,128)(2,1)S(1)}, u32[]{:S(2)}, u32[]{:S(2)}) collective-permute-start(bf16[208,512]{1,0:T(8,128)(2,1)S(1)} %dynamic-slice_add_fusion.4), channel_id=1, source_target_pairs={{0,16},{1,3},{2,18},{3,1},{4,20},{5,7},{6,22},{7,5},{8,24},{9,11},... | collective-permute-start | bytes 638984 | tf_op jit(solution)/shard_map/ppermute | solution.py:658
  130.2 10.3 %collective-permute-start.17 = (bf16[80,512]{1,0:T(8,128)(2,1)S(1)}, bf16[80,512]{1,0:T(8,128)(2,1)S(1)}, u32[]{:S(2)}, u32[]{:S(2)}) collective-permute-start(bf16[80,512]{1,0:T(8,128)(2,1)S(1)} %dynamic-slice_add_fusion.8), channel_id=1, source_target_pairs={{0,16},{1,17},{2,18},{3,19},{4,20},{5,21},{6,22},{7,23},{8,24},{9,... | collective-permute-start | bytes 245768 | tf_op jit(solution)/shard_map/ppermute | solution.py:658
  131.8 8.8 %collective-permute-start.18 = (bf16[192,512]{1,0:T(8,128)(2,1)S(1)}, bf16[192,512]{1,0:T(8,128)(2,1)S(1)}, u32[]{:S(2)}, u32[]{:S(2)}) collective-permute-start(bf16[192,512]{1,0:T(8,128)(2,1)S(1)} %constant_dynamic-slice_fusion.1), channel_id=1, source_target_pairs={{0,4},{1,9},{2,6},{3,11},{4,0},{5,13},{6,2},{7,15},{8,12},{9,1},{1... | collective-permute-start | bytes 589832 | tf_op jit(solution)/shard_map/ppermute | solution.py:658
  140.6 10.2 %collective-permute-start.19 = (bf16[208,512]{1,0:T(8,128)(2,1)S(1)}, bf16[208,512]{1,0:T(8,128)(2,1)S(1)}, u32[]{:S(2)}, u32[]{:S(2)}) collective-permute-start(bf16[208,512]{1,0:T(8,128)(2,1)S(1)} %add.117), channel_id=1, source_target_pairs={{0,8},{1,17},{2,10},{3,19},{4,12},{5,21},{6,14},{7,23},{8,0},{9,25... | collective-permute-start | bytes 638984 | tf_op jit(solution)/shard_map/ppermute | solution.py:658
  140.9 9.9 %collective-permute-start.20 = (bf16[80,512]{1,0:T(8,128)(2,1)S(1)}, bf16[80,512]{1,0:T(8,128)(2,1)S(1)}, u32[]{:S(2)}, u32[]{:S(2)}) collective-permute-start(bf16[80,512]{1,0:T(8,128)(2,1)S(1)} %add.118), channel_id=1, source_target_pairs={{0,4},{1,5},{2,6},{3,7},{4,0},{5,1},{6,2},{7,3},{8,12},{9,13},{10,... | collective-permute-start | bytes 245768 | tf_op jit(solution)/shard_map/ppermute | solution.py:658
  142.1 0.7 copy-start.11
  143.7 7.0 %collective-permute-start.21 = (bf16[96,512]{1,0:T(8,128)(2,1)S(1)}, bf16[96,512]{1,0:T(8,128)(2,1)S(1)}, u32[]{:S(2)}, u32[]{:S(2)}) collective-permute-start(bf16[96,512]{1,0:T(8,128)(2,1)S(1)} %constant_dynamic-slice_fusion), channel_id=1, source_target_pairs={{0,8},{1,17},{2,10},{3,19},{4,12},{5,21},{6,14},{7,23},{8,0},{9,25... | collective-permute-start | bytes 294920 | tf_op jit(solution)/shard_map/ppermute | solution.py:658
  145.6 5.1 %collective-permute-start.22 = (bf16[32,512]{1,0:T(8,128)(2,1)S(1)}, bf16[32,512]{1,0:T(8,128)(2,1)S(1)}, u32[]{:S(2)}, u32[]{:S(2)}) collective-permute-start(bf16[32,512]{1,0:T(8,128)(2,1)S(1)} %get-tuple-element.274), channel_id=1, source_target_pairs={{0,1},{1,0},{2,3},{3,2},{4,5},{5,4},{6,7},{7,6},{8,9},{9,8},{10,11... | collective-permute-start | bytes 98312 | tf_op jit(solution)/shard_map/ppermute | solution.py:681
  151.0 8.9 %collective-permute-start.23 = (bf16[416,512]{1,0:T(8,128)(2,1)S(1)}, bf16[416,512]{1,0:T(8,128)(2,1)S(1)}, u32[]{:S(2)}, u32[]{:S(2)}) collective-permute-start(bf16[416,512]{1,0:T(8,128)(2,1)S(1)} %pad_maximum_fusion.5), channel_id=1, source_target_pairs={{0,4},{1,9},{2,6},{3,11},{4,0},{5,13},{6,2},{7,15},{8,12},{9,1},{1... | collective-permute-start | bytes 1277960 | tf_op jit(solution)/shard_map/ppermute | solution.py:658
  151.9 8.0 %collective-permute-start.24 = (bf16[160,512]{1,0:T(8,128)(2,1)S(1)}, bf16[160,512]{1,0:T(8,128)(2,1)S(1)}, u32[]{:S(2)}, u32[]{:S(2)}) collective-permute-start(bf16[160,512]{1,0:T(8,128)(2,1)S(1)} %pad_maximum_fusion.11), channel_id=1, source_target_pairs={{0,2},{1,3},{2,0},{3,1},{4,6},{5,7},{6,4},{7,5},{8,10},{9,11},{10,... | collective-permute-start | bytes 491528 | tf_op jit(solution)/shard_map/ppermute | solution.py:658
  152.9 7.0 %collective-permute-start.25 = (bf16[128,512]{1,0:T(8,128)(2,1)S(1)}, bf16[128,512]{1,0:T(8,128)(2,1)S(1)}, u32[]{:S(2)}, u32[]{:S(2)}) collective-permute-start(bf16[128,512]{1,0:T(8,128)(2,1)S(1)} %pad_maximum_fusion.12), channel_id=1, source_target_pairs={{0,16},{1,3},{2,18},{3,1},{4,20},{5,7},{6,22},{7,5},{8,24},{9,11},... | collective-permute-start | bytes 393224 | tf_op jit(solution)/shard_map/ppermute | solution.py:658
  160.1 9.7 %collective-permute-start.26 = (bf16[416,512]{1,0:T(8,128)(2,1)S(1)}, bf16[416,512]{1,0:T(8,128)(2,1)S(1)}, u32[]{:S(2)}, u32[]{:S(2)}) collective-permute-start(bf16[416,512]{1,0:T(8,128)(2,1)S(1)} %get-tuple-element.293), channel_id=1, source_target_pairs={{0,2},{1,5},{2,0},{3,7},{4,6},{5,1},{6,4},{7,3},{8,10},{9,13},{10,... | collective-permute-start | bytes 1277960 | tf_op jit(solution)/shard_map/ppermute | solution.py:658
  161.4 8.4 %collective-permute-start.27 = (bf16[160,512]{1,0:T(8,128)(2,1)S(1)}, bf16[160,512]{1,0:T(8,128)(2,1)S(1)}, u32[]{:S(2)}, u32[]{:S(2)}) collective-permute-start(bf16[160,512]{1,0:T(8,128)(2,1)S(1)} %get-tuple-element.294), channel_id=1, source_target_pairs={{0,8},{1,9},{2,10},{3,11},{4,12},{5,13},{6,14},{7,15},{8,0},{9,1},... | collective-permute-start | bytes 491528 | tf_op jit(solution)/shard_map/ppermute | solution.py:658
  162.2 7.6 %collective-permute-start.28 = (bf16[128,512]{1,0:T(8,128)(2,1)S(1)}, bf16[128,512]{1,0:T(8,128)(2,1)S(1)}, u32[]{:S(2)}, u32[]{:S(2)}) collective-permute-start(bf16[128,512]{1,0:T(8,128)(2,1)S(1)} %pad_maximum_fusion.13), channel_id=1, source_target_pairs={{0,8},{1,17},{2,10},{3,19},{4,12},{5,21},{6,14},{7,23},{8,0},{9,25... | collective-permute-start | bytes 393224 | tf_op jit(solution)/shard_map/ppermute | solution.py:658
  169.9 8.2 %collective-permute-start.29 = (bf16[416,512]{1,0:T(8,128)(2,1)S(1)}, bf16[416,512]{1,0:T(8,128)(2,1)S(1)}, u32[]{:S(2)}, u32[]{:S(2)}) collective-permute-start(bf16[416,512]{1,0:T(8,128)(2,1)S(1)} %get-tuple-element.305), channel_id=1, source_target_pairs={{0,2},{1,5},{2,0},{3,7},{4,6},{5,1},{6,4},{7,3},{8,10},{9,13},{10,... | collective-permute-start | bytes 1277960 | tf_op jit(solution)/shard_map/ppermute | solution.py:658
  171.0 7.1 %collective-permute-start.30 = (bf16[160,512]{1,0:T(8,128)(2,1)S(1)}, bf16[160,512]{1,0:T(8,128)(2,1)S(1)}, u32[]{:S(2)}, u32[]{:S(2)}) collective-permute-start(bf16[160,512]{1,0:T(8,128)(2,1)S(1)} %get-tuple-element.306), channel_id=1, source_target_pairs={{0,8},{1,9},{2,10},{3,11},{4,12},{5,13},{6,14},{7,15},{8,0},{9,1},... | collective-permute-start | bytes 491528 | tf_op jit(solution)/shard_map/ppermute | solution.py:658
  171.9 6.2 %collective-permute-start.31 = (bf16[224,512]{1,0:T(8,128)(2,1)S(1)}, bf16[224,512]{1,0:T(8,128)(2,1)S(1)}, u32[]{:S(2)}, u32[]{:S(2)}) collective-permute-start(bf16[224,512]{1,0:T(8,128)(2,1)S(1)} %pad_maximum_fusion.9), channel_id=1, source_target_pairs={{0,4},{1,9},{2,6},{3,11},{4,0},{5,13},{6,2},{7,15},{8,12},{9,1},{1... | collective-permute-start | bytes 688136 | tf_op jit(solution)/shard_map/ppermute | solution.py:658
  178.2 8.2 %collective-permute-start.32 = (bf16[416,512]{1,0:T(8,128)(2,1)S(1)}, bf16[416,512]{1,0:T(8,128)(2,1)S(1)}, u32[]{:S(2)}, u32[]{:S(2)}) collective-permute-start(bf16[416,512]{1,0:T(8,128)(2,1)S(1)} %pad_maximum_fusion.6), channel_id=1, source_target_pairs={{0,2},{1,5},{2,0},{3,7},{4,6},{5,1},{6,4},{7,3},{8,10},{9,13},{10,... | collective-permute-start | bytes 1277960 | tf_op jit(solution)/shard_map/ppermute | solution.py:658

commit v3 on v2

--- a/solution.py
+++ b/solution.py
@@ -436,7 +436,7 @@
             pltpu.VMEM((8, 2048), F32),
             pltpu.VMEM((4, 8, 512), F32),
         ],
-        compiler_params=params(50),
+        compiler_params=params(48),
         cost_estimate=cost(50e9, 40e6),
     )(mixed, go, att, *small)
 

time: 188 us -> 186 us (0.989)
  no operation moved by 1% of the time
where the time goes in v3:
time: 186 us
  Pallas kernels  123 us (66%)
  starting transfers between devices  29.6 us (16%)
  waiting for transfers between devices  19.2 us (10%)
  other arithmetic  8.66 us (5%)
  local copies, waits for them, and re-layouts  4.14 us (2%)
    pallas_call x1, Pallas kernels, ffn(): pl.pallas_call(ffn_body, name='feed_forward', grid=(rows // DENSE,), in_s...  39.6 us
    ppermute x23, starting transfers between devices, move(): return lax.ppermute(send, ('dp', 'tp'), perm)  27 us
    pallas_call x1, Pallas kernels, attn_bwd(): pl.pallas_call(attn_bwd_body, name='attn_bwd', grid=(rows // ROWS + 1,),...  25 us
    pallas_call x1, Pallas kernels, attn_fwd(): pl.pallas_call(attn_fwd_body, name='attn_fwd', grid=(rows // ROWS + 1,),...  24.7 us
    ppermute x23, waiting for transfers between devices, move(): return lax.ppermute(send, ('dp', 'tp'), perm)  18.7 us
    pallas_call x3, Pallas kernels, input_grad(): pl.pallas_call(input_grad_body, name='input_grad', grid=(THIRD,), in_spec...  16.2 us
    pallas_call x3, Pallas kernels, out_rows(): pl.pallas_call(out_body, name='block_out', grid=(THIRD,), in_specs=[spec(...  15.4 us
  transfers between devices with their start and end apart: 33, of which 8 were waited for; matrix products, arithmetic and copies ran while one was open for 3% of the time, Pallas kernels for 44%

profile of v3, /device:TPU:0, one launch (start us, length us, event | category | flops | bytes accessed | tf_op | source)
XLA Modules:
  0.0 185.8 jit_solution(1461282498016067565)
XLA Ops:
  0.6 0.5 collective-permute-start
  1.2 0.4 collective-permute-start.1
  1.8 0.8 reshape.30
  2.6 0.6 pad.4
  3.2 0.4 collective-permute-done.1.qvb_ref
  3.8 0.4 collective-permute-start.4
  4.2 0.1 collective-permute-start.5
  4.4 0.4 collective-permute-start.6
  4.7 24.7 %attn_fwd.1 = (bf16[2400,512]{1,0:T(8,128)(2,1)}, bf16[24,128,1536]{2,1,0:T(8,128)(2,1)}, f32[2400,512]{1,0:T(8,128)}, bf16[2400,512]{1,0:T(8,128)(2,1)}, bf16[2...) custom-call(bf16[2400,512]{1,0:T(8,128)(2,1)} %x_ref.4, bf16[2400,512]{1,0:T(8,128)(2,1)} %x_ref.4, f32[24,1,128]{2,1,0:T(1,128)} %bitcast.8, ...), custom_call_target="tpu_custom_call" | custom-call | tf_op jit(solution)/shard_map/attn_fwd/pallas_call | solution.py:378
  29.5 1.1 copy-done.4
  30.7 39.6 %feed_forward.1 = (bf16[2400,2048]{1,0:T(8,128)(2,1)}, f32[2400,512]{1,0:T(8,128)}, bf16[2400,512]{1,0:T(8,128)(2,1)}, bf16[2304,512]{1,0:T(8,128)(2,1)}, bf16[2...) custom-call(f32[2400,512]{1,0:T(8,128)} %get-tuple-element.296.mixed_ref, ...), custom_call_target="tpu_custom_call" | custom-call | flops 49999998976 | bytes 40000000 | tf_op jit(solution)/shard_map/feed_forward/pallas_call | solution.py:416
  70.3 0.4 collective-permute-start.7
  70.7 5.2 %block_out.3.refs_0_ = bf16[2400,512]{1,0:T(8,128)(2,1)} custom-call(f32[2400,512]{1,0:T(8,128)} %get-tuple-element.296.mixed_ref, bf16[2400,2048]{1,0:T(8,128)(2,1)} %get-tuple-element.297.act_ref, bf16[1024,512]{1,0:T(8,128)(2,1)} %w2a_ref.4, bf16[1024,512]{1,0:T(8,128)(2,1)} %copy-done.1, f32[2,512]{1,0:T(2,128)} %ob_ref.4), custom_call_target="tpu_custom_call" | custom-call | flops 3000000000 | bytes 7000000 | tf_op jit(solution)/shard_map/block_out/pallas_call | solution.py:451
  76.0 2.3 %add.100 = bf16[2304,512]{1,0:T(8,128)(2,1)S(1)} add(bf16[2304,512]{1,0:T(8,128)(2,1)S(1)} %copy-done.16, bf16[2304,512]{1,0:T(8,128)(2,1)} %collective-permute-done.7) | non-fusion elementwise | flops 1179648 | bytes 7077888 | tf_op jit(solution)/shard_map/add | solution.py:687
  78.6 2.7 %collective-permute-start.8 = (bf16[832,512]{1,0:T(8,128)(2,1)S(1)}, bf16[832,512]{1,0:T(8,128)(2,1)S(1)}, u32[]{:S(2)}, u32[]{:S(2)}) collective-permute-start(bf16[832,512]{1,0:T(8,128)(2,1)S(1)} %constant_dynamic-slice_fusion.8), channel_id=1, source_target_pairs={{0,2},{1,5},{2,0},{3,7},{4,6},{5,1},{6,4},{7,3},{8,10},{9,13},{10,... | collective-permute-start | bytes 2555912 | tf_op jit(solution)/shard_map/ppermute | solution.py:658
  81.3 1.6 collective-permute-start.9
  82.8 25.0 %attn_bwd.1 = (bf16[2400,1536]{1,0:T(8,128)(2,1)}, f32[8,104,256]{2,1,0:T(8,128)}, bf16[768,512]{1,0:T(8,128)(2,1)}, bf16[768,512]{1,0:T(8,128)(2,1)}, f32[2,512]{1,0:T(2,128)}) custom-call(bf16[2400,512]{1,0:T(8,128)(2,1)} %get-tuple-element.192.n_ref, bf16[2400,512]{1,0:T(8,128)(2,1)} %get-tuple-element.193.do_ref, ...), custom_call_target="tpu_custom_call" | custom-call | flops 30000001024 | bytes 60000000 | tf_op jit(solution)/shard_map/attn_bwd/pallas_call | solution.py:469
  107.9 0.2 dynamic-slice_add_fusion
  108.4 1.6 collective-permute-start.10
  110.0 0.5 collective-permute-start.11
  110.5 5.4 %input_grad.3 = (bf16[2400,512]{1,0:T(8,128)(2,1)}, f32[2,512]{1,0:T(2,128)}) custom-call(bf16[2400,512]{1,0:T(8,128)(2,1)} %x_ref.4, f32[2400,512]{1,0:T(8,128)} %get-tuple-element.242.gm_ref, bf16[2400,1536]{1,0:T(8,128)(2,1)} %get-tuple-element.243.d_ref, bf16[3,512,256]{2,1,0:T(8,128)(2,1)} %wa_ref.4, bf16[3,512,256]{2,1,0:T(8,128)(2,1)} %copy-done.15, ...), custom_call_target="tpu_custom_call" | custom-call | flops 3000000000 | bytes 7000000 | tf_op jit(solution)/shard_map/input_grad/pallas_call | solution.py:495
  115.9 0.7 collective-permute-done.10
  116.8 0.2 copy-done.17
  117.0 0.2 add.111
  117.3 1.6 collective-permute-start.15
  118.8 0.5 collective-permute-start.13
  119.3 0.5 collective-permute-start.14
  119.8 5.4 %input_grad.4 = (bf16[2400,512]{1,0:T(8,128)(2,1)}, f32[2,512]{1,0:T(2,128)}) custom-call(bf16[2400,512]{1,0:T(8,128)(2,1)} %x_ref.4, f32[2400,512]{1,0:T(8,128)} %get-tuple-element.242.gm_ref, bf16[2400,1536]{1,0:T(8,128)(2,1)} %get-tuple-element.243.d_ref, bf16[3,512,256]{2,1,0:T(8,128)(2,1)} %wa_ref.4, ...), custom_call_target="tpu_custom_call", output_to_operand_aliasing={{0}: (6, {})} | custom-call | flops 3000000000 | bytes 7000000 | tf_op jit(solution)/shard_map/input_grad/pallas_call | solution.py:495
  125.2 1.2 collective-permute-done.13
  126.5 0.1 dynamic-slice_add_fusion.2
  126.7 1.4 collective-permute-start.16
  128.2 1.6 collective-permute-start.17
  129.7 0.3 collective-permute-start.18
  130.1 5.4 %input_grad.5 = (bf16[2400,512]{1,0:T(8,128)(2,1)}, f32[2,512]{1,0:T(2,128)}) custom-call(bf16[2400,512]{1,0:T(8,128)(2,1)} %x_ref.4, f32[2400,512]{1,0:T(8,128)} %get-tuple-element.242.gm_ref, bf16[2400,1536]{1,0:T(8,128)(2,1)} %get-tuple-element.243.d_ref, bf16[3,512,256]{2,1,0:T(8,128)(2,1)} %wa_ref.4, ...), custom_call_target="tpu_custom_call", output_to_operand_aliasing={{0}: (6, {})} | custom-call | flops 3000000000 | bytes 7000000 | tf_op jit(solution)/shard_map/input_grad/pallas_call | solution.py:495
  135.5 3.0 %collective-permute-done.17 = bf16[80,512]{1,0:T(8,128)(2,1)S(1)} collective-permute-done((bf16[80,512]{1,0:T(8,128)(2,1)S(1)}, bf16[80,512]{1,0:T(8,128)(2,1)S(1)}, u32[]{:S(2)}, u32[]{:S(2)}) %collective-permute-start.17) | collective-permute-done | bytes 81952 | tf_op jit(solution)/shard_map/ppermute | solution.py:658
  138.6 0.2 collective-permute-start.19
  138.8 1.2 collective-permute-start.20
  140.1 0.7 copy-done.12
  140.8 0.8 small_sums.1
  141.7 1.9 %collective-permute-start.21 = (bf16[96,512]{1,0:T(8,128)(2,1)S(1)}, bf16[96,512]{1,0:T(8,128)(2,1)S(1)}, u32[]{:S(2)}, u32[]{:S(2)}) collective-permute-start(bf16[96,512]{1,0:T(8,128)(2,1)S(1)} %constant_dynamic-slice_fusion), channel_id=1, source_target_pairs={{0,8},{1,17},{2,10},{3,19},{4,12},{5,21},{6,14},{7,23},{8,0},{9,25... | collective-permute-start | bytes 294920 | tf_op jit(solution)/shard_map/ppermute | solution.py:658
  143.6 5.1 %block_out.4.refs_0_ = bf16[2400,512]{1,0:T(8,128)(2,1)} custom-call(f32[2400,512]{1,0:T(8,128)} %get-tuple-element.296.mixed_ref, bf16[2400,2048]{1,0:T(8,128)(2,1)} %get-tuple-element.297.act_ref, bf16[1024,512]{1,0:T(8,128)(2,1)} %w2a_ref.4, bf16[1024,512]{1,0:T(8,128)(2,1)} %copy-done.1, f32[2,512]{1,0:T(2,128)} %ob_ref.4, ...), custom_call_target="tpu_custom_call", output_to_operand_aliasing={{}: (5, {})} | custom-call | flops 3000000000 | bytes 7000000 | tf_op jit(solution)/shard_map/block_out/pallas_call | solution.py:451
  148.9 0.9 collective-permute-start.23
  149.8 1.0 collective-permute-start.24
  150.8 1.8 collective-permute-start.25
  152.7 5.1 %collective-permute-done.25 = bf16[128,512]{1,0:T(8,128)(2,1)S(1)} collective-permute-done((bf16[128,512]{1,0:T(8,128)(2,1)S(1)}, bf16[128,512]{1,0:T(8,128)(2,1)S(1)}, u32[]{:S(2)}, u32[]{:S(2)}) %collective-permute-start.25) | collective-permute-done | bytes 131104 | tf_op jit(solution)/shard_map/ppermute | solution.py:658
  157.8 0.2 broadcast_select_fusion.2
  158.1 1.3 collective-permute-start.26
  159.3 0.8 collective-permute-start.27
  160.1 1.2 collective-permute-start.28
  161.4 5.1 %block_out.5 = bf16[2400,512]{1,0:T(8,128)(2,1)} custom-call(f32[2400,512]{1,0:T(8,128)} %get-tuple-element.296.mixed_ref, bf16[2400,2048]{1,0:T(8,128)(2,1)} %get-tuple-element.297.act_ref, bf16[1024,512]{1,0:T(8,128)(2,1)} %w2a_ref.4, bf16[1024,512]{1,0:T(8,128)(2,1)} %copy-done.1, f32[2,512]{1,0:T(2,128)} %ob_ref.4, ...), custom_call_target="tpu_custom_call", output_to_operand_aliasing={{}: (5, {})} | custom-call | flops 3000000000 | bytes 7000000 | tf_op jit(solution)/shard_map/block_out/pallas_call | solution.py:451
  166.5 1.3 collective-permute-done.28
  167.8 1.1 collective-permute-start.29
  168.9 0.9 collective-permute-start.30
  169.8 1.1 collective-permute-start.31
  171.0 5.0 %collective-permute-done.30 = bf16[160,512]{1,0:T(8,128)(2,1)S(1)} collective-permute-done((bf16[160,512]{1,0:T(8,128)(2,1)S(1)}, bf16[160,512]{1,0:T(8,128)(2,1)S(1)}, u32[]{:S(2)}, u32[]{:S(2)}) %collective-permute-start.30) | collective-permute-done | bytes 163872 | tf_op jit(solution)/shard_map/ppermute | solution.py:658
  176.2 1.2 collective-permute-start.32
  177.4 0.1 broadcast_select_fusion.6
  177.6 0.3 broadcast_select_fusion
  177.9 1.6 fusion
  179.6 1.6 fusion.2
  181.1 0.9 slice_convert_fusion
  182.0 2.4 %collective-permute-done.32 = bf16[416,512]{1,0:T(8,128)(2,1)S(1)} collective-permute-done((bf16[416,512]{1,0:T(8,128)(2,1)S(1)}, bf16[416,512]{1,0:T(8,128)(2,1)S(1)}, u32[]{:S(2)}, u32[]{:S(2)}) %collective-permute-start.32) | collective-permute-done | bytes 426016 | tf_op jit(solution)/shard_map/ppermute | solution.py:658
  184.4 0.1 broadcast_select_fusion.5
  184.6 1.3 finish.1
  (110 shorter events, 1.9 us)
Async XLA Ops:
  0.6 3.0 %collective-permute-start = (bf16[3,512,256]{2,1,0:T(8,128)(2,1)}, bf16[3,512,256]{2,1,0:T(8,128)(2,1)S(1)}, u32[]{:S(2)}, u32[]{:S(2)}) collective-permute-start(bf16[3,512,256]{2,1,0:T(8,128)(2,1)} %wa_ref.4), channel_id=1, source_target_pairs={{0,1},{1,0},{2,3},{3,2},{4,5},{5,4},{6,7},{7,6},{8,9},{9,8},{10,11... | collective-permute-start | bytes 2359304 | tf_op jit(solution)/shard_map/ppermute | solution.py:771
  1.2 2.5 %collective-permute-start.2 = (bf16[256,512]{1,0:T(8,128)(2,1)}, bf16[256,512]{1,0:T(8,128)(2,1)S(1)}, u32[]{:S(2)}, u32[]{:S(2)}) collective-permute-start(bf16[256,512]{1,0:T(8,128)(2,1)} %pa_ref.3), channel_id=1, source_target_pairs={{0,1},{1,0},{2,3},{3,2},{4,5},{5,4},{6,7},{7,6},{8,9},{9,8},{10,11... | collective-permute-start | bytes 786440 | tf_op jit(solution)/shard_map/ppermute | solution.py:771
  1.2 2.4 %collective-permute-start.1 = (f32[2,256]{1,0:T(2,128)}, f32[2,256]{1,0:T(2,128)S(1)}, u32[]{:S(2)}, u32[]{:S(2)}) collective-permute-start(f32[2,256]{1,0:T(2,128)} %qva_ref.1), channel_id=1, source_target_pairs={{0,1},{1,0},{2,3},{3,2},{4,5},{5,4},{6,7},{7,6},{8,9},{9,8},{10,11... | collective-permute-start | bytes 6152 | tf_op jit(solution)/shard_map/ppermute | solution.py:771
  1.7 2.0 %collective-permute-start.3 = (f32[8,361]{1,0:T(8,128)}, f32[8,361]{1,0:T(8,128)S(1)}, u32[]{:S(2)}, u32[]{:S(2)}) collective-permute-start(f32[8,361]{1,0:T(8,128)} %bitcast.9), channel_id=1, source_target_pairs={{0,1},{1,0},{2,3},{3,2},{4,5},{5,4},{6,7},{7,6},{8,9},{9,8},{10,11... | collective-permute-start | bytes 34664 | tf_op jit(solution)/shard_map/ppermute | solution.py:771
  3.7 1.1 copy-start.19
  3.7 1.1 copy-start.18
  3.7 1.1 copy-start.3
  3.7 1.0 copy-start.15
  3.7 25.8 %copy-start = (bf16[1024,512]{1,0:T(8,128)(2,1)S(1)}, bf16[1024,512]{1,0:T(8,128)(2,1)}, u32[]{:S(2)}) copy-start(bf16[1024,512]{1,0:T(8,128)(2,1)} %w2a_ref.4) | copy-start | bytes 3145732
  3.7 25.8 %copy-start.2 = (bf16[256,512]{1,0:T(8,128)(2,1)S(1)}, bf16[256,512]{1,0:T(8,128)(2,1)}, u32[]{:S(2)}) copy-start(bf16[256,512]{1,0:T(8,128)(2,1)} %pa_ref.3) | copy-start | bytes 786436
  3.7 25.8 %copy-start.5 = (f32[2,512]{1,0:T(2,128)S(1)}, f32[2,512]{1,0:T(2,128)}, u32[]{:S(2)}) copy-start(f32[2,512]{1,0:T(2,128)} %gain_ref.6) | copy-start | bytes 12292
  3.7 25.8 %copy-start.6 = (f32[2,512]{1,0:T(2,128)S(1)}, f32[2,512]{1,0:T(2,128)}, u32[]{:S(2)}) copy-start(f32[2,512]{1,0:T(2,128)} %shift_ref.3) | copy-start | bytes 12292
  3.8 25.7 %copy-start.7 = (bf16[512,1024]{1,0:T(8,128)(2,1)S(1)}, bf16[512,1024]{1,0:T(8,128)(2,1)}, u32[]{:S(2)}) copy-start(bf16[512,1024]{1,0:T(8,128)(2,1)} %w1a_ref.1) | copy-start | bytes 3145732
  3.8 25.7 %copy-start.9 = (f32[1024]{0:T(1024)S(1)}, f32[1024]{0:T(1024)}, u32[]{:S(2)}) copy-start(f32[1024]{0:T(1024)} %param.21) | copy-start | bytes 12292
  3.8 25.7 %collective-permute-start.4 = (bf16[512,1024]{1,0:T(8,128)(2,1)}, bf16[512,1024]{1,0:T(8,128)(2,1)S(1)}, u32[]{:S(2)}, u32[]{:S(2)}) collective-permute-start(bf16[512,1024]{1,0:T(8,128)(2,1)} %w1a_ref.1), channel_id=1, source_target_pairs={{0,1},{1,0},{2,3},{3,2},{4,5},{5,4},{6,7},{7,6},{8,9},{9,8},{10,11... | collective-permute-start | bytes 3145736 | tf_op jit(solution)/shard_map/ppermute | solution.py:771
  4.2 25.2 %collective-permute-start.5 = (bf16[1024,512]{1,0:T(8,128)(2,1)}, bf16[1024,512]{1,0:T(8,128)(2,1)S(1)}, u32[]{:S(2)}, u32[]{:S(2)}) collective-permute-start(bf16[1024,512]{1,0:T(8,128)(2,1)} %w2a_ref.4), channel_id=1, source_target_pairs={{0,1},{1,0},{2,3},{3,2},{4,5},{5,4},{6,7},{7,6},{8,9},{9,8},{10,11... | collective-permute-start | bytes 3145736 | tf_op jit(solution)/shard_map/ppermute | solution.py:771
  4.4 25.1 %collective-permute-start.6 = (f32[1024]{0:T(1024)}, f32[1024]{0:T(1024)S(1)}, u32[]{:S(2)}, u32[]{:S(2)}) collective-permute-start(f32[1024]{0:T(1024)} %param.21), channel_id=1, source_target_pairs={{0,1},{1,0},{2,3},{3,2},{4,5},{5,4},{6,7},{7,6},{8,9},{9,8},{10,11... | collective-permute-start | bytes 12296 | tf_op jit(solution)/shard_map/ppermute | solution.py:771
  29.5 40.8 %copy-start.1 = (bf16[1024,512]{1,0:T(8,128)(2,1)}, bf16[1024,512]{1,0:T(8,128)(2,1)S(1)}, u32[]{:S(2)}) copy-start(bf16[1024,512]{1,0:T(8,128)(2,1)S(1)} %collective-permute-done.5.w2b_ref) | copy-start | bytes 3145732
  29.5 1.2 copy-start.4
  70.3 5.7 %collective-permute-start.7 = (bf16[2304,512]{1,0:T(8,128)(2,1)}, bf16[2304,512]{1,0:T(8,128)(2,1)}, u32[]{:S(2)}, u32[]{:S(2)}) collective-permute-start(bf16[2304,512]{1,0:T(8,128)(2,1)} %get-tuple-element.179), channel_id=1, source_target_pairs={{0,1},{1,0},{2,3},{3,2},{4,5},{5,4},{6,7},{7,6},{8,9},{9,8},{10,11... | collective-permute-start | bytes 7077896 | tf_op jit(solution)/shard_map/ppermute | solution.py:681
  70.7 5.2 %copy-start.16 = (bf16[2304,512]{1,0:T(8,128)(2,1)S(1)}, bf16[2304,512]{1,0:T(8,128)(2,1)}, u32[]{:S(2)}) copy-start(bf16[2304,512]{1,0:T(8,128)(2,1)} %get-tuple-element.176) | copy-start | bytes 7077892
  78.6 29.3 %collective-permute-start.8 = (bf16[832,512]{1,0:T(8,128)(2,1)S(1)}, bf16[832,512]{1,0:T(8,128)(2,1)S(1)}, u32[]{:S(2)}, u32[]{:S(2)}) collective-permute-start(bf16[832,512]{1,0:T(8,128)(2,1)S(1)} %constant_dynamic-slice_fusion.8), channel_id=1, source_target_pairs={{0,2},{1,5},{2,0},{3,7},{4,6},{5,1},{6,4},{7,3},{8,10},{9,13},{10,... | collective-permute-start | bytes 2555912 | tf_op jit(solution)/shard_map/ppermute | solution.py:658
  81.3 26.6 %collective-permute-start.9 = (bf16[320,512]{1,0:T(8,128)(2,1)S(1)}, bf16[320,512]{1,0:T(8,128)(2,1)S(1)}, u32[]{:S(2)}, u32[]{:S(2)}) collective-permute-start(bf16[320,512]{1,0:T(8,128)(2,1)S(1)} %constant_dynamic-slice_fusion.7), channel_id=1, source_target_pairs={{0,8},{1,9},{2,10},{3,11},{4,12},{5,13},{6,14},{7,15},{8,0},{9,1},... | collective-permute-start | bytes 983048 | tf_op jit(solution)/shard_map/ppermute | solution.py:658
  108.3 8.3 %collective-permute-start.12 = (bf16[768,512]{1,0:T(8,128)(2,1)}, bf16[768,512]{1,0:T(8,128)(2,1)S(1)}, u32[]{:S(2)}, u32[]{:S(2)}) collective-permute-start(bf16[768,512]{1,0:T(8,128)(2,1)} %get-tuple-element.208), channel_id=1, source_target_pairs={{0,1},{1,0},{2,3},{3,2},{4,5},{5,4},{6,7},{7,6},{8,9},{9,8},{10,11... | collective-permute-start | bytes 2359304 | tf_op jit(solution)/shard_map/ppermute | solution.py:681
  108.4 8.2 %collective-permute-start.10 = (bf16[416,512]{1,0:T(8,128)(2,1)S(1)}, bf16[416,512]{1,0:T(8,128)(2,1)S(1)}, u32[]{:S(2)}, u32[]{:S(2)}) collective-permute-start(bf16[416,512]{1,0:T(8,128)(2,1)S(1)} %constant_dynamic-slice_fusion.6), channel_id=1, source_target_pairs={{0,4},{1,9},{2,6},{3,11},{4,0},{5,13},{6,2},{7,15},{8,12},{9,1},{1... | collective-permute-start | bytes 1277960 | tf_op jit(solution)/shard_map/ppermute | solution.py:658
  110.0 5.9 %collective-permute-start.11 = (bf16[160,512]{1,0:T(8,128)(2,1)S(1)}, bf16[160,512]{1,0:T(8,128)(2,1)S(1)}, u32[]{:S(2)}, u32[]{:S(2)}) collective-permute-start(bf16[160,512]{1,0:T(8,128)(2,1)S(1)} %constant_dynamic-slice_fusion.5), channel_id=1, source_target_pairs={{0,2},{1,3},{2,0},{3,1},{4,6},{5,7},{6,4},{7,5},{8,10},{9,11},{10,... | collective-permute-start | bytes 491528 | tf_op jit(solution)/shard_map/ppermute | solution.py:658
  115.9 1.1 copy-start.17
  117.3 9.2 %collective-permute-start.15 = (bf16[384,512]{1,0:T(8,128)(2,1)S(1)}, bf16[384,512]{1,0:T(8,128)(2,1)S(1)}, u32[]{:S(2)}, u32[]{:S(2)}) collective-permute-start(bf16[384,512]{1,0:T(8,128)(2,1)S(1)} %constant_dynamic-slice_fusion.2), channel_id=1, source_target_pairs={{0,2},{1,5},{2,0},{3,7},{4,6},{5,1},{6,4},{7,3},{8,10},{9,13},{10,... | collective-permute-start | bytes 1179656 | tf_op jit(solution)/shard_map/ppermute | solution.py:658
  118.8 7.6 %collective-permute-start.13 = (bf16[208,512]{1,0:T(8,128)(2,1)S(1)}, bf16[208,512]{1,0:T(8,128)(2,1)S(1)}, u32[]{:S(2)}, u32[]{:S(2)}) collective-permute-start(bf16[208,512]{1,0:T(8,128)(2,1)S(1)} %constant_dynamic-slice_fusion.4), channel_id=1, source_target_pairs={{0,8},{1,17},{2,10},{3,19},{4,12},{5,21},{6,14},{7,23},{8,0},{9,25... | collective-permute-start | bytes 638984 | tf_op jit(solution)/shard_map/ppermute | solution.py:658
  119.3 5.9 %collective-permute-start.14 = (bf16[80,512]{1,0:T(8,128)(2,1)S(1)}, bf16[80,512]{1,0:T(8,128)(2,1)S(1)}, u32[]{:S(2)}, u32[]{:S(2)}) collective-permute-start(bf16[80,512]{1,0:T(8,128)(2,1)S(1)} %constant_dynamic-slice_fusion.3), channel_id=1, source_target_pairs={{0,4},{1,5},{2,6},{3,7},{4,0},{5,1},{6,2},{7,3},{8,12},{9,13},{10,... | collective-permute-start | bytes 245768 | tf_op jit(solution)/shard_map/ppermute | solution.py:658
  126.7 13.4 %copy-start.8 = (f32[16,256]{1,0:T(8,128)S(1)}, f32[16,256]{1,0:T(8,128)}, u32[]{:S(2)}) copy-start(f32[16,256]{1,0:T(8,128)} %get-tuple-element.263.idx_ref) | copy-start | bytes 49156
  126.7 13.3 %copy-start.10 = (f32[2,512]{1,0:T(2,128)S(1)}, f32[2,512]{1,0:T(2,128)}, u32[]{:S(2)}) copy-start(f32[2,512]{1,0:T(2,128)} %get-tuple-element.266.gs1a_ref) | copy-start | bytes 12292
  126.7 13.3 %copy-start.11 = (f32[2,512]{1,0:T(2,128)S(1)}, f32[2,512]{1,0:T(2,128)}, u32[]{:S(2)}) copy-start(f32[2,512]{1,0:T(2,128)} %get-tuple-element.267.gs1b_ref) | copy-start | bytes 12292
  126.7 13.3 %copy-start.13 = (f32[8,104,256]{2,1,0:T(8,128)S(1)}, f32[8,104,256]{2,1,0:T(8,128)}, u32[]{:S(2)}) copy-start(f32[8,104,256]{2,1,0:T(8,128)} %get-tuple-element.264.t_ref) | copy-start | bytes 2555908
  126.7 13.3 %copy-start.14 = (f32[2,512]{1,0:T(2,128)S(1)}, f32[2,512]{1,0:T(2,128)}, u32[]{:S(2)}) copy-start(f32[2,512]{1,0:T(2,128)} %get-tuple-element.270.gqv_ref) | copy-start | bytes 12292
  126.7 11.8 %collective-permute-start.16 = (bf16[208,512]{1,0:T(8,128)(2,1)S(1)}, bf16[208,512]{1,0:T(8,128)(2,1)S(1)}, u32[]{:S(2)}, u32[]{:S(2)}) collective-permute-start(bf16[208,512]{1,0:T(8,128)(2,1)S(1)} %dynamic-slice_add_fusion.4), channel_id=1, source_target_pairs={{0,16},{1,3},{2,18},{3,1},{4,20},{5,7},{6,22},{7,5},{8,24},{9,11},... | collective-permute-start | bytes 638984 | tf_op jit(solution)/shard_map/ppermute | solution.py:658
  128.2 10.3 %collective-permute-start.17 = (bf16[80,512]{1,0:T(8,128)(2,1)S(1)}, bf16[80,512]{1,0:T(8,128)(2,1)S(1)}, u32[]{:S(2)}, u32[]{:S(2)}) collective-permute-start(bf16[80,512]{1,0:T(8,128)(2,1)S(1)} %dynamic-slice_add_fusion.8), channel_id=1, source_target_pairs={{0,16},{1,17},{2,18},{3,19},{4,20},{5,21},{6,22},{7,23},{8,24},{9,... | collective-permute-start | bytes 245768 | tf_op jit(solution)/shard_map/ppermute | solution.py:658
  129.7 8.8 %collective-permute-start.18 = (bf16[192,512]{1,0:T(8,128)(2,1)S(1)}, bf16[192,512]{1,0:T(8,128)(2,1)S(1)}, u32[]{:S(2)}, u32[]{:S(2)}) collective-permute-start(bf16[192,512]{1,0:T(8,128)(2,1)S(1)} %constant_dynamic-slice_fusion.1), channel_id=1, source_target_pairs={{0,4},{1,9},{2,6},{3,11},{4,0},{5,13},{6,2},{7,15},{8,12},{9,1},{1... | collective-permute-start | bytes 589832 | tf_op jit(solution)/shard_map/ppermute | solution.py:658
  138.6 10.1 %collective-permute-start.19 = (bf16[208,512]{1,0:T(8,128)(2,1)S(1)}, bf16[208,512]{1,0:T(8,128)(2,1)S(1)}, u32[]{:S(2)}, u32[]{:S(2)}) collective-permute-start(bf16[208,512]{1,0:T(8,128)(2,1)S(1)} %add.117), channel_id=1, source_target_pairs={{0,8},{1,17},{2,10},{3,19},{4,12},{5,21},{6,14},{7,23},{8,0},{9,25... | collective-permute-start | bytes 638984 | tf_op jit(solution)/shard_map/ppermute | solution.py:658
  138.8 9.9 %collective-permute-start.20 = (bf16[80,512]{1,0:T(8,128)(2,1)S(1)}, bf16[80,512]{1,0:T(8,128)(2,1)S(1)}, u32[]{:S(2)}, u32[]{:S(2)}) collective-permute-start(bf16[80,512]{1,0:T(8,128)(2,1)S(1)} %add.118), channel_id=1, source_target_pairs={{0,4},{1,5},{2,6},{3,7},{4,0},{5,1},{6,2},{7,3},{8,12},{9,13},{10,... | collective-permute-start | bytes 245768 | tf_op jit(solution)/shard_map/ppermute | solution.py:658
  140.1 0.7 copy-start.12
  141.7 7.0 %collective-permute-start.21 = (bf16[96,512]{1,0:T(8,128)(2,1)S(1)}, bf16[96,512]{1,0:T(8,128)(2,1)S(1)}, u32[]{:S(2)}, u32[]{:S(2)}) collective-permute-start(bf16[96,512]{1,0:T(8,128)(2,1)S(1)} %constant_dynamic-slice_fusion), channel_id=1, source_target_pairs={{0,8},{1,17},{2,10},{3,19},{4,12},{5,21},{6,14},{7,23},{8,0},{9,25... | collective-permute-start | bytes 294920 | tf_op jit(solution)/shard_map/ppermute | solution.py:658
  143.5 5.1 %collective-permute-start.22 = (bf16[32,512]{1,0:T(8,128)(2,1)S(1)}, bf16[32,512]{1,0:T(8,128)(2,1)S(1)}, u32[]{:S(2)}, u32[]{:S(2)}) collective-permute-start(bf16[32,512]{1,0:T(8,128)(2,1)S(1)} %get-tuple-element.274), channel_id=1, source_target_pairs={{0,1},{1,0},{2,3},{3,2},{4,5},{5,4},{6,7},{7,6},{8,9},{9,8},{10,11... | collective-permute-start | bytes 98312 | tf_op jit(solution)/shard_map/ppermute | solution.py:681
  148.9 8.9 %collective-permute-start.23 = (bf16[416,512]{1,0:T(8,128)(2,1)S(1)}, bf16[416,512]{1,0:T(8,128)(2,1)S(1)}, u32[]{:S(2)}, u32[]{:S(2)}) collective-permute-start(bf16[416,512]{1,0:T(8,128)(2,1)S(1)} %pad_maximum_fusion.5), channel_id=1, source_target_pairs={{0,4},{1,9},{2,6},{3,11},{4,0},{5,13},{6,2},{7,15},{8,12},{9,1},{1... | collective-permute-start | bytes 1277960 | tf_op jit(solution)/shard_map/ppermute | solution.py:658
  149.8 8.0 %collective-permute-start.24 = (bf16[160,512]{1,0:T(8,128)(2,1)S(1)}, bf16[160,512]{1,0:T(8,128)(2,1)S(1)}, u32[]{:S(2)}, u32[]{:S(2)}) collective-permute-start(bf16[160,512]{1,0:T(8,128)(2,1)S(1)} %pad_maximum_fusion.11), channel_id=1, source_target_pairs={{0,2},{1,3},{2,0},{3,1},{4,6},{5,7},{6,4},{7,5},{8,10},{9,11},{10,... | collective-permute-start | bytes 491528 | tf_op jit(solution)/shard_map/ppermute | solution.py:658
  150.8 6.9 %collective-permute-start.25 = (bf16[128,512]{1,0:T(8,128)(2,1)S(1)}, bf16[128,512]{1,0:T(8,128)(2,1)S(1)}, u32[]{:S(2)}, u32[]{:S(2)}) collective-permute-start(bf16[128,512]{1,0:T(8,128)(2,1)S(1)} %pad_maximum_fusion.12), channel_id=1, source_target_pairs={{0,16},{1,3},{2,18},{3,1},{4,20},{5,7},{6,22},{7,5},{8,24},{9,11},... | collective-permute-start | bytes 393224 | tf_op jit(solution)/shard_map/ppermute | solution.py:658
  158.1 9.7 %collective-permute-start.26 = (bf16[416,512]{1,0:T(8,128)(2,1)S(1)}, bf16[416,512]{1,0:T(8,128)(2,1)S(1)}, u32[]{:S(2)}, u32[]{:S(2)}) collective-permute-start(bf16[416,512]{1,0:T(8,128)(2,1)S(1)} %get-tuple-element.293), channel_id=1, source_target_pairs={{0,2},{1,5},{2,0},{3,7},{4,6},{5,1},{6,4},{7,3},{8,10},{9,13},{10,... | collective-permute-start | bytes 1277960 | tf_op jit(solution)/shard_map/ppermute | solution.py:658
  159.3 8.4 %collective-permute-start.27 = (bf16[160,512]{1,0:T(8,128)(2,1)S(1)}, bf16[160,512]{1,0:T(8,128)(2,1)S(1)}, u32[]{:S(2)}, u32[]{:S(2)}) collective-permute-start(bf16[160,512]{1,0:T(8,128)(2,1)S(1)} %get-tuple-element.294), channel_id=1, source_target_pairs={{0,8},{1,9},{2,10},{3,11},{4,12},{5,13},{6,14},{7,15},{8,0},{9,1},... | collective-permute-start | bytes 491528 | tf_op jit(solution)/shard_map/ppermute | solution.py:658
  160.1 7.6 %collective-permute-start.28 = (bf16[128,512]{1,0:T(8,128)(2,1)S(1)}, bf16[128,512]{1,0:T(8,128)(2,1)S(1)}, u32[]{:S(2)}, u32[]{:S(2)}) collective-permute-start(bf16[128,512]{1,0:T(8,128)(2,1)S(1)} %pad_maximum_fusion.13), channel_id=1, source_target_pairs={{0,8},{1,17},{2,10},{3,19},{4,12},{5,21},{6,14},{7,23},{8,0},{9,25... | collective-permute-start | bytes 393224 | tf_op jit(solution)/shard_map/ppermute | solution.py:658
  167.8 8.2 %collective-permute-start.29 = (bf16[416,512]{1,0:T(8,128)(2,1)S(1)}, bf16[416,512]{1,0:T(8,128)(2,1)S(1)}, u32[]{:S(2)}, u32[]{:S(2)}) collective-permute-start(bf16[416,512]{1,0:T(8,128)(2,1)S(1)} %get-tuple-element.305), channel_id=1, source_target_pairs={{0,2},{1,5},{2,0},{3,7},{4,6},{5,1},{6,4},{7,3},{8,10},{9,13},{10,... | collective-permute-start | bytes 1277960 | tf_op jit(solution)/shard_map/ppermute | solution.py:658
  168.9 7.1 %collective-permute-start.30 = (bf16[160,512]{1,0:T(8,128)(2,1)S(1)}, bf16[160,512]{1,0:T(8,128)(2,1)S(1)}, u32[]{:S(2)}, u32[]{:S(2)}) collective-permute-start(bf16[160,512]{1,0:T(8,128)(2,1)S(1)} %get-tuple-element.306), channel_id=1, source_target_pairs={{0,8},{1,9},{2,10},{3,11},{4,12},{5,13},{6,14},{7,15},{8,0},{9,1},... | collective-permute-start | bytes 491528 | tf_op jit(solution)/shard_map/ppermute | solution.py:658
  169.8 6.2 %collective-permute-start.31 = (bf16[224,512]{1,0:T(8,128)(2,1)S(1)}, bf16[224,512]{1,0:T(8,128)(2,1)S(1)}, u32[]{:S(2)}, u32[]{:S(2)}) collective-permute-start(bf16[224,512]{1,0:T(8,128)(2,1)S(1)} %pad_maximum_fusion.9), channel_id=1, source_target_pairs={{0,4},{1,9},{2,6},{3,11},{4,0},{5,13},{6,2},{7,15},{8,12},{9,1},{1... | collective-permute-start | bytes 688136 | tf_op jit(solution)/shard_map/ppermute | solution.py:658
  176.2 8.2 %collective-permute-start.32 = (bf16[416,512]{1,0:T(8,128)(2,1)S(1)}, bf16[416,512]{1,0:T(8,128)(2,1)S(1)}, u32[]{:S(2)}, u32[]{:S(2)}) collective-permute-start(bf16[416,512]{1,0:T(8,128)(2,1)S(1)} %pad_maximum_fusion.6), channel_id=1, source_target_pairs={{0,2},{1,5},{2,0},{3,7},{4,6},{5,1},{6,4},{7,3},{8,10},{9,13},{10,... | collective-permute-start | bytes 1277960 | tf_op jit(solution)/shard_map/ppermute | solution.py:658
